TPU v7x, 128 devices: a whole 4x4x4 slice. The times are simulated.
128 devices in a mesh: seq: 8 (over x_lo, y), head: 16 (over z, x_hi, core).
Axes of the slice: x: 4 (x_hi: 2, x_lo: 2; x = x_hi * 2 + x_lo), y: 4, z: 4, core: 2. Of those that a mesh axis runs over, the one named last changes fastest.
Arguments:
- queries: bfloat16 [4096, 8192], P('seq', 'head'), may hold values from -150 to 150
- keys: bfloat16 [4096, 1024], P('seq'), may hold values from -4 to 4
- values: bfloat16 [4096, 1024], P('seq'), may hold values from -6 to 6
- length: int32 [1], replicated, may hold values from 3585 to 4096
- mixer_values: bfloat16 [4096, 1024], P('seq'), may hold values from -6 to 6
- mixer_keys: bfloat16 [4096, 1024], P('seq'), may hold values from -6 to 6
- mixer_queries: bfloat16 [4096, 8192], P('seq', 'head'), may hold values from -0.5 to 0.5
- gate_values: bfloat16 [4096, 8192], P('seq', 'head'), may hold values from -6 to 6
- step_size: float32 [64, 4096], P('head', 'seq'), may hold values from 0.025 to 0.4
- decay_rate: float32 [64], P('head'), as said below
- skip_gain: float32 [64], P('head'), may hold values from 0.5 to 1.5
- out_weight: bfloat16 [8192, 8192], P('head'), may hold values from -0.0625 to 0.0625
Outputs:
- attn_heads: bfloat16 [4096, 8192], P('seq', 'head')
- ssm_out: bfloat16 [4096, 8192], P('seq', 'head')
- final_states: float32 [64, 128, 128], P('head', 'seq')
Inputs may be any that keep to these rules, and one draw needn't show every extreme that they name: `decay_rate`: positive.
All inputs are finite; a program needn't handle non-finite values.
Results may differ from a plain program's by a relative error of at most 0.022.
Values may be sent and summed in bfloat16 or wider, within the bound.
No kernel may reach another device: no remote copies, remote signals or barrier semaphores. Data moves between devices by JAX's collectives and lax.ppermute only.
A program may use at most 128 MiB of HBM per device.

v0:
```python
import math

import jax
import jax.numpy as jnp
from jax import lax
from jax.sharding import PartitionSpec as P

H = 64
KVH = 8
XG = 8
HD = 128
NST = 128


def prefix(value, axis, join, neutral):
    place = lax.axis_index(axis)
    gathered = jax.tree.map(
        lambda a, kind: lax.all_gather(a.astype(kind), axis), value, (jnp.bfloat16, jnp.bfloat16)
    )
    state = jax.tree.map(lambda a, e: jnp.zeros_like(a) + jnp.asarray(e, a.dtype), value, neutral)

    def one(step, state):
        return join(
            state,
            jax.tree.map(
                lambda a, own: lax.dynamic_index_in_dim(a, step, 0, False).astype(own.dtype),
                gathered,
                value,
            ),
        )

    return lax.fori_loop(0, place, one, state)


def broadcast(value, axis, root):
    mine = lax.axis_index(axis) == root
    return lax.psum(jnp.where(mine, value, jnp.zeros_like(value)), axis)


def attend(queries, keys, values, length):
    rows_here = queries.shape[0]
    heads_here = queries.shape[1] // HD
    shared_head = lax.axis_index("head") * heads_here // (H // KVH)
    key_block = lax.dynamic_slice_in_dim(keys, shared_head * HD, HD, 1)
    value_block = lax.dynamic_slice_in_dim(values, shared_head * HD, HD, 1)
    query_heads = queries.reshape(rows_here, heads_here, HD)
    query_pos = lax.axis_index("seq") * rows_here + jnp.arange(rows_here, dtype=jnp.int32)
    last_query = query_pos[rows_here - 1]
    limit = length[0]
    factor_scale = 1.0 / math.sqrt(HD)
    start_carry = (
        jnp.full((heads_here, rows_here), -1e30, jnp.float32),
        jnp.zeros((heads_here, rows_here), jnp.float32),
        jnp.zeros((heads_here, rows_here, HD), jnp.float32),
    )
    carry = start_carry
    key_piece = lax.all_gather(key_block, "seq", axis=0, tiled=True)
    value_piece = lax.all_gather(value_block, "seq", axis=0, tiled=True)
    count_rows = key_piece.shape[0]
    width = math.gcd(count_rows, 512)
    blocks = count_rows // width
    key_tiles = key_piece.reshape(blocks, width, HD)
    value_tiles = value_piece.reshape(blocks, width, HD)
    offsets = width * jnp.arange(blocks, dtype=jnp.int32)

    def update(state, item):
        key_tile, value_tile, offset = item
        best, total, summed = state
        key_pos = offset + jnp.arange(width, dtype=jnp.int32)
        allowed = (key_pos[None, :] <= query_pos[:, None]) & (key_pos[None, :] < limit)
        scores = (
            jnp.einsum("thd,sd->hts", query_heads, key_tile, preferred_element_type=jnp.float32)
            * factor_scale
        )
        scores = jnp.where(allowed[None], scores, -jnp.inf)
        new_best = jnp.maximum(best, jnp.max(scores, axis=2))
        weights = jnp.where(allowed[None], jnp.exp(scores - new_best[:, :, None]), 0.0)
        shrink = jnp.exp(best - new_best)
        total = total * shrink + jnp.sum(weights, axis=2)
        summed = summed * shrink[:, :, None] + jnp.einsum(
            "hts,sd->htd",
            weights.astype(jnp.bfloat16),
            value_tile,
            preferred_element_type=jnp.float32,
        )
        return (new_best, total, summed)

    def visit(state, item):
        return (
            lax.cond(
                item[2] > last_query, lambda inner: inner, lambda inner: update(inner, item), state
            ),
            None,
        )

    carry, unused = lax.scan(visit, carry, (key_tiles, value_tiles, offsets))
    best, total, summed = carry
    attended = summed / total[:, :, None]
    return attended.transpose(1, 0, 2).reshape(rows_here, heads_here * HD).astype(jnp.bfloat16)


def combine_states(earlier, later):
    return (earlier[0] * later[0], later[0][:, None, None] * earlier[1] + later[1])


def body(
    queries,
    keys,
    values,
    length,
    mixer_values,
    mixer_keys,
    mixer_queries,
    gate_values,
    step_size,
    decay_rate,
    skip_gain,
    out_weight,
):
    attn_heads = attend(queries, keys, values, length)
    rows_here = mixer_values.shape[0]
    heads_here = step_size.shape[0]
    group_here = lax.axis_index("head") * heads_here // (H // XG)
    input_vals = lax.dynamic_slice_in_dim(mixer_values, group_here * HD, HD, 1)
    input_keys = lax.dynamic_slice_in_dim(mixer_keys, group_here * NST, NST, 1)
    output_keys = mixer_queries.reshape(rows_here, heads_here, NST)
    gate_heads = gate_values.reshape(rows_here, heads_here, HD)
    positions = lax.axis_index("seq") * rows_here + jnp.arange(rows_here, dtype=jnp.int32)
    step = jnp.where(positions[None, :] < length[0], step_size, 0.0)
    cum = jnp.cumsum(-step * decay_rate[:, None], axis=1)
    local_pos = jnp.arange(rows_here, dtype=jnp.int32)
    causal = local_pos[:, None] >= local_pos[None, :]
    inner = jnp.einsum("thn,sn->hts", output_keys, input_keys, preferred_element_type=jnp.float32)
    diff = jnp.where(causal[None], cum[:, :, None] - cum[:, None, :], -jnp.inf)
    mix = (jnp.exp(diff) * inner * step[:, None, :]).astype(jnp.bfloat16)
    result = jnp.einsum("hts,sp->thp", mix, input_vals, preferred_element_type=jnp.float32)
    tail = jnp.exp(cum[:, -1:] - cum) * step
    weighted = input_vals.astype(jnp.float32)[None] * tail[:, :, None]
    local_state = jnp.einsum(
        "hsp,sn->hpn", weighted, input_keys.astype(jnp.float32), precision=lax.Precision.HIGHEST
    )
    block_log = cum[:, -1]
    block_decay = jnp.exp(block_log)
    identity = (jnp.ones_like(block_decay), jnp.zeros_like(local_state))
    prior_decay, previous = prefix((block_decay, local_state), "seq", combine_states, identity)
    ending = block_decay[:, None, None] * previous + local_state
    final_full = broadcast(ending.astype(jnp.bfloat16), "seq", lax.axis_size("seq") - 1).astype(
        ending.dtype
    )
    carried = jnp.einsum(
        "thn,hpn->thp", output_keys.astype(jnp.float32), previous, precision=lax.Precision.HIGHEST
    )
    result = result + jnp.exp(cum).T[:, :, None] * carried
    result = result + skip_gain[None, :, None] * input_vals.astype(jnp.float32)[:, None, :]
    gated = (
        (result * jax.nn.silu(gate_heads.astype(jnp.float32)))
        .astype(jnp.bfloat16)
        .reshape(rows_here, heads_here * HD)
    )
    share = HD // lax.axis_size("seq")
    final_states = lax.dynamic_slice_in_dim(final_full, lax.axis_index("seq") * share, share, 1)
    partial_terms = jnp.dot(gated, out_weight, preferred_element_type=jnp.float32)
    summed = lax.psum_scatter(
        partial_terms.astype(jnp.bfloat16), "head", scatter_dimension=1, tiled=True
    )
    return (attn_heads, summed, final_states)


def solution(mesh):
    placed = (
        P("seq", "head"),
        P("seq", None),
        P("seq", None),
        P(),
        P("seq", None),
        P("seq", None),
        P("seq", "head"),
        P("seq", "head"),
        P("head", "seq"),
        P("head"),
        P("head"),
        P("head", None),
    )
    return jax.shard_map(
        body,
        mesh=mesh,
        in_specs=placed,
        out_specs=(P("seq", "head"), P("seq", "head"), P("head", "seq", None)),
        check_vma=False,
    )
```

profile of v0, /device:TPU:0, one launch (start us, length us, event | category | flops | bytes accessed | tf_op | source)
XLA Modules:
  0.0 323.3 jit_solution(2563190595670413268)
XLA Ops:
  7.2 0.0 copy-start
  7.2 0.0 copy-start.2
  7.2 0.0 all-gather.10.cloned.1.call-start
  8.0 0.8 negate_multiply_fusion
  8.8 1.2 reduce-window.6
  10.0 0.2 slice_reduce_fusion
  10.2 0.2 reduce-window.9
  10.4 0.1 add_bitcast_fusion
  10.5 0.2 slice_reduce_fusion.1
  10.7 0.9 constant_dynamic-slice_fusion
  11.6 0.1 copy.38
  11.7 0.1 exponential_bitcast_fusion
  11.8 1.3 fusion.54
  13.1 0.0 all-gather.10.cloned.1.call-update
  13.1 0.0 all-gather.6.cloned.1.call-start
  13.2 1.6 constant_dynamic-slice_fusion.2
  14.8 0.0 all-gather.6.cloned.1.call-update
  14.8 0.0 all-gather.8.cloned.1.call-start
  14.8 1.6 constant_dynamic-slice_fusion.1
  16.4 0.0 all-gather.8.cloned.1.call-update
  16.5 0.0 all-reduce.3.cloned.1.call-start
  16.5 0.2 fusion.52
  16.7 0.1 iota_compare_fusion
  16.8 1.2 dynamic-slice
  18.6 0.2 dynamic-update-slice
  18.9 20.0 %all-reduce = bf16[32]{0:T(256)(128)(2,1)S(1)} all-reduce(bf16[32]{0:T(256)(128)(2,1)S(1)} %dynamic-update-slice), channel_id=2, replica_groups=mesh['seq'=8,'head'=16] {'seq'}, use_global_device_ids=true, to_apply=%add | all-reduce | flops 32 | bytes 128
  38.9 0.1 reshape.178
  38.9 1.3 copy.35
  40.2 0.0 copy-start.3
  40.2 3.7 %fusion.24 = f32[512,4,128]{0,2,1:T(8,128)} fusion(f32[4,512]{1,0:T(4,128)S(1)} %get-tuple-element.286, f32[4,512]{1,0:T(4,128)S(1)} %bitcast.125, pred[512,512]{0,1:T(8,128)(4,1)S(1)} %iota_compare_fusion, bf16[512,1024]{1,0:T(8,128)(2,1)S(1)} %copy-done, s32[]{:T(128)S(6)} %select_n.49, bf16[512,1024]{1,0:T(8,128)(2,1)} %param.22, ...), kind=kOutput, calls=%fused_computation.32 | convolution fusion | flops 542113792 | bytes 2122752 | tf_op jit(solution)/shard_map/hts,sp->thp/dot_general | solution.py:136
  43.9 11.1 %all-gather.10.cloned.1.call-done = bf16[32,128,128]{2,1,0:T(8,128)(2,1)} async-done(((bf16[4,128,128]{2,1,0:T(8,128)(2,1)}), bf16[32,128,128]{2,1,0:T(8,128)(2,1)}) %all-gather.10.cloned.1.call-update) | async-done | bytes 1048592 | tf_op jit(solution)/shard_map/all_gather | solution.py:18
  55.0 0.8 fusion.41
  55.8 0.0 all-reduce.3.cloned.1.call-update
  55.8 0.0 reduce-scatter.2.cloned.1.call-start
  55.9 2.1 fusion.29
  57.9 10.1 %convolution_convert_fusion = bf16[512,8192]{1,0:T(8,128)(2,1)} fusion(bf16[512,512]{0,1:T(8,128)(2,1)S(1)} %bitcast.120, bf16[512,8192]{1,0:T(8,128)(2,1)} %param.29), kind=kOutput, calls=%fused_computation.27 | convolution fusion | flops 4299161600 | bytes 17301504 | tf_op jit(solution)/shard_map/dot_general | solution.py:162
  68.1 0.0 reduce-scatter.2.cloned.1.call-update
  68.1 0.7 slice.13
  68.8 0.3 copy-done.1
  69.1 0.2 copy.28
  69.3 0.3 copy.29
  69.6 25.5 %all-gather.6.cloned.1.call-done = bf16[4096,128]{1,0:T(8,128)(2,1)} async-done(((bf16[512,128]{1,0:T(8,128)(2,1)}), bf16[4096,128]{1,0:T(8,128)(2,1)}) %all-gather.6.cloned.1.call-update) | async-done | bytes 1048592 | tf_op jit(solution)/shard_map/all_gather | solution.py:57
  95.1 39.6 %all-gather.8.cloned.1.call-done = bf16[4096,128]{1,0:T(8,128)(2,1)} async-done(((bf16[512,128]{1,0:T(8,128)(2,1)}), bf16[4096,128]{1,0:T(8,128)(2,1)}) %all-gather.8.cloned.1.call-update) | async-done | bytes 1048592 | tf_op jit(solution)/shard_map/all_gather | solution.py:58
  134.8 0.1 broadcast_in_dim.84
  134.8 22.4 %while.28 = (s32[]{:T(128)}, f32[4,512]{1,0:T(4,128)S(1)}, f32[4,512]{1,0:T(4,128)S(1)}, f32[4,512,128]{2,1,0:T(8,128)S(1)}, s32[8]{0:T(128)S(1)}, /*index=5*/s3...) while((s32[]{:T(128)}, f32[4,512]{1,0:T(4,128)S(1)}, ...), condition=%wide.region_5.6_spmd.clone, body=%wide.region_0.5_spmd.clone.sunk | while | flops 551557120 | bytes 16660783 | solution.py:96
  134.8 0.6 dynamic_slice.88
  136.7 7.4 %conditional.3 = (f32[4,512]{1,0:T(4,128)S(1)}, f32[4,512]{1,0:T(4,128)S(1)}, f32[4,512,128]{2,1,0:T(8,128)S(1)}) conditional(s32[]{:T(128)} %convert_element_type.120, (s32[]{:T(128)}, s32[]{:T(128)}, s32[]{:T(128)}, bf16[8,512,128]{2,1,0:T(8,128)(2,1)}, s32[]{:T(128)}, /*index=5*/bf16[512,4,128]{2,0,1:T(8,128)(2,1)S(1)}, f32[4,512]{1,0:T(4,128)S(1)}, ...), branch_computations={%region_1.3_spmd, %region_4.4_spmd} | conditional | flops 551557120 | bytes 16642088 | solution.py:90
  136.7 1.2 broadcast_compare_fusion
  137.9 0.6 iota_add_fusion
  138.4 0.2 compare_and_fusion
  138.7 1.8 fusion.2
  140.5 1.0 fusion.4
  141.5 2.5 fusion.8
  144.1 0.6 dynamic_slice.88
  146.0 0.6 dynamic_slice.88
  147.9 0.6 dynamic_slice.88
  149.8 0.6 dynamic_slice.88
  151.6 0.6 dynamic_slice.88
  153.5 0.6 dynamic_slice.88
  155.4 0.6 dynamic_slice.88
  157.3 1.1 copy_bitcast_fusion
  158.4 51.1 %all-reduce.3.cloned.1.call-done = bf16[4,128,128]{2,1,0:T(8,128)(2,1)} async-done(((bf16[4,128,128]{2,1,0:T(8,128)(2,1)}), bf16[4,128,128]{2,1,0:T(8,128)(2,1)}) %all-reduce.3.cloned.1.call-update) | async-done | bytes 131088 | tf_op jit(solution)/shard_map/psum | solution.py:37
  209.5 1.3 dynamic-slice_convert_fusion
  210.8 105.9 %reduce-scatter.2.cloned.1.call-done = bf16[512,512]{1,0:T(8,128)(2,1)} async-done(((bf16[512,8192]{1,0:T(8,128)(2,1)}), bf16[512,512]{1,0:T(8,128)(2,1)}) %reduce-scatter.2.cloned.1.call-update) | async-done | bytes 524304 | tf_op jit(solution)/shard_map/reduce_scatter | solution.py:163
  (48 shorter events, 0.4 us)
Async XLA Ops:
  7.2 4.6 %copy-start = (bf16[512,1024]{1,0:T(8,128)(2,1)S(1)}, bf16[512,1024]{1,0:T(8,128)(2,1)}, u32[]{:S(2)}) copy-start(bf16[512,1024]{1,0:T(8,128)(2,1)} %param.23) | copy-start | bytes 3145732
  7.2 33.0 %copy-start.2 = (bf16[512,512]{1,0:T(8,128)(2,1)S(1)}, bf16[512,512]{1,0:T(8,128)(2,1)}, u32[]{:S(2)}) copy-start(bf16[512,512]{1,0:T(8,128)(2,1)} %param.24) | copy-start | bytes 1572868
  7.2 47.8 %all-gather.10.cloned.1.call-start = ((), (), s32[]{:S(2)}) async-start(), calls=%async_computation.5 | async-start | bytes 1179648 | tf_op jit(solution)/shard_map/all_gather | solution.py:18
  13.1 81.9 %all-gather.6.cloned.1.call-start = ((), (), s32[]{:S(2)}) async-start(), calls=%async_computation.1 | async-start | bytes 1179648 | tf_op jit(solution)/shard_map/all_gather | solution.py:57
  14.8 119.9 %all-gather.8.cloned.1.call-start = ((), (), s32[]{:S(2)}) async-start(), calls=%async_computation.2 | async-start | bytes 1179648 | tf_op jit(solution)/shard_map/all_gather | solution.py:58
  16.5 193.0 %all-reduce.3.cloned.1.call-start = ((), (), s32[]{:S(2)}) async-start(), calls=%async_computation.4 | async-start | bytes 262144 | tf_op jit(solution)/shard_map/psum | solution.py:37
  40.2 15.6 %copy-start.3 = (f32[4]{0:T(128)S(1)}, f32[4]{0:T(128)}, u32[]{:S(2)}) copy-start(f32[4]{0:T(128)} %param.28) | copy-start | bytes 52
  55.8 260.9 %reduce-scatter.2.cloned.1.call-start = ((), (), s32[]{:S(2)}) async-start(), calls=%async_computation.3 | async-start | bytes 8912896 | tf_op jit(solution)/shard_map/reduce_scatter | solution.py:163
  68.1 1.0 copy-start.1
Sparse Core Ops, SparseCore 0:
  13.3 41.6 all-gather.9
  57.2 37.8 all-gather.5
  96.7 37.9 all-gather.7
  137.1 72.3 all-reduce.2
  214.8 101.9 reduce-scatter.1
where the time goes:
time: 324 us; the launch traced here: 323 us
  waiting for transfers between devices  233 us (72%)
  matrix products  21.5 us (7%)
  blocking collectives  20 us (6%)
  between operations  15.3 us (5%)
  local copies, waits for them, and re-layouts  13.5 us (4%)
  loops' own time  10.5 us (3%)
  other arithmetic  8.93 us (3%)
    reduce_scatter x1, waiting for transfers between devices, body(): lax.psum_scatter(partial_terms.astype(jnp.bfloat16), 'head', scatter_dime...  106 us
    psum x1, waiting for transfers between devices, broadcast(): return lax.psum(jnp.where(mine, value, jnp.zeros_like(value)), axis)  51.1 us
    all_gather x1, waiting for transfers between devices, attend(): value_piece = lax.all_gather(value_block, 'seq', axis=0, tiled=True)  39.6 us
    all_gather x1, waiting for transfers between devices, attend(): key_piece = lax.all_gather(key_block, 'seq', axis=0, tiled=True)  25.5 us
    unnamed x1, blocking collectives  20 us
    all_gather x1, waiting for transfers between devices, prefix(): lax.all_gather(a.astype(kind), axis)  11.1 us
    another operation x1, loops' own time, attend(): carry, unused = lax.scan(visit, carry, (key_tiles, value_tiles, offsets))  10.2 us
    dot_general x1, matrix products, body(): jnp.dot(gated, out_weight, preferred_element_type=jnp.float32)  10.1 us
  transfers between devices with their start and end apart: 5, of which 5 were waited for; matrix products, arithmetic and copies ran while one was open for 12% of the time, Pallas kernels for 0%

commit v1 on v0

v1 whole, which is shorter than its diff:
```python
import math

import jax
import jax.numpy as jnp
from jax import lax
from jax.experimental import pallas as pl
from jax.experimental.pallas import tpu as pltpu
from jax.sharding import PartitionSpec as P

H = 64
KVH = 8
HD = 128
NST = 128
TOK = 512
HEADS = 4
ROWS = HEADS * HD
MSG = ROWS + 32
CB = 256
BF = jnp.bfloat16
F32 = jnp.float32
NT = (((1,), (1,)), ((), ()))
VMEM_LIMIT = 48 * 1024 * 1024

SEQ, CORE, GROUP, LENGTH, YPOS, XLO, ZPOS, XHI = range(8)


def call(kernel, info, args, in_specs, out_specs, out_shape, grid=(1,), scratch=(), flops=0, nbytes=0, trans=0, alias=None, extra=()):
    spec = pltpu.PrefetchScalarGridSpec(
        num_scalar_prefetch=1 + len(extra),
        grid=grid,
        in_specs=in_specs,
        out_specs=out_specs,
        scratch_shapes=list(scratch),
    )
    return pl.pallas_call(
        kernel,
        grid_spec=spec,
        out_shape=out_shape,
        input_output_aliases=alias or {},
        compiler_params=pltpu.CompilerParams(vmem_limit_bytes=VMEM_LIMIT),
        cost_estimate=pl.CostEstimate(flops=flops, bytes_accessed=nbytes, transcendentals=trans),
    )(info, *extra, *args)


def full(shape):
    return pl.BlockSpec(shape, lambda i, *_: (0,) * len(shape))


def grouped():
    return pl.BlockSpec((TOK, HD), lambda i, info, *_: (0, info[GROUP]))


SMEM = pl.BlockSpec(memory_space=pltpu.SMEM)


def shape(dims, kind):
    return jax.ShapeDtypeStruct(dims, kind)


def split2(a):
    high = a.astype(BF)
    return high, (a - high.astype(F32)).astype(BF)


def prep_kernel(info, k_ref, v_ref, mv_ref, mk_ref, step_ref, rate_ref, kv_ref, msg_ref, cum_ref):
    @pl.when(info[CORE] == 0)
    def _():
        kv_ref[...] = k_ref[...]

    @pl.when(info[CORE] == 1)
    def _():
        for i in range(TOK // HD):
            part = pl.ds(i * HD, HD)
            kv_ref[part, :] = v_ref[part, :].astype(F32).T.astype(BF)

    row = lax.broadcasted_iota(jnp.int32, (8, TOK), 0)
    lane = lax.broadcasted_iota(jnp.int32, (8, TOK), 1)
    step = jnp.concatenate([step_ref[...], jnp.zeros((8 - HEADS, TOK), F32)], axis=0)
    step = jnp.where(info[SEQ] * TOK + lane < info[LENGTH], step, 0.0)
    rate = jnp.zeros((8, TOK), F32)
    for h in range(HEADS):
        rate = jnp.where(row == h, rate_ref[h], rate)
    cum = -step * rate
    shift = 1
    while shift < TOK:
        cum = cum + jnp.where(lane >= shift, pltpu.roll(cum, shift, 1), 0.0)
        shift *= 2
    cum_ref[0:8, :] = cum
    cum_ref[8:16, :] = step
    last = cum[:, TOK - 1 : TOK]
    tail = jnp.exp(last - cum) * step
    log = jnp.broadcast_to(last, (8, HD))
    high = log.astype(BF).astype(F32)
    mid = (log - high).astype(BF).astype(F32)
    low = log - high - mid
    msg_ref[ROWS:MSG, :] = jnp.concatenate([high, mid, low, jnp.zeros_like(low)], axis=0).astype(BF)
    vt = mv_ref[...].astype(F32).T
    mk = mk_ref[...]
    for h in range(HEADS):
        high, low = split2(vt * tail[h : h + 1, :])
        state = jnp.dot(high, mk, preferred_element_type=F32) + jnp.dot(low, mk, preferred_element_type=F32)
        msg_ref[h * HD : (h + 1) * HD, :] = state.astype(BF)


def log_of(msg):
    tail = msg[ROWS:MSG, :].astype(F32)
    return tail[0:8] + tail[8:16] + tail[16:24]


def combine_kernel(info, m0, m1, m2, m3, prefix_ref, pdec_ref, total_ref):
    y = info[YPOS]
    msgs = (m0, m1, m2, m3)
    place = [lax.rem(y - d + 4, 4) for d in range(4)]
    logs = [log_of(m) for m in msgs]
    pre, tot = [], []
    for d in range(4):
        in_pre = jnp.zeros_like(logs[0])
        in_tot = jnp.zeros_like(logs[0])
        for e in range(4):
            if e == d:
                continue
            after = place[e] > place[d]
            in_tot = in_tot + jnp.where(after, logs[e], 0.0)
            in_pre = in_pre + jnp.where(jnp.logical_and(after, place[e] < y), logs[e], 0.0)
        tot.append(jnp.exp(in_tot))
        pre.append(jnp.where(place[d] < y, jnp.exp(in_pre), 0.0))
    whole = logs[0] + logs[1] + logs[2] + logs[3]
    before = jnp.zeros_like(whole)
    for e in range(4):
        before = before + jnp.where(place[e] < y, logs[e], 0.0)
    pdec_ref[...] = jnp.exp(before)
    for h in range(HEADS):
        part = slice(h * HD, (h + 1) * HD)
        own = [m[part, :].astype(F32) for m in msgs]
        total = own[0] * tot[0][h : h + 1]
        prefix = own[1] * pre[1][h : h + 1]
        for d in range(1, 4):
            total = total + own[d] * tot[d][h : h + 1]
        for d in range(2, 4):
            prefix = prefix + own[d] * pre[d][h : h + 1]
        prefix_ref[part, :] = prefix
        total_ref[part, :] = total.astype(BF)
    high = whole.astype(BF).astype(F32)
    mid = (whole - high).astype(BF).astype(F32)
    low = whole - high - mid
    total_ref[ROWS:MSG, :] = jnp.concatenate([high, mid, low, jnp.zeros_like(low)], axis=0).astype(BF)


def intra_kernel(info, cum_ref, c_ref, mk_ref, mv_ref, skip_ref, y_ref):
    cum = cum_ref[0:8, :]
    step = cum_ref[8:16, :]
    cols = cum.T
    half = TOK // 2
    for h in range(HEADS):
        part = slice(h * HD, (h + 1) * HD)
        for i in range(2):
            here = slice(i * half, (i + 1) * half)
            wide = (i + 1) * half
            inner = lax.dot_general(c_ref[here, part], mk_ref[0:wide, :], NT, preferred_element_type=F32)
            t = i * half + lax.broadcasted_iota(jnp.int32, (half, wide), 0)
            s = lax.broadcasted_iota(jnp.int32, (half, wide), 1)
            diff = jnp.where(s <= t, cols[here, h : h + 1] - cum[h : h + 1, 0:wide], -jnp.inf)
            mix = (jnp.exp(diff) * inner * step[h : h + 1, 0:wide]).astype(BF)
            y = jnp.dot(mix, mv_ref[0:wide, :], preferred_element_type=F32)
            y_ref[here, part] = y + skip_ref[h] * mv_ref[here, :].astype(F32)


def gate_kernel(info, cum_ref, c_ref, y_ref, g_ref, prefix_ref, pdec_ref, own_ref, got_ref, out_ref, fin_ref):
    second = info[XLO] == 1
    ecols = jnp.exp(cum_ref[0:8, :]).T
    for h in range(HEADS):
        part = slice(h * HD, (h + 1) * HD)
        far = pdec_ref[h : h + 1, :] * got_ref[part, :].astype(F32)
        state = prefix_ref[part, :] + jnp.where(second, far, 0.0)
        high, low = split2(state)
        c = c_ref[:, part]
        carried = lax.dot_general(
            jnp.concatenate([c, c], axis=1), jnp.concatenate([high, low], axis=1), NT, preferred_element_type=F32
        )
        y = y_ref[:, part] + ecols[:, h : h + 1] * carried
        g = g_ref[:, part].astype(F32)
        out_ref[:, part] = (y * (g / (1.0 + jnp.exp(-g)))).astype(BF)
    own_log = log_of(own_ref)
    got_log = log_of(got_ref)
    later = jnp.exp(jnp.where(second, own_log, got_log))
    for h in range(HEADS):
        rows = pl.ds(pl.multiple_of(h * HD + info[SEQ] * (HD // 8), HD // 8), HD // 8)
        own = own_ref[rows, :].astype(F32)
        got = got_ref[rows, :].astype(F32)
        first = jnp.where(second, got, own)
        last = jnp.where(second, own, got)
        fin_ref[h] = last + later[h : h + 1, :] * first


def place_kernel(info, *refs):
    mine, other, (k_ref, v_ref) = refs[0:5], refs[5:10], refs[10:12]
    zero = info[CORE] == 0
    y, x = info[YPOS], info[XLO]

    def put(a, b, where):
        rows = pl.ds(pl.multiple_of(where * TOK, TOK), TOK)
        a, b = a.astype(F32), b.astype(F32)
        k_ref[rows, :] = jnp.where(zero, a, b).astype(BF)
        v_ref[rows, :] = jnp.where(zero, b, a).astype(BF)

    put(mine[0][...], other[0][...], x * 4 + y)
    put(mine[1][...], other[1][...], (1 - x) * 4 + y)
    for d in range(1, 4):
        ypos = lax.rem(y - d + 4, 4)
        put(mine[d + 1][0:TOK, :], other[d + 1][0:TOK, :], x * 4 + ypos)
        put(mine[d + 1][TOK : 2 * TOK, :], other[d + 1][TOK : 2 * TOK, :], (1 - x) * 4 + ypos)


def attend_kernel(info, q_ref, k_ref, v_ref, *rest):
    out_ref = rest[-1]
    seq = info[SEQ]
    scale = math.log2(math.e) / math.sqrt(HD)
    half = TOK // 2
    queries = [q_ref[i * half : (i + 1) * half, :] for i in range(2)]
    ones = jnp.ones((16, TOK), BF)

    def tile(j):
        base = pl.multiple_of(j * TOK, TOK)
        k = k_ref[pl.ds(base, TOK), :]
        vt = jnp.concatenate([v_ref[pl.ds(base + i * HD, HD), :] for i in range(TOK // HD)], axis=1)
        return k, jnp.concatenate([vt, ones], axis=0)

    k, vt = tile(seq)
    state = []
    for i in range(2):
        wide = (i + 1) * half
        scores = lax.dot_general(k[0:wide], queries[i], NT, preferred_element_type=F32)
        s = lax.broadcasted_iota(jnp.int32, (wide, half), 0)
        t = i * half + lax.broadcasted_iota(jnp.int32, (wide, half), 1)
        keep = jnp.logical_and(s <= t, s < info[LENGTH] - seq * TOK)
        scores = jnp.where(keep, scores, -jnp.inf)
        best = jnp.max(scores, axis=0, keepdims=True)
        weights = jnp.exp2((scores - best) * scale).astype(BF)
        state += [best, jnp.dot(vt[:, 0:wide], weights, preferred_element_type=F32)]

    def one(j, state):
        k, vt = tile(j)
        new = []
        for i in range(2):
            best, summed = state[2 * i], state[2 * i + 1]
            scores = lax.dot_general(k, queries[i], NT, preferred_element_type=F32)
            top = jnp.maximum(best, jnp.max(scores, axis=0, keepdims=True))
            weights = jnp.exp2((scores - top) * scale).astype(BF)
            shrink = jnp.exp2((best - top) * scale)
            new += [top, summed * shrink + jnp.dot(vt, weights, preferred_element_type=F32)]
        return tuple(new)

    state = lax.fori_loop(0, seq, one, tuple(state))
    for i in range(2):
        summed = state[2 * i + 1]
        out = summed[0:HD] * (1.0 / summed[HD : HD + 1])
        out_ref[i * half : (i + 1) * half, :] = out.T.astype(BF)


def project_kernel(n_got, info, columns, *refs):
    g0, g1, w0, w1 = refs[0:4]
    got, out_ref = refs[4 : 4 + n_got], refs[4 + n_got]
    acc = jnp.dot(g0[...], w0[...], preferred_element_type=F32) + jnp.dot(
        g1[...], w1[...], preferred_element_type=F32
    )
    for r in got:
        acc = acc + r[...].reshape(TOK, CB).astype(F32)
    out_ref[...] = acc.astype(BF).reshape(out_ref.shape)


def project(info, operands, columns, got=(), got_specs=()):
    n = columns.shape[0]
    weight = pl.BlockSpec((TOK, CB), lambda i, info, columns: (0, columns[i]))
    return call(
        lambda *refs: project_kernel(len(got), *refs),
        info,
        (*operands, *got),
        [full((TOK, TOK)), full((TOK, TOK)), weight, weight, *got_specs],
        pl.BlockSpec((1, TOK, CB), lambda i, *_: (i, 0, 0)),
        shape((n, TOK, CB), BF),
        grid=(n,),
        flops=2 * n * TOK * 1024 * CB,
        nbytes=n * 1024 * CB * 2 + 2**20,
        extra=(columns,),
    )


def finish_kernel(info, columns, g0, g1, w0, w1, a1, a2, a3, ax, b1, b2, b3, bx, out_ref):
    acc = jnp.dot(g0[...], w0[...], preferred_element_type=F32) + jnp.dot(
        g1[...], w1[...], preferred_element_type=F32
    )

    @pl.when(pl.program_id(0) == 0)
    def _():
        total = acc
        for r in (a1, a2, a3):
            total = total + r[0].astype(F32)
        out_ref[...] = (total + ax[0].astype(F32)).astype(BF)

    @pl.when(pl.program_id(0) == 1)
    def _():
        total = acc + bx[0].astype(F32)
        for r in (b1, b2, b3):
            total = total + r[0].astype(F32)
        out_ref[...] = total.astype(BF)


def head_perm(move):
    pairs = []
    for z in range(4):
        for x in range(2):
            for c in range(2):
                z2, x2, c2 = move(z, x, c)
                pairs.append((z * 4 + x * 2 + c, (z2 % 4) * 4 + (x2 % 2) * 2 + c2 % 2))
    return pairs


CORE_SWAP = head_perm(lambda z, x, c: (z, x, c + 1))
X_SWAP = head_perm(lambda z, x, c: (z, x + 1, c))
Z_MOVE = {d: head_perm(lambda z, x, c, d=d: (z + d, x, c)) for d in (1, 2, 3)}
LO_SWAP = [(i, (i + 4) % 8) for i in range(8)]
Y_MOVE = {d: [(x * 4 + y, x * 4 + (y + d) % 4) for x in range(2) for y in range(4)] for d in (1, 2, 3)}


def body(
    queries,
    keys,
    values,
    length,
    mixer_values,
    mixer_keys,
    mixer_queries,
    gate_values,
    step_size,
    decay_rate,
    skip_gain,
    out_weight,
):
    seq = lax.axis_index("seq")
    head = lax.axis_index("head")
    z, x, c = head // 4, (head // 2) % 2, head % 2
    info = jnp.stack([seq, c, head // 2, length[0], seq % 4, seq // 4, z, x]).astype(jnp.int32)
    core = lambda a: lax.ppermute(a, "head", CORE_SWAP)
    lo = lambda a: lax.ppermute(a, "seq", LO_SWAP)
    along_y = lambda a, d: lax.ppermute(a, "seq", Y_MOVE[d])
    along_z = lambda a, d: lax.ppermute(a, "head", Z_MOVE[d])

    far_weight = core(out_weight)

    kv, msg, cum = call(
        prep_kernel,
        info,
        (keys, values, mixer_values, mixer_keys, step_size, decay_rate),
        [grouped(), grouped(), grouped(), grouped(), full((HEADS, TOK)), SMEM],
        [full((TOK, HD)), full((MSG, HD)), full((16, TOK))],
        [shape((TOK, HD), BF), shape((MSG, HD), BF), shape((16, TOK), F32)],
        flops=2 * 2 * TOK * TOK * HD,
        nbytes=2**20,
    )
    msgs = [msg] + [along_y(msg, d) for d in (1, 2, 3)]
    kv_far = lo(kv)

    y_in = call(
        intra_kernel,
        info,
        (cum, mixer_queries, mixer_keys, mixer_values, skip_gain),
        [full((16, TOK)), full((TOK, ROWS)), grouped(), grouped(), SMEM],
        full((TOK, ROWS)),
        shape((TOK, ROWS), F32),
        flops=4 * 2 * 2 * TOK * TOK * HD,
        nbytes=2**21,
        trans=4 * TOK * TOK,
    )
    prefix, pdec, total = call(
        combine_kernel,
        info,
        msgs,
        [full((MSG, HD))] * 4,
        [full((ROWS, HD)), full((8, HD)), full((MSG, HD))],
        [shape((ROWS, HD), F32), shape((8, HD), F32), shape((MSG, HD), BF)],
        flops=2**20,
        nbytes=2**20,
    )
    total_far = lo(total)
    gated, final_states = call(
        gate_kernel,
        info,
        (cum, mixer_queries, y_in, gate_values, prefix, pdec, total, total_far),
        [
            full((16, TOK)),
            full((TOK, ROWS)),
            full((TOK, ROWS)),
            full((TOK, ROWS)),
            full((ROWS, HD)),
            full((8, HD)),
            full((MSG, HD)),
            full((MSG, HD)),
        ],
        [full((TOK, ROWS)), full((HEADS, HD // 8, NST))],
        [shape((TOK, ROWS), BF), shape((HEADS, HD // 8, NST), F32)],
        flops=4 * 2 * TOK * 256 * HD,
        nbytes=2**21,
    )
    far_gated = core(gated)

    kv_pair = jnp.concatenate([kv, kv_far], axis=0)
    mine = [kv, kv_far] + [along_y(kv_pair, d) for d in (1, 2, 3)]
    other = [core(a) for a in mine]
    pieces = [full((TOK, HD))] * 2 + [full((2 * TOK, HD))] * 3
    k_all, v_all = call(
        place_kernel,
        info,
        (*mine, *other),
        pieces * 2,
        [full((8 * TOK, HD))] * 2,
        [shape((8 * TOK, HD), BF)] * 2,
        flops=2**20,
        nbytes=2**22,
    )
    attended = None
    for h in range(HEADS):
        column = pl.BlockSpec((TOK, HD), lambda i, info, h=h: (0, h))
        prior = () if attended is None else (attended,)
        attended = call(
            attend_kernel,
            info,
            (queries, k_all, v_all, *prior),
            [column, full((8 * TOK, HD)), full((8 * TOK, HD))] + [pl.BlockSpec(memory_space=pl.ANY)] * len(prior),
            column,
            shape((TOK, ROWS), BF),
            flops=2 * 2 * TOK * HD * TOK * 8,
            nbytes=2**21,
            trans=8 * TOK * TOK,
            alias={4: 0} if prior else None,
        )

    operands = (gated, far_gated, out_weight, far_weight)
    block = lambda zz, xx, half: ((zz % 4) * 4 + (xx % 2) * 2 + c) * 2 + half
    cols = lambda items: jnp.stack(items).astype(jnp.int32)

    to_x = project(info, operands, cols([block(i, x + 1, 1) for i in range(4)]))
    from_x = lax.ppermute(to_x, "head", X_SWAP)
    from_z = {}
    for d in (2, 1, 3):
        to_z = project(info, operands, cols([block(z + d, i, 0) for i in range(2)]))
        from_z[d] = along_z(to_z, d)

    arrived = [from_z[d] for d in (1, 2, 3)]
    turned = pl.BlockSpec((1, TOK, CB), lambda i, info, columns: (1 - info[XHI], 0, 0))
    to_x2 = project(info, operands, cols([block(z, x + 1, 0)]), arrived, [turned] * 3)
    from_x2 = lax.ppermute(to_x2, "head", X_SWAP)
    from_z2 = {}
    for d in (2, 1, 3):
        row = pl.BlockSpec((1, TOK, CB), lambda i, info, columns, d=d: (lax.rem(info[ZPOS] + d, 4), 0, 0))
        to_z2 = project(info, operands, cols([block(z + d, x, 1)]), [from_x], [row])
        from_z2[d] = along_z(to_z2, d)

    own_x = pl.BlockSpec((1, TOK, CB), lambda i, info, columns: (info[XHI], 0, 0))
    own_z = pl.BlockSpec((1, TOK, CB), lambda i, info, columns: (info[ZPOS], 0, 0))
    one = full((1, TOK, CB))
    weight = pl.BlockSpec((TOK, CB), lambda i, info, columns: (0, columns[i]))
    summed = call(
        finish_kernel,
        info,
        (*operands, *arrived, from_x2, from_z2[1], from_z2[2], from_z2[3], from_x),
        [full((TOK, TOK)), full((TOK, TOK)), weight, weight, own_x, own_x, own_x, one, one, one, one, own_z],
        pl.BlockSpec((TOK, CB), lambda i, *_: (0, i)),
        shape((TOK, ROWS), BF),
        grid=(2,),
        flops=2 * 2 * TOK * 1024 * CB,
        nbytes=2**22,
        extra=(cols([block(z, x, 0), block(z, x, 1)]),),
    )
    return (attended, summed, final_states)


def solution(mesh):
    placed = (
        P("seq", "head"),
        P("seq", None),
        P("seq", None),
        P(),
        P("seq", None),
        P("seq", None),
        P("seq", "head"),
        P("seq", "head"),
        P("head", "seq"),
        P("head"),
        P("head"),
        P("head", None),
    )
    return jax.shard_map(
        body,
        mesh=mesh,
        in_specs=placed,
        out_specs=(P("seq", "head"), P("seq", "head"), P("head", "seq", None)),
        check_vma=False,
    )
```

time: 324 us -> 141 us (0.44)
  the two profiles are of different devices: /device:TPU:0 before, /device:TPU:94 now
where the time goes in v1:
time: 141 us; the launch traced here: 140 us
  Pallas kernels  72.1 us (51%)
  waiting for transfers between devices  25.6 us (18%)
  starting transfers between devices  23.7 us (17%)
  local copies, waits for them, and re-layouts  16.4 us (12%)
  between operations  1.51 us (1%)
    pallas_call x18, Pallas kernels, call(): pl.pallas_call(kernel, grid_spec=spec, out_shape=out_shape, input_output_...  72.1 us
    unnamed x39, local copies, waits for them, and re-layouts  16.3 us
    ppermute x6, waiting for transfers between devices, body(): along_y = lambda a, d: lax.ppermute(a, 'seq', Y_MOVE[d])  13.9 us
    ppermute x6, starting transfers between devices, body(): along_z = lambda a, d: lax.ppermute(a, 'head', Z_MOVE[d])  9.79 us
    ppermute x6, starting transfers between devices, body(): along_y = lambda a, d: lax.ppermute(a, 'seq', Y_MOVE[d])  7.45 us
    ppermute x6, waiting for transfers between devices, body(): along_z = lambda a, d: lax.ppermute(a, 'head', Z_MOVE[d])  5.35 us
    ppermute x2, waiting for transfers between devices, body(): lo = lambda a: lax.ppermute(a, 'seq', LO_SWAP)  4.63 us
  transfers between devices with their start and end apart: 23, of which 6 were waited for; matrix products, arithmetic and copies ran while one was open for 0% of the time, Pallas kernels for 49%

profile of v1, /device:TPU:94, one launch (start us, length us, event | category | flops | bytes accessed | tf_op | source)
XLA Modules:
  0.0 139.7 jit_solution(11559423157139368465)
XLA Ops:
  0.6 0.1 collective-permute-start.14
  1.4 0.1 stack.94.info.refs_0_
  1.5 1.2 copy-done
  2.7 1.2 copy-done.2
  4.0 1.2 copy-done.6
  5.2 1.2 copy-done.7
  6.4 0.7 copy-done.15
  7.1 0.7 copy-done.16
  7.8 2.1 %shard_map.139 = (bf16[512,128]{1,0:T(8,128)(2,1)S(1)}, bf16[544,128]{1,0:T(8,128)(2,1)S(1)}, f32[16,512]{1,0:T(8,128)S(1)}) custom-call(s32[8]{0:T(128)S(1)} %stack.94.info.refs_0_, bf16[512,1024]{1,0:T(8,128)(2,1)S(1)} %copy-done.6, bf16[512,1024]{1,0:T(8,128)(2,1)S(1)} %copy-done.7, bf16[512,1024]{1,0:T(8,128)(2,1)S(1)} %copy-done, ...), custom_call_target="tpu_custom_call" | custom-call | flops 134217728 | bytes 1048576 | tf_op jit(solution)/shard_map/pallas_call | solution.py:35
  9.9 1.3 collective-permute-start.10
  11.2 3.2 %collective-permute-start.9 = (bf16[544,128]{1,0:T(8,128)(2,1)S(1)}, bf16[544,128]{1,0:T(8,128)(2,1)S(1)}, u32[]{:S(2)}, u32[]{:S(2)}) collective-permute-start(bf16[544,128]{1,0:T(8,128)(2,1)S(1)} %get-tuple-element.17.m0), channel_id=1, source_target_pairs={{0,16},{16,32},{32,48},{48,0},{64,80},{80,96},{96,112},{112,64},{1... | collective-permute-start | bytes 417800 | tf_op jit(solution)/shard_map/ppermute | solution.py:345
  14.4 3.5 %collective-permute-done.10.m2 = bf16[544,128]{1,0:T(8,128)(2,1)S(1)} collective-permute-done((bf16[544,128]{1,0:T(8,128)(2,1)S(1)}, bf16[544,128]{1,0:T(8,128)(2,1)S(1)}, u32[]{:S(2)}, u32[]{:S(2)}) %collective-permute-start.10) | collective-permute-done | bytes 139296 | tf_op jit(solution)/shard_map/ppermute | solution.py:345
  18.0 2.6 %collective-permute-done.11.m3 = bf16[544,128]{1,0:T(8,128)(2,1)S(1)} collective-permute-done((bf16[544,128]{1,0:T(8,128)(2,1)S(1)}, bf16[544,128]{1,0:T(8,128)(2,1)S(1)}, u32[]{:S(2)}, u32[]{:S(2)}) %collective-permute-start.11) | collective-permute-done | bytes 139296 | tf_op jit(solution)/shard_map/ppermute | solution.py:345
  20.6 0.7 shard_map.146
  21.3 0.9 collective-permute-start.12
  22.3 1.2 copy-done.1
  23.5 1.2 copy-done.3
  24.7 1.0 copy-done.4
  25.7 0.7 copy-done.17
  26.4 2.8 %shard_map.145.y_ref = f32[512,512]{1,0:T(8,128)S(1)} custom-call(s32[8]{0:T(128)S(1)} %stack.94.info.refs_0_, f32[16,512]{1,0:T(8,128)S(1)} %get-tuple-element.16.cum_ref, bf16[512,512]{1,0:T(8,128)(2,1)S(1)} %copy-done.4, bf16[512,1024]{1,0:T(8,128)(2,1)S(1)} %copy-done.3, bf16[512,1024]{1,0:T(8,128)(2,1)S(1)} %copy-done.1, f32[4]{0:T(128)S(1)} %copy-done.17), custom_call_target="tpu_custom_call" | custom-call | flops 536870912 | bytes 2097152 | tf_op jit(solution)/shard_map/pallas_call | solution.py:35
  29.2 1.8 %shard_map.147 = (bf16[512,512]{1,0:T(8,128)(2,1)S(1)}, f32[4,16,128]{2,1,0:T(8,128)}) custom-call(s32[8]{0:T(128)S(1)} %stack.94.info.refs_0_, f32[16,512]{1,0:T(8,128)S(1)} %get-tuple-element.16.cum_ref, bf16[512,512]{1,0:T(8,128)(2,1)S(1)} %copy-done.5, f32[512,512]{1,0:T(8,128)S(1)} %shard_map.145.y_ref, bf16[512,512]{1,0:T(8,128)(2,1)S(1)} %copy-done.8, ...), custom_call_target="tpu_custom_call" | custom-call | flops 134217728 | bytes 2097152 | tf_op jit(solution)/shard_map/pallas_call | solution.py:35
  31.0 1.2 collective-permute-start
  32.2 0.1 pad_add_fusion.4.refs_1_
  32.3 4.6 %collective-permute-done.refs_1_ = bf16[512,128]{1,0:T(8,128)(2,1)S(1)} collective-permute-done((bf16[512,128]{1,0:T(8,128)(2,1)S(1)}, bf16[512,128]{1,0:T(8,128)(2,1)S(1)}, u32[]{:S(2)}, u32[]{:S(2)}) %collective-permute-start) | collective-permute-done | bytes 131104 | tf_op jit(solution)/shard_map/ppermute | solution.py:344
  36.9 0.7 collective-permute-start.1
  37.7 5.0 %shard_map.152 = bf16[4,512,256]{2,1,0:T(8,128)(2,1)} custom-call(s32[8]{0:T(128)S(1)} %stack.94.info.refs_0_, s32[4]{0:T(128)S(1)} %pad_add_fusion.4.refs_1_, bf16[512,512]{1,0:T(8,128)(2,1)S(1)} %get-tuple-element.21.refs_2_.g0, bf16[512,512]{1,0:T(8,128)(2,1)S(1)} %collective-permute-done.13.refs_3_.g1, bf16[512,8192]{1,0:T(8,128)(2,1)} %w0.1, ...), custom_call_target="tpu_custom_call" | custom-call | flops 1073741824 | bytes 3145728 | tf_op jit(solution)/shard_map/pallas_call | solution.py:35
  42.6 1.1 collective-permute-start.19
  43.7 2.2 %collective-permute-start.2 = (bf16[1024,128]{1,0:T(8,128)(2,1)S(1)}, bf16[1024,128]{1,0:T(8,128)(2,1)}, u32[]{:S(2)}, u32[]{:S(2)}) collective-permute-start(bf16[1024,128]{1,0:T(8,128)(2,1)S(1)} %constant_dynamic-update-slice_fusion), channel_id=1, source_target_pairs={{0,32},{16,48},{32,0},{48,16},{64,96},{80,112},{96,64},{112,80},{1... | collective-permute-start | bytes 786440 | tf_op jit(solution)/shard_map/ppermute | solution.py:345
  45.9 0.1 pad_add_fusion.3.refs_1_
  46.0 0.1 pad_add_fusion.2.refs_1_
  46.1 0.0 collective-permute-start.3
  46.1 0.3 collective-permute-start.6
  46.4 0.1 pad_add_fusion.1.refs_1_
  46.5 0.3 collective-permute-start.5
  46.8 7.7 %collective-permute-done.2.refs_3_ = bf16[1024,128]{1,0:T(8,128)(2,1)} collective-permute-done((bf16[1024,128]{1,0:T(8,128)(2,1)S(1)}, bf16[1024,128]{1,0:T(8,128)(2,1)}, u32[]{:S(2)}, u32[]{:S(2)}) %collective-permute-start.2) | collective-permute-done | bytes 262176 | tf_op jit(solution)/shard_map/ppermute | solution.py:345
  54.5 3.2 %shard_map.150 = bf16[2,512,256]{2,1,0:T(8,128)(2,1)} custom-call(s32[8]{0:T(128)S(1)} %stack.94.info.refs_0_, s32[2]{0:T(128)S(1)} %pad_add_fusion.3.refs_1_, bf16[512,512]{1,0:T(8,128)(2,1)S(1)} %get-tuple-element.21.refs_2_.g0, bf16[512,512]{1,0:T(8,128)(2,1)S(1)} %collective-permute-done.13.refs_3_.g1, bf16[512,8192]{1,0:T(8,128)(2,1)} %w0.1, ...), custom_call_target="tpu_custom_call" | custom-call | flops 536870912 | bytes 2097152 | tf_op jit(solution)/shard_map/pallas_call | solution.py:35
  57.7 3.2 %shard_map.149 = bf16[2,512,256]{2,1,0:T(8,128)(2,1)} custom-call(s32[8]{0:T(128)S(1)} %stack.94.info.refs_0_, s32[2]{0:T(128)S(1)} %pad_add_fusion.2.refs_1_, bf16[512,512]{1,0:T(8,128)(2,1)S(1)} %get-tuple-element.21.refs_2_.g0, bf16[512,512]{1,0:T(8,128)(2,1)S(1)} %collective-permute-done.13.refs_3_.g1, bf16[512,8192]{1,0:T(8,128)(2,1)} %w0.1, ...), custom_call_target="tpu_custom_call" | custom-call | flops 536870912 | bytes 2097152 | tf_op jit(solution)/shard_map/pallas_call | solution.py:35
  60.9 3.2 %shard_map.148 = bf16[2,512,256]{2,1,0:T(8,128)(2,1)} custom-call(s32[8]{0:T(128)S(1)} %stack.94.info.refs_0_, s32[2]{0:T(128)S(1)} %pad_add_fusion.1.refs_1_, bf16[512,512]{1,0:T(8,128)(2,1)S(1)} %get-tuple-element.21.refs_2_.g0, bf16[512,512]{1,0:T(8,128)(2,1)S(1)} %collective-permute-done.13.refs_3_.g1, bf16[512,8192]{1,0:T(8,128)(2,1)} %w0.1, ...), custom_call_target="tpu_custom_call" | custom-call | flops 536870912 | bytes 2097152 | tf_op jit(solution)/shard_map/pallas_call | solution.py:35
  64.1 0.7 copy-done.13
  64.8 0.1 collective-permute-start.17
  64.9 3.6 %collective-permute-start.16 = (bf16[2,512,256]{2,1,0:T(8,128)(2,1)}, bf16[2,512,256]{2,1,0:T(8,128)(2,1)S(1)}, u32[]{:S(2)}, u32[]{:S(2)}) collective-permute-start(bf16[2,512,256]{2,1,0:T(8,128)(2,1)} %shard_map.149), channel_id=1, source_target_pairs={{0,8},{1,9},{2,10},{3,11},{4,12},{5,13},{6,14},{7,15},{8,0},{9,1},... | collective-permute-start | bytes 1572872 | tf_op jit(solution)/shard_map/ppermute | solution.py:346
  68.5 0.7 copy-done.9
  69.2 0.7 copy-done.11
  69.9 0.1 pad_add_fusion.columns
  70.0 1.8 %collective-permute-done.8.refs_9_ = bf16[1024,128]{1,0:T(8,128)(2,1)} collective-permute-done((bf16[1024,128]{1,0:T(8,128)(2,1)}, bf16[1024,128]{1,0:T(8,128)(2,1)}, u32[]{:S(2)}, u32[]{:S(2)}) %collective-permute-start.8) | collective-permute-done | bytes 262176 | tf_op jit(solution)/shard_map/ppermute | solution.py:343
  71.8 0.9 copy-done.10
  72.7 0.9 copy-done.12
  73.7 0.9 copy-done.14
  74.6 2.2 %shard_map.140 = (bf16[4096,128]{1,0:T(8,128)(2,1)S(1)}, bf16[4096,128]{1,0:T(8,128)(2,1)S(1)}) custom-call(s32[8]{0:T(128)S(1)} %stack.94.info.refs_0_, bf16[512,128]{1,0:T(8,128)(2,1)S(1)} %get-tuple-element.13.refs_0_, bf16[512,128]{1,0:T(8,128)(2,1)S(1)} %collective-permute-done.refs_1_, bf16[1024,128]{1,0:T(8,128)(2,1)} %collective-permute-done.1.refs_2_, ...), custom_call_target="tpu_custom_call" | custom-call | flops 1048576 | bytes 4194304 | tf_op jit(solution)/shard_map/pallas_call | solution.py:35
  76.8 1.0 copy-done.18
  77.9 9.2 %shard_map.141.rest_0_ = bf16[512,512]{1,0:T(8,128)(2,1)} custom-call(s32[8]{0:T(128)S(1)} %stack.94.info.refs_0_, bf16[512,512]{1,0:T(8,128)(2,1)S(1)} %copy-done.18, bf16[4096,128]{1,0:T(8,128)(2,1)S(1)} %get-tuple-element.14.k_ref, bf16[4096,128]{1,0:T(8,128)(2,1)S(1)} %get-tuple-element.15.v_ref), custom_call_target="tpu_custom_call" | custom-call | flops 1073741824 | bytes 2097152 | tf_op jit(solution)/shard_map/pallas_call | solution.py:35
  87.0 5.3 %collective-permute-done.15.refs_6_.a1 = bf16[2,512,256]{2,1,0:T(8,128)(2,1)} collective-permute-done((bf16[2,512,256]{2,1,0:T(8,128)(2,1)}, bf16[2,512,256]{2,1,0:T(8,128)(2,1)}, u32[]{:S(2)}, u32[]{:S(2)}) %collective-permute-start.15) | collective-permute-done | bytes 524320 | tf_op jit(solution)/shard_map/ppermute | solution.py:346
  92.4 2.1 %shard_map.151 = bf16[1,512,256]{2,1,0:T(8,128)(2,1)S(1)} custom-call(s32[8]{0:T(128)S(1)} %stack.94.info.refs_0_, s32[1]{0:T(128)} %bitcast.15.refs_1_, bf16[512,512]{1,0:T(8,128)(2,1)S(1)} %get-tuple-element.21.refs_2_.g0, bf16[512,512]{1,0:T(8,128)(2,1)S(1)} %collective-permute-done.13.refs_3_.g1, bf16[512,8192]{1,0:T(8,128)(2,1)} %w0.1, ...), custom_call_target="tpu_custom_call" | custom-call | flops 268435456 | bytes 1572864 | tf_op jit(solution)/shard_map/pallas_call | solution.py:35
  94.5 2.5 %collective-permute-start.18 = (bf16[1,512,256]{2,1,0:T(8,128)(2,1)S(1)}, bf16[1,512,256]{2,1,0:T(8,128)(2,1)S(1)}, u32[]{:S(2)}, u32[]{:S(2)}) collective-permute-start(bf16[1,512,256]{2,1,0:T(8,128)(2,1)S(1)} %shard_map.151), channel_id=1, source_target_pairs={{0,2},{1,3},{2,0},{3,1},{4,6},{5,7},{6,4},{7,5},{8,10},{9,11},{10,... | collective-permute-start | bytes 786440 | tf_op jit(solution)/shard_map/ppermute | solution.py:451
  97.0 2.0 %shard_map.155 = bf16[1,512,256]{2,1,0:T(8,128)(2,1)S(1)} custom-call(s32[8]{0:T(128)S(1)} %stack.94.info.refs_0_, s32[1]{0:T(128)} %bitcast.22.refs_1_, bf16[512,512]{1,0:T(8,128)(2,1)S(1)} %get-tuple-element.21.refs_2_.g0, bf16[512,512]{1,0:T(8,128)(2,1)S(1)} %collective-permute-done.13.refs_3_.g1, bf16[512,8192]{1,0:T(8,128)(2,1)} %w0.1, ...), custom_call_target="tpu_custom_call" | custom-call | flops 268435456 | bytes 1572864 | tf_op jit(solution)/shard_map/pallas_call | solution.py:35
  99.0 0.7 collective-permute-start.22
  99.7 2.0 %shard_map.154 = bf16[1,512,256]{2,1,0:T(8,128)(2,1)S(1)} custom-call(s32[8]{0:T(128)S(1)} %stack.94.info.refs_0_, s32[1]{0:T(128)} %bitcast.21.refs_1_, bf16[512,512]{1,0:T(8,128)(2,1)S(1)} %get-tuple-element.21.refs_2_.g0, bf16[512,512]{1,0:T(8,128)(2,1)S(1)} %collective-permute-done.13.refs_3_.g1, bf16[512,8192]{1,0:T(8,128)(2,1)} %w0.1, ...), custom_call_target="tpu_custom_call" | custom-call | flops 268435456 | bytes 1572864 | tf_op jit(solution)/shard_map/pallas_call | solution.py:35
  101.7 3.3 %collective-permute-start.21 = (bf16[1,512,256]{2,1,0:T(8,128)(2,1)S(1)}, bf16[1,512,256]{2,1,0:T(8,128)(2,1)S(1)}, u32[]{:S(2)}, u32[]{:S(2)}) collective-permute-start(bf16[1,512,256]{2,1,0:T(8,128)(2,1)S(1)} %shard_map.154), channel_id=1, source_target_pairs={{0,8},{1,9},{2,10},{3,11},{4,12},{5,13},{6,14},{7,15},{8,0},{9,1},... | collective-permute-start | bytes 786440 | tf_op jit(solution)/shard_map/ppermute | solution.py:346
  105.0 2.0 %shard_map.153 = bf16[1,512,256]{2,1,0:T(8,128)(2,1)S(1)} custom-call(s32[8]{0:T(128)S(1)} %stack.94.info.refs_0_, s32[1]{0:T(128)} %bitcast.16.refs_1_, bf16[512,512]{1,0:T(8,128)(2,1)S(1)} %get-tuple-element.21.refs_2_.g0, bf16[512,512]{1,0:T(8,128)(2,1)S(1)} %collective-permute-done.13.refs_3_.g1, bf16[512,8192]{1,0:T(8,128)(2,1)} %w0.1, ...), custom_call_target="tpu_custom_call" | custom-call | flops 268435456 | bytes 1572864 | tf_op jit(solution)/shard_map/pallas_call | solution.py:35
  107.0 2.1 %collective-permute-start.20 = (bf16[1,512,256]{2,1,0:T(8,128)(2,1)S(1)}, bf16[1,512,256]{2,1,0:T(8,128)(2,1)S(1)}, u32[]{:S(2)}, u32[]{:S(2)}) collective-permute-start(bf16[1,512,256]{2,1,0:T(8,128)(2,1)S(1)} %shard_map.153), channel_id=1, source_target_pairs={{0,4},{1,5},{2,6},{3,7},{4,8},{5,9},{6,10},{7,11},{8,12},{9,13},{1... | collective-permute-start | bytes 786440 | tf_op jit(solution)/shard_map/ppermute | solution.py:346
  109.1 9.0 %shard_map.142.rest_0_ = bf16[512,512]{1,0:T(8,128)(2,1)} custom-call(s32[8]{0:T(128)S(1)} %stack.94.info.refs_0_, bf16[512,512]{1,0:T(8,128)(2,1)S(1)} %copy-done.18, bf16[4096,128]{1,0:T(8,128)(2,1)S(1)} %get-tuple-element.14.k_ref, bf16[4096,128]{1,0:T(8,128)(2,1)S(1)} %get-tuple-element.15.v_ref, ...), custom_call_target="tpu_custom_call", output_to_operand_aliasing={{}: (4, {})} | custom-call | flops 1073741824 | bytes 2097152 | tf_op jit(solution)/shard_map/pallas_call | solution.py:35
  118.1 9.0 %shard_map.143.rest_0_ = bf16[512,512]{1,0:T(8,128)(2,1)} custom-call(s32[8]{0:T(128)S(1)} %stack.94.info.refs_0_, bf16[512,512]{1,0:T(8,128)(2,1)S(1)} %copy-done.18, bf16[4096,128]{1,0:T(8,128)(2,1)S(1)} %get-tuple-element.14.k_ref, bf16[4096,128]{1,0:T(8,128)(2,1)S(1)} %get-tuple-element.15.v_ref, ...), custom_call_target="tpu_custom_call", output_to_operand_aliasing={{}: (4, {})} | custom-call | flops 1073741824 | bytes 2097152 | tf_op jit(solution)/shard_map/pallas_call | solution.py:35
  127.1 9.0 %shard_map.144 = bf16[512,512]{1,0:T(8,128)(2,1)} custom-call(s32[8]{0:T(128)S(1)} %stack.94.info.refs_0_, bf16[512,512]{1,0:T(8,128)(2,1)S(1)} %copy-done.18, bf16[4096,128]{1,0:T(8,128)(2,1)S(1)} %get-tuple-element.14.k_ref, bf16[4096,128]{1,0:T(8,128)(2,1)S(1)} %get-tuple-element.15.v_ref, ...), custom_call_target="tpu_custom_call", output_to_operand_aliasing={{}: (4, {})} | custom-call | flops 1073741824 | bytes 2097152 | tf_op jit(solution)/shard_map/pallas_call | solution.py:35
  136.1 3.7 %shard_map.156 = bf16[512,512]{1,0:T(8,128)(2,1)} custom-call(s32[8]{0:T(128)S(1)} %stack.94.info.refs_0_, s32[2]{0:T(128)S(1)} %pad_add_fusion.columns, bf16[512,512]{1,0:T(8,128)(2,1)S(1)} %get-tuple-element.21.refs_2_.g0, bf16[512,512]{1,0:T(8,128)(2,1)S(1)} %collective-permute-done.13.refs_3_.g1, bf16[512,8192]{1,0:T(8,128)(2,1)} %w0.1, ...), custom_call_target="tpu_custom_call" | custom-call | flops 536870912 | bytes 4194304 | tf_op jit(solution)/shard_map/pallas_call | solution.py:35
  (46 shorter events, 0.1 us)
Async XLA Ops:
  0.6 37.0 %collective-permute-start.14 = (bf16[512,8192]{1,0:T(8,128)(2,1)}, bf16[512,8192]{1,0:T(8,128)(2,1)}, u32[]{:S(2)}, u32[]{:S(2)}) collective-permute-start(bf16[512,8192]{1,0:T(8,128)(2,1)} %w0.1), channel_id=1, source_target_pairs={{0,1},{1,0},{2,3},{3,2},{4,5},{5,4},{6,7},{7,6},{8,9},{9,8},{10,11... | collective-permute-start | bytes 25165832 | tf_op jit(solution)/shard_map/ppermute | solution.py:343
  1.5 1.2 copy-start
  2.7 1.2 copy-start.2
  4.0 1.2 copy-start.6
  5.2 1.2 copy-start.7
  6.4 0.7 copy-start.15
  7.1 0.7 copy-start.16
  7.8 21.4 %copy-start.5 = (bf16[512,512]{1,0:T(8,128)(2,1)S(1)}, bf16[512,512]{1,0:T(8,128)(2,1)}, u32[]{:S(2)}) copy-start(bf16[512,512]{1,0:T(8,128)(2,1)} %c_ref.3) | copy-start | bytes 1572868
  7.8 21.4 %copy-start.8 = (bf16[512,512]{1,0:T(8,128)(2,1)S(1)}, bf16[512,512]{1,0:T(8,128)(2,1)}, u32[]{:S(2)}) copy-start(bf16[512,512]{1,0:T(8,128)(2,1)} %g_ref.1) | copy-start | bytes 1572868
  9.9 8.1 %collective-permute-start.10 = (bf16[544,128]{1,0:T(8,128)(2,1)S(1)}, bf16[544,128]{1,0:T(8,128)(2,1)S(1)}, u32[]{:S(2)}, u32[]{:S(2)}) collective-permute-start(bf16[544,128]{1,0:T(8,128)(2,1)S(1)} %get-tuple-element.17.m0), channel_id=1, source_target_pairs={{0,32},{16,48},{32,0},{48,16},{64,96},{80,112},{96,64},{112,80},{1... | collective-permute-start | bytes 417800 | tf_op jit(solution)/shard_map/ppermute | solution.py:345
  11.2 9.4 %collective-permute-start.11 = (bf16[544,128]{1,0:T(8,128)(2,1)S(1)}, bf16[544,128]{1,0:T(8,128)(2,1)S(1)}, u32[]{:S(2)}, u32[]{:S(2)}) collective-permute-start(bf16[544,128]{1,0:T(8,128)(2,1)S(1)} %get-tuple-element.17.m0), channel_id=1, source_target_pairs={{0,48},{16,0},{32,16},{48,32},{64,112},{80,64},{96,80},{112,96},{1... | collective-permute-start | bytes 417800 | tf_op jit(solution)/shard_map/ppermute | solution.py:345
  11.2 9.4 %collective-permute-start.9 = (bf16[544,128]{1,0:T(8,128)(2,1)S(1)}, bf16[544,128]{1,0:T(8,128)(2,1)S(1)}, u32[]{:S(2)}, u32[]{:S(2)}) collective-permute-start(bf16[544,128]{1,0:T(8,128)(2,1)S(1)} %get-tuple-element.17.m0), channel_id=1, source_target_pairs={{0,16},{16,32},{32,48},{48,0},{64,80},{80,96},{96,112},{112,64},{1... | collective-permute-start | bytes 417800 | tf_op jit(solution)/shard_map/ppermute | solution.py:345
  21.3 7.9 %collective-permute-start.12 = (bf16[544,128]{1,0:T(8,128)(2,1)S(1)}, bf16[544,128]{1,0:T(8,128)(2,1)S(1)}, u32[]{:S(2)}, u32[]{:S(2)}) collective-permute-start(bf16[544,128]{1,0:T(8,128)(2,1)S(1)} %get-tuple-element.20.own_ref), channel_id=1, source_target_pairs={{0,64},{16,80},{32,96},{48,112},{64,0},{80,16},{96,32},{112,48},{1... | collective-permute-start | bytes 417800 | tf_op jit(solution)/shard_map/ppermute | solution.py:344
  22.3 1.2 copy-start.1
  23.5 1.2 copy-start.3
  24.7 1.0 copy-start.4
  25.7 0.7 copy-start.17
  31.0 6.6 %collective-permute-start.13 = (bf16[512,512]{1,0:T(8,128)(2,1)S(1)}, bf16[512,512]{1,0:T(8,128)(2,1)S(1)}, u32[]{:S(2)}, u32[]{:S(2)}) collective-permute-start(bf16[512,512]{1,0:T(8,128)(2,1)S(1)} %get-tuple-element.21.refs_2_.g0), channel_id=1, source_target_pairs={{0,1},{1,0},{2,3},{3,2},{4,5},{5,4},{6,7},{7,6},{8,9},{9,8},{10,11... | collective-permute-start | bytes 1572872 | tf_op jit(solution)/shard_map/ppermute | solution.py:343
  31.0 5.9 %collective-permute-start = (bf16[512,128]{1,0:T(8,128)(2,1)S(1)}, bf16[512,128]{1,0:T(8,128)(2,1)S(1)}, u32[]{:S(2)}, u32[]{:S(2)}) collective-permute-start(bf16[512,128]{1,0:T(8,128)(2,1)S(1)} %get-tuple-element.13.refs_0_), channel_id=1, source_target_pairs={{0,64},{16,80},{32,96},{48,112},{64,0},{80,16},{96,32},{112,48},{1... | collective-permute-start | bytes 393224 | tf_op jit(solution)/shard_map/ppermute | solution.py:344
  36.9 9.1 %collective-permute-start.1 = (bf16[1024,128]{1,0:T(8,128)(2,1)S(1)}, bf16[1024,128]{1,0:T(8,128)(2,1)}, u32[]{:S(2)}, u32[]{:S(2)}) collective-permute-start(bf16[1024,128]{1,0:T(8,128)(2,1)S(1)} %constant_dynamic-update-slice_fusion), channel_id=1, source_target_pairs={{0,16},{16,32},{32,48},{48,0},{64,80},{80,96},{96,112},{112,64},{1... | collective-permute-start | bytes 786440 | tf_op jit(solution)/shard_map/ppermute | solution.py:345
  42.6 54.4 %collective-permute-start.19 = (bf16[4,512,256]{2,1,0:T(8,128)(2,1)}, bf16[4,512,256]{2,1,0:T(8,128)(2,1)S(1)}, u32[]{:S(2)}, u32[]{:S(2)}) collective-permute-start(bf16[4,512,256]{2,1,0:T(8,128)(2,1)} %shard_map.152), channel_id=1, source_target_pairs={{0,2},{1,3},{2,0},{3,1},{4,6},{5,7},{6,4},{7,5},{8,10},{9,11},{10,... | collective-permute-start | bytes 3145736 | tf_op jit(solution)/shard_map/ppermute | solution.py:442
  43.7 2.8 %collective-permute-start.4 = (bf16[512,128]{1,0:T(8,128)(2,1)S(1)}, bf16[512,128]{1,0:T(8,128)(2,1)S(1)}, u32[]{:S(2)}, u32[]{:S(2)}) collective-permute-start(bf16[512,128]{1,0:T(8,128)(2,1)S(1)} %get-tuple-element.13.refs_0_), channel_id=1, source_target_pairs={{0,1},{1,0},{2,3},{3,2},{4,5},{5,4},{6,7},{7,6},{8,9},{9,8},{10,11... | collective-permute-start | bytes 393224 | tf_op jit(solution)/shard_map/ppermute | solution.py:343
  43.7 10.8 %collective-permute-start.2 = (bf16[1024,128]{1,0:T(8,128)(2,1)S(1)}, bf16[1024,128]{1,0:T(8,128)(2,1)}, u32[]{:S(2)}, u32[]{:S(2)}) collective-permute-start(bf16[1024,128]{1,0:T(8,128)(2,1)S(1)} %constant_dynamic-update-slice_fusion), channel_id=1, source_target_pairs={{0,32},{16,48},{32,0},{48,16},{64,96},{80,112},{96,64},{112,80},{1... | collective-permute-start | bytes 786440 | tf_op jit(solution)/shard_map/ppermute | solution.py:345
  46.1 18.8 %collective-permute-start.3 = (bf16[1024,128]{1,0:T(8,128)(2,1)S(1)}, bf16[1024,128]{1,0:T(8,128)(2,1)}, u32[]{:S(2)}, u32[]{:S(2)}) collective-permute-start(bf16[1024,128]{1,0:T(8,128)(2,1)S(1)} %constant_dynamic-update-slice_fusion), channel_id=1, source_target_pairs={{0,48},{16,0},{32,16},{48,32},{64,112},{80,64},{96,80},{112,96},{1... | collective-permute-start | bytes 786440 | tf_op jit(solution)/shard_map/ppermute | solution.py:345
  46.1 22.4 %collective-permute-start.6 = (bf16[1024,128]{1,0:T(8,128)(2,1)}, bf16[1024,128]{1,0:T(8,128)(2,1)S(1)}, u32[]{:S(2)}, u32[]{:S(2)}) collective-permute-start(bf16[1024,128]{1,0:T(8,128)(2,1)} %collective-permute-done.1.refs_2_), channel_id=1, source_target_pairs={{0,1},{1,0},{2,3},{3,2},{4,5},{5,4},{6,7},{7,6},{8,9},{9,8},{10,11... | collective-permute-start | bytes 786440 | tf_op jit(solution)/shard_map/ppermute | solution.py:343
  46.5 17.6 %collective-permute-start.5 = (bf16[512,128]{1,0:T(8,128)(2,1)S(1)}, bf16[512,128]{1,0:T(8,128)(2,1)S(1)}, u32[]{:S(2)}, u32[]{:S(2)}) collective-permute-start(bf16[512,128]{1,0:T(8,128)(2,1)S(1)} %collective-permute-done.refs_1_), channel_id=1, source_target_pairs={{0,1},{1,0},{2,3},{3,2},{4,5},{5,4},{6,7},{7,6},{8,9},{9,8},{10,11... | collective-permute-start | bytes 393224 | tf_op jit(solution)/shard_map/ppermute | solution.py:343
  54.5 14.7 %collective-permute-start.7 = (bf16[1024,128]{1,0:T(8,128)(2,1)}, bf16[1024,128]{1,0:T(8,128)(2,1)S(1)}, u32[]{:S(2)}, u32[]{:S(2)}) collective-permute-start(bf16[1024,128]{1,0:T(8,128)(2,1)} %collective-permute-done.2.refs_3_), channel_id=1, source_target_pairs={{0,1},{1,0},{2,3},{3,2},{4,5},{5,4},{6,7},{7,6},{8,9},{9,8},{10,11... | collective-permute-start | bytes 786440 | tf_op jit(solution)/shard_map/ppermute | solution.py:343
  64.1 0.7 copy-start.13
  64.8 22.3 %collective-permute-start.17 = (bf16[2,512,256]{2,1,0:T(8,128)(2,1)}, bf16[2,512,256]{2,1,0:T(8,128)(2,1)S(1)}, u32[]{:S(2)}, u32[]{:S(2)}) collective-permute-start(bf16[2,512,256]{2,1,0:T(8,128)(2,1)} %shard_map.150), channel_id=1, source_target_pairs={{0,12},{1,13},{2,14},{3,15},{4,0},{5,1},{6,2},{7,3},{8,4},{9,5},{1... | collective-permute-start | bytes 1572872 | tf_op jit(solution)/shard_map/ppermute | solution.py:346
  64.9 22.1 %collective-permute-start.16 = (bf16[2,512,256]{2,1,0:T(8,128)(2,1)}, bf16[2,512,256]{2,1,0:T(8,128)(2,1)S(1)}, u32[]{:S(2)}, u32[]{:S(2)}) collective-permute-start(bf16[2,512,256]{2,1,0:T(8,128)(2,1)} %shard_map.149), channel_id=1, source_target_pairs={{0,8},{1,9},{2,10},{3,11},{4,12},{5,13},{6,14},{7,15},{8,0},{9,1},... | collective-permute-start | bytes 1572872 | tf_op jit(solution)/shard_map/ppermute | solution.py:346
  68.5 0.7 copy-start.9
  69.2 23.2 %collective-permute-start.15 = (bf16[2,512,256]{2,1,0:T(8,128)(2,1)}, bf16[2,512,256]{2,1,0:T(8,128)(2,1)}, u32[]{:S(2)}, u32[]{:S(2)}) collective-permute-start(bf16[2,512,256]{2,1,0:T(8,128)(2,1)} %shard_map.148), channel_id=1, source_target_pairs={{0,4},{1,5},{2,6},{3,7},{4,8},{5,9},{6,10},{7,11},{8,12},{9,13},{1... | collective-permute-start | bytes 1572872 | tf_op jit(solution)/shard_map/ppermute | solution.py:346
  69.2 0.7 copy-start.11
  69.9 1.9 %collective-permute-start.8 = (bf16[1024,128]{1,0:T(8,128)(2,1)}, bf16[1024,128]{1,0:T(8,128)(2,1)}, u32[]{:S(2)}, u32[]{:S(2)}) collective-permute-start(bf16[1024,128]{1,0:T(8,128)(2,1)} %collective-permute-done.3.refs_4_), channel_id=1, source_target_pairs={{0,1},{1,0},{2,3},{3,2},{4,5},{5,4},{6,7},{7,6},{8,9},{9,8},{10,11... | collective-permute-start | bytes 786440 | tf_op jit(solution)/shard_map/ppermute | solution.py:343
  71.8 1.0 copy-start.10
  72.7 0.9 copy-start.12
  73.7 0.9 copy-start.14
  76.8 1.0 copy-start.18
  94.5 41.6 %collective-permute-start.18 = (bf16[1,512,256]{2,1,0:T(8,128)(2,1)S(1)}, bf16[1,512,256]{2,1,0:T(8,128)(2,1)S(1)}, u32[]{:S(2)}, u32[]{:S(2)}) collective-permute-start(bf16[1,512,256]{2,1,0:T(8,128)(2,1)S(1)} %shard_map.151), channel_id=1, source_target_pairs={{0,2},{1,3},{2,0},{3,1},{4,6},{5,7},{6,4},{7,5},{8,10},{9,11},{10,... | collective-permute-start | bytes 786440 | tf_op jit(solution)/shard_map/ppermute | solution.py:451
  99.0 37.1 %collective-permute-start.22 = (bf16[1,512,256]{2,1,0:T(8,128)(2,1)S(1)}, bf16[1,512,256]{2,1,0:T(8,128)(2,1)S(1)}, u32[]{:S(2)}, u32[]{:S(2)}) collective-permute-start(bf16[1,512,256]{2,1,0:T(8,128)(2,1)S(1)} %shard_map.155), channel_id=1, source_target_pairs={{0,12},{1,13},{2,14},{3,15},{4,0},{5,1},{6,2},{7,3},{8,4},{9,5},{1... | collective-permute-start | bytes 786440 | tf_op jit(solution)/shard_map/ppermute | solution.py:346
  101.7 34.4 %collective-permute-start.21 = (bf16[1,512,256]{2,1,0:T(8,128)(2,1)S(1)}, bf16[1,512,256]{2,1,0:T(8,128)(2,1)S(1)}, u32[]{:S(2)}, u32[]{:S(2)}) collective-permute-start(bf16[1,512,256]{2,1,0:T(8,128)(2,1)S(1)} %shard_map.154), channel_id=1, source_target_pairs={{0,8},{1,9},{2,10},{3,11},{4,12},{5,13},{6,14},{7,15},{8,0},{9,1},... | collective-permute-start | bytes 786440 | tf_op jit(solution)/shard_map/ppermute | solution.py:346
  107.0 29.0 %collective-permute-start.20 = (bf16[1,512,256]{2,1,0:T(8,128)(2,1)S(1)}, bf16[1,512,256]{2,1,0:T(8,128)(2,1)S(1)}, u32[]{:S(2)}, u32[]{:S(2)}) collective-permute-start(bf16[1,512,256]{2,1,0:T(8,128)(2,1)S(1)} %shard_map.153), channel_id=1, source_target_pairs={{0,4},{1,5},{2,6},{3,7},{4,8},{5,9},{6,10},{7,11},{8,12},{9,13},{1... | collective-permute-start | bytes 786440 | tf_op jit(solution)/shard_map/ppermute | solution.py:346

commit v2 on v1

v2 whole, which is shorter than its diff:
```python
import math

import jax
import jax.numpy as jnp
from jax import lax
from jax.experimental import pallas as pl
from jax.experimental.pallas import tpu as pltpu
from jax.sharding import PartitionSpec as P

H = 64
KVH = 8
HD = 128
NST = 128
TOK = 512
HEADS = 4
ROWS = HEADS * HD
MSG = ROWS + 32
CB = 256
BF = jnp.bfloat16
F32 = jnp.float32
US = 10**5
NT = (((1,), (1,)), ((), ()))
VMEM_LIMIT = 28 * 1024 * 1024

SEQ, CORE, GROUP, LENGTH, YPOS, XLO, ZPOS, XHI = range(8)


def call(kernel, info, args, in_specs, out_specs, out_shape, grid=(1,), scratch=(), flops=0, nbytes=0, trans=0, extra=(), after=(), limit=VMEM_LIMIT, alias=None):
    scalars = 1 + len(extra)
    first = scalars + len(args)

    def run(*refs):
        kernel(*refs[:first], *refs[first + len(after) :])

    aliases = {} if alias is None else {first + alias: 0}

    spec = pltpu.PrefetchScalarGridSpec(
        num_scalar_prefetch=scalars,
        grid=grid,
        in_specs=[*in_specs, *[ANY] * len(after)],
        out_specs=out_specs,
        scratch_shapes=list(scratch),
    )
    return pl.pallas_call(
        run,
        grid_spec=spec,
        out_shape=out_shape,
        input_output_aliases=aliases,
        compiler_params=pltpu.CompilerParams(vmem_limit_bytes=limit),
        cost_estimate=pl.CostEstimate(flops=flops, bytes_accessed=nbytes, transcendentals=trans),
    )(info, *extra, *args, *after)


def full(shape):
    return pl.BlockSpec(shape, lambda i, *_: (0,) * len(shape))


def hbm(a):
    return pltpu.with_memory_space_constraint(a, pltpu.HBM)


ANY = pl.BlockSpec(memory_space=pl.ANY)
HBM = pl.BlockSpec(memory_space=pltpu.HBM)
VMEM = pl.BlockSpec(memory_space=pltpu.VMEM)
SMEM = pl.BlockSpec(memory_space=pltpu.SMEM)


def shape(dims, kind):
    return jax.ShapeDtypeStruct(dims, kind)


def split2(a):
    high = a.astype(BF)
    return high, (a - high.astype(F32)).astype(BF)


def prep_kernel(
    info, k_hbm, v_hbm, mv_hbm, mk_hbm, step_ref, rate_ref, k_ref, vt_ref, kv_ref, msg_ref, cum_ref, mv_ref, mk_ref, v_ref, sems
):
    columns = pl.ds(pl.multiple_of(info[GROUP] * HD, HD), HD)
    pairs = ((mv_hbm, mv_ref), (mk_hbm, mk_ref), (k_hbm, k_ref), (v_hbm, v_ref))
    copies = [pltpu.make_async_copy(a.at[:, columns], b, sems.at[i]) for i, (a, b) in enumerate(pairs)]
    for copy in copies:
        copy.start()

    row = lax.broadcasted_iota(jnp.int32, (8, TOK), 0)
    lane = lax.broadcasted_iota(jnp.int32, (8, TOK), 1)
    step = jnp.concatenate([step_ref[...], jnp.zeros((8 - HEADS, TOK), F32)], axis=0)
    step = jnp.where(info[SEQ] * TOK + lane < info[LENGTH], step, 0.0)
    rate = jnp.zeros((8, TOK), F32)
    for h in range(HEADS):
        rate = jnp.where(row == h, rate_ref[h], rate)
    cum = -step * rate
    shift = 1
    while shift < TOK:
        cum = cum + jnp.where(lane >= shift, pltpu.roll(cum, shift, 1), 0.0)
        shift *= 2
    cum_ref[0:8, :] = cum
    cum_ref[8:16, :] = step
    last = cum[:, TOK - 1 : TOK]
    tail = jnp.exp(last - cum) * step
    log = jnp.broadcast_to(last, (8, HD))
    high = log.astype(BF).astype(F32)
    mid = (log - high).astype(BF).astype(F32)
    low = log - high - mid
    msg_ref[ROWS:MSG, :] = jnp.concatenate([high, mid, low, jnp.zeros_like(low)], axis=0).astype(BF)
    copies[0].wait()
    copies[1].wait()
    vt = mv_ref[...].astype(F32).T
    mk = mk_ref[...]
    for h in range(HEADS):
        high, low = split2(vt * tail[h : h + 1, :])
        state = jnp.dot(high, mk, preferred_element_type=F32) + jnp.dot(low, mk, preferred_element_type=F32)
        msg_ref[h * HD : (h + 1) * HD, :] = state.astype(BF)
    copies[2].wait()
    copies[3].wait()
    zero = info[CORE] == 0
    for i in range(TOK // HD):
        part = pl.ds(i * HD, HD)
        turned = v_ref[part, :].astype(F32).T
        vt_ref[part, :] = turned.astype(BF)
        kv_ref[part, :] = jnp.where(zero, k_ref[part, :].astype(F32), turned).astype(BF)


def log_of(msg):
    tail = msg[ROWS:MSG, :].astype(F32)
    return tail[0:8] + tail[8:16] + tail[16:24]


def combine_kernel(info, m0, m1, m2, m3, kv, kv_far, prefix_ref, pdec_ref, total_ref, pair_ref):
    pair_ref[0:TOK, :] = kv[...]
    pair_ref[TOK : 2 * TOK, :] = kv_far[...]
    y = info[YPOS]
    msgs = (m0, m1, m2, m3)
    place = [lax.rem(y - d + 4, 4) for d in range(4)]
    logs = [log_of(m) for m in msgs]
    pre, tot = [], []
    for d in range(4):
        in_pre = jnp.zeros_like(logs[0])
        in_tot = jnp.zeros_like(logs[0])
        for e in range(4):
            if e == d:
                continue
            after = place[e] > place[d]
            in_tot = in_tot + jnp.where(after, logs[e], 0.0)
            in_pre = in_pre + jnp.where(jnp.logical_and(after, place[e] < y), logs[e], 0.0)
        tot.append(jnp.exp(in_tot))
        pre.append(jnp.where(place[d] < y, jnp.exp(in_pre), 0.0))
    whole = logs[0] + logs[1] + logs[2] + logs[3]
    before = jnp.zeros_like(whole)
    for e in range(4):
        before = before + jnp.where(place[e] < y, logs[e], 0.0)
    pdec_ref[...] = jnp.exp(before)
    for h in range(HEADS):
        part = slice(h * HD, (h + 1) * HD)
        own = [m[part, :].astype(F32) for m in msgs]
        total = own[0] * tot[0][h : h + 1]
        prefix = own[1] * pre[1][h : h + 1]
        for d in range(1, 4):
            total = total + own[d] * tot[d][h : h + 1]
        for d in range(2, 4):
            prefix = prefix + own[d] * pre[d][h : h + 1]
        prefix_ref[part, :] = prefix
        total_ref[part, :] = total.astype(BF)
    high = whole.astype(BF).astype(F32)
    mid = (whole - high).astype(BF).astype(F32)
    low = whole - high - mid
    total_ref[ROWS:MSG, :] = jnp.concatenate([high, mid, low, jnp.zeros_like(low)], axis=0).astype(BF)


def intra_kernel(info, cum_ref, c_ref, mk_ref, mv_ref, skip_ref, y_ref):
    cum = cum_ref[0:8, :]
    step = cum_ref[8:16, :]
    cols = cum.T
    half = TOK // 2
    for h in range(HEADS):
        part = slice(h * HD, (h + 1) * HD)
        for i in range(2):
            here = slice(i * half, (i + 1) * half)
            wide = (i + 1) * half
            inner = lax.dot_general(c_ref[here, part], mk_ref[0:wide, :], NT, preferred_element_type=F32)
            t = i * half + lax.broadcasted_iota(jnp.int32, (half, wide), 0)
            s = lax.broadcasted_iota(jnp.int32, (half, wide), 1)
            diff = jnp.where(s <= t, cols[here, h : h + 1] - cum[h : h + 1, 0:wide], -jnp.inf)
            mix = (jnp.exp(diff) * inner * step[h : h + 1, 0:wide]).astype(BF)
            y = jnp.dot(mix, mv_ref[0:wide, :], preferred_element_type=F32)
            y_ref[here, part] = y + skip_ref[h] * mv_ref[here, :].astype(F32)


def gate_kernel(info, cum_ref, c_ref, y_ref, g_ref, prefix_ref, pdec_ref, own_ref, got_ref, out0, out1, out2, out3, fin_ref):
    second = info[XLO] == 1
    ecols = jnp.exp(cum_ref[0:8, :]).T
    for h in range(HEADS):
        part = slice(h * HD, (h + 1) * HD)
        far = pdec_ref[h : h + 1, :] * got_ref[part, :].astype(F32)
        state = prefix_ref[part, :] + jnp.where(second, far, 0.0)
        high, low = split2(state)
        c = c_ref[:, part]
        carried = lax.dot_general(
            jnp.concatenate([c, c], axis=1), jnp.concatenate([high, low], axis=1), NT, preferred_element_type=F32
        )
        y = y_ref[:, part] + ecols[:, h : h + 1] * carried
        g = g_ref[:, part].astype(F32)
        (out0, out1, out2, out3)[h][...] = (y * (g / (1.0 + jnp.exp(-g)))).astype(BF)
    own_log = log_of(own_ref)
    got_log = log_of(got_ref)
    later = jnp.exp(jnp.where(second, own_log, got_log))
    for h in range(HEADS):
        rows = pl.ds(pl.multiple_of(h * HD + info[SEQ] * (HD // 8), HD // 8), HD // 8)
        own = own_ref[rows, :].astype(F32)
        got = got_ref[rows, :].astype(F32)
        first = jnp.where(second, got, own)
        last = jnp.where(second, own, got)
        fin_ref[h] = last + later[h : h + 1, :] * first


def place_kernel(info, *refs):
    mine, other, (k_ref, v_ref) = refs[0:5], refs[5:10], refs[10:12]
    zero = info[CORE] == 0
    y, x = info[YPOS], info[XLO]

    def put(a, b, where):
        rows = pl.ds(pl.multiple_of(where * TOK, TOK), TOK)
        a, b = a.astype(F32), b.astype(F32)
        k_ref[rows, :] = jnp.where(zero, a, b).astype(BF)
        v_ref[rows, :] = jnp.where(zero, b, a).astype(BF)

    put(mine[0][...], other[0][...], x * 4 + y)
    put(mine[1][...], other[1][...], (1 - x) * 4 + y)
    for d in range(1, 4):
        ypos = lax.rem(y - d + 4, 4)
        put(mine[d + 1][0:TOK, :], other[d + 1][0:TOK, :], x * 4 + ypos)
        put(mine[d + 1][TOK : 2 * TOK, :], other[d + 1][TOK : 2 * TOK, :], (1 - x) * 4 + ypos)


SCALE = math.log2(math.e) / math.sqrt(HD)
HALF = TOK // 2
UNITS = [(h, i) for h in range(HEADS) for i in range(2)]
ACC = HD + 16


def with_ones(panels):
    vt = jnp.concatenate(panels, axis=1)
    return jnp.concatenate([vt, jnp.ones((16, vt.shape[1]), BF)], axis=0)


def diagonal_kernel(info, q_ref, k_ref, v_ref, best_ref, acc_ref):
    limit = info[LENGTH] - info[SEQ] * TOK
    vt = with_ones([v_ref[i * HD : (i + 1) * HD, :] for i in range(TOK // HD)])
    for u, (h, i) in enumerate(UNITS):
        wide = (i + 1) * HALF
        q = q_ref[i * HALF : (i + 1) * HALF, h * HD : (h + 1) * HD]
        scores = lax.dot_general(k_ref[0:wide, :], q, NT, preferred_element_type=F32)
        s = lax.broadcasted_iota(jnp.int32, (wide, HALF), 0)
        t = i * HALF + lax.broadcasted_iota(jnp.int32, (wide, HALF), 1)
        keep = jnp.logical_and(s <= t, s < limit)
        scores = jnp.where(keep, scores, -jnp.inf)
        best = jnp.max(scores, axis=0, keepdims=True)
        weights = jnp.exp2((scores - best) * SCALE).astype(BF)
        best_ref[u] = jnp.broadcast_to(best, (8, HALF))
        acc_ref[u] = jnp.dot(vt[:, 0:wide], weights, preferred_element_type=F32)


def earlier_kernel(heads, info, q_ref, k_ref, v_ref, best_ref, acc_ref, out_ref):
    units = [(h, i) for h in range(heads) for i in range(2)]
    queries = [q_ref[i * HALF : (i + 1) * HALF, h * HD : (h + 1) * HD] for h, i in units]

    def one(j, state):
        base = pl.multiple_of(j * TOK, TOK)
        k = k_ref[pl.ds(base, TOK), :]
        vt = with_ones([v_ref[pl.ds(base + i * HD, HD), :] for i in range(TOK // HD)])
        scores = [lax.dot_general(k, q, NT, preferred_element_type=F32) for q in queries]
        new = []
        for u in range(len(units)):
            best, summed = state[2 * u], state[2 * u + 1]
            top = jnp.maximum(best, jnp.max(scores[u], axis=0, keepdims=True))
            weights = jnp.exp2((scores[u] - top) * SCALE).astype(BF)
            shrink = jnp.exp2((best - top) * SCALE)
            new += [top, summed * shrink + jnp.dot(vt, weights, preferred_element_type=F32)]
        return tuple(new)

    start = []
    for u in range(len(units)):
        start += [best_ref[u, 0:1, :], acc_ref[u]]
    state = lax.fori_loop(0, info[SEQ], one, tuple(start))
    for u, (h, i) in enumerate(units):
        summed = state[2 * u + 1]
        out = summed[0:HD] * (1.0 / summed[HD : HD + 1])
        out_ref[i * HALF : (i + 1) * HALF, h * HD : (h + 1) * HD] = out.T.astype(BF)


def weights_kernel(info, columns, near, far, out_ref, sems):
    def copies(k):
        part = pl.ds(pl.multiple_of(columns[k] * CB, CB), CB)
        return (
            pltpu.make_async_copy(near.at[:, part], out_ref.at[k, 0:TOK, :], sems.at[0, k]),
            pltpu.make_async_copy(far.at[:, part], out_ref.at[k, TOK : 2 * TOK, :], sems.at[1, k]),
        )

    for k in range(16):
        for copy in copies(k):
            copy.start()
    for k in range(16):
        for copy in copies(k):
            copy.wait()


def product(gated, weights, first, n):
    g = jnp.concatenate([r[...] for r in gated], axis=1)
    w = jnp.concatenate([weights[first + k] for k in range(n)], axis=1)
    return jnp.dot(g, w, preferred_element_type=F32)


def first_kernel(info, *refs):
    gated, weights, to_x, to_z = refs[0:8], refs[8], refs[9], refs[10:13]
    for i in range(2):
        acc = product(gated, weights, 2 * i, 2).astype(BF)
        to_x[2 * i] = acc[:, 0:CB]
        to_x[2 * i + 1] = acc[:, CB : 2 * CB]
    for d in range(3):
        acc = product(gated, weights, 4 + 2 * d, 2).astype(BF)
        to_z[d][0] = acc[:, 0:CB]
        to_z[d][1] = acc[:, CB : 2 * CB]


def second_kernel(info, *refs):
    gated, (weights, z1, z2, z3, x, to_x), to_z = refs[0:8], refs[8:14], refs[14:17]
    acc = product(gated, weights, 10, 2)
    total = acc[:, 0:CB]
    for r in (z1, z2, z3):
        total = total + r[1 - info[XHI]].astype(F32)
    to_x[...] = total.astype(BF)
    part = acc[:, CB : 2 * CB]
    to_z[0][...] = (part + x[lax.rem(info[ZPOS] + 1, 4)].astype(F32)).astype(BF)
    acc = product(gated, weights, 12, 2)
    for d in (1, 2):
        part = acc[:, (d - 1) * CB : d * CB]
        to_z[d][...] = (part + x[lax.rem(info[ZPOS] + d + 1, 4)].astype(F32)).astype(BF)


def keep_kernel(info, *refs):
    gated, (weights, z1, z2, z3, x, out_ref) = refs[0:8], refs[8:14]
    acc = product(gated, weights, 14, 2)
    total = acc[:, 0:CB]
    for r in (z1, z2, z3):
        total = total + r[info[XHI]].astype(F32)
    out_ref[:, 0:CB] = total
    out_ref[:, CB : 2 * CB] = acc[:, CB : 2 * CB] + x[info[ZPOS]].astype(F32)


def finish_kernel(info, kept, x, z1, z2, z3, out_ref):
    out_ref[:, 0:CB] = (kept[:, 0:CB] + x[...].astype(F32)).astype(BF)
    total = kept[:, CB : 2 * CB]
    for r in (z1, z2, z3):
        total = total + r[...].astype(F32)
    out_ref[:, CB : 2 * CB] = total.astype(BF)


def head_perm(move):
    pairs = []
    for z in range(4):
        for x in range(2):
            for c in range(2):
                z2, x2, c2 = move(z, x, c)
                pairs.append((z * 4 + x * 2 + c, (z2 % 4) * 4 + (x2 % 2) * 2 + c2 % 2))
    return pairs


CORE_SWAP = head_perm(lambda z, x, c: (z, x, c + 1))
X_SWAP = head_perm(lambda z, x, c: (z, x + 1, c))
Z_MOVE = {d: head_perm(lambda z, x, c, d=d: (z + d, x, c)) for d in (1, 2, 3)}
LO_SWAP = [(i, (i + 4) % 8) for i in range(8)]
Y_MOVE = {d: [(x * 4 + y, x * 4 + (y + d) % 4) for x in range(2) for y in range(4)] for d in (1, 2, 3)}


def body(
    queries,
    keys,
    values,
    length,
    mixer_values,
    mixer_keys,
    mixer_queries,
    gate_values,
    step_size,
    decay_rate,
    skip_gain,
    out_weight,
):
    seq = lax.axis_index("seq")
    head = lax.axis_index("head")
    z, x, c = head // 4, (head // 2) % 2, head % 2
    info = jnp.stack([seq, c, head // 2, length[0], seq % 4, seq // 4, z, x]).astype(jnp.int32)
    core = lambda a: lax.ppermute(a, "head", CORE_SWAP)
    lo = lambda a: lax.ppermute(a, "seq", LO_SWAP)
    along_y = lambda a, d: lax.ppermute(a, "seq", Y_MOVE[d])
    along_z = lambda a, d: lax.ppermute(a, "head", Z_MOVE[d])

    far_weight = core(out_weight)
    keys, values, mixer_values, mixer_keys = hbm(keys), hbm(values), hbm(mixer_values), hbm(mixer_keys)
    queries, mixer_queries, gate_values = hbm(queries), hbm(mixer_queries), hbm(gate_values)

    k_own, vt_own, kv, msg, cum, mv, mk = call(
        prep_kernel,
        info,
        (keys, values, mixer_values, mixer_keys, step_size, decay_rate),
        [HBM, HBM, HBM, HBM, full((HEADS, TOK)), SMEM],
        [full((TOK, HD))] * 3 + [full((MSG, HD)), full((16, TOK))] + [full((TOK, HD))] * 2,
        [shape((TOK, HD), BF)] * 3 + [shape((MSG, HD), BF), shape((16, TOK), F32)] + [shape((TOK, HD), BF)] * 2,
        scratch=[pltpu.VMEM((TOK, HD), BF), pltpu.SemaphoreType.DMA((4,))],
        flops=US,
    )
    msgs = [msg] + [along_y(msg, d) for d in (1, 2, 3)]
    kv_far = lo(kv)

    y_in = call(
        intra_kernel,
        info,
        (cum, mixer_queries, mk, mv, skip_gain),
        [full((16, TOK)), full((TOK, ROWS)), full((TOK, HD)), full((TOK, HD)), SMEM],
        full((TOK, ROWS)),
        shape((TOK, ROWS), F32),
        flops=US,
    )
    best, acc = call(
        diagonal_kernel,
        info,
        (queries, k_own, vt_own),
        [full((TOK, ROWS)), full((TOK, HD)), full((TOK, HD))],
        [full((8, 8, HALF)), full((8, ACC, HALF))],
        [shape((8, 8, HALF), F32), shape((8, ACC, HALF), F32)],
        flops=US,
    )
    block = lambda zz, xx, half: ((zz % 4) * 4 + (xx % 2) * 2 + c) * 2 + half
    columns = jnp.stack(
        [block(i, x + 1, 1) for i in range(4)]
        + [block(z + d, i, 0) for d in (1, 2, 3) for i in range(2)]
        + [block(z, x + 1, 0)]
        + [block(z + d, x, 1) for d in (1, 2, 3)]
        + [block(z, x, 0), block(z, x, 1)]
    ).astype(jnp.int32)
    weights = call(
        weights_kernel,
        info,
        (hbm(out_weight), hbm(far_weight)),
        [HBM, HBM],
        VMEM,
        pltpu.VMEM((16, 2 * TOK, CB), BF),
        scratch=[pltpu.SemaphoreType.DMA((2, 16))],
        flops=US,
        extra=(columns,),
        after=(acc, y_in),
    )
    prefix, pdec, total, kv_pair = call(
        combine_kernel,
        info,
        (*msgs, kv, kv_far),
        [full((MSG, HD))] * 4 + [full((TOK, HD))] * 2,
        [full((ROWS, HD)), full((8, HD)), full((MSG, HD)), full((2 * TOK, HD))],
        [shape((ROWS, HD), F32), shape((8, HD), F32), shape((MSG, HD), BF), shape((2 * TOK, HD), BF)],
        flops=US,
        after=(y_in, acc, weights),
    )
    total_far = lo(total)
    from_y = [along_y(kv_pair, d) for d in (1, 2, 3)]
    *gated, final_states = call(
        gate_kernel,
        info,
        (cum, mixer_queries, y_in, gate_values, prefix, pdec, total, total_far),
        [
            full((16, TOK)),
            full((TOK, ROWS)),
            full((TOK, ROWS)),
            full((TOK, ROWS)),
            full((ROWS, HD)),
            full((8, HD)),
            full((MSG, HD)),
            full((MSG, HD)),
        ],
        [full((TOK, HD))] * 4 + [full((HEADS, HD // 8, NST))],
        [shape((TOK, HD), BF)] * 4 + [shape((HEADS, HD // 8, NST), F32)],
        flops=US,
    )
    gated += [core(a) for a in gated]

    to_x, *to_z = call(
        first_kernel,
        info,
        (*gated, weights),
        [VMEM] * 9,
        [VMEM] * 4,
        [shape((4, TOK, CB), BF)] + [shape((2, TOK, CB), BF)] * 3,
        flops=US,
        after=from_y,
    )
    from_x = lax.ppermute(to_x, "head", X_SWAP)
    from_z = [along_z(to_z[d - 1], d) for d in (1, 2, 3)]

    mine = [kv, kv_far] + from_y
    other = [core(a) for a in mine]
    pieces = [full((TOK, HD))] * 2 + [full((2 * TOK, HD))] * 3
    k_all, v_all = call(
        place_kernel,
        info,
        (*mine, *other),
        pieces * 2,
        [full((8 * TOK, HD))] * 2,
        [shape((8 * TOK, HD), BF)] * 2,
        flops=US,
        after=(to_z[0],),
    )

    def earlier(heads, first, after, prior=None):
        part = lambda *dims: pl.BlockSpec((2 * heads, *dims), lambda i, info: (first // heads, 0, 0))
        column = pl.BlockSpec((TOK, heads * HD), lambda i, info: (0, first // heads))
        return call(
            lambda *refs: earlier_kernel(heads, *refs),
            info,
            (queries, k_all, v_all, best, acc),
            [column, full((8 * TOK, HD)), full((8 * TOK, HD)), part(8, HALF), part(ACC, HALF)],
            column,
            shape((TOK, ROWS), BF),
            flops=US,
            after=after if prior is None else (prior, *after),
            alias=None if prior is None else 0,
        )

    attended = earlier(2, 0, (to_z[0],))

    to_x2, *to_z2 = call(
        second_kernel,
        info,
        (*gated, weights, *from_z, from_x),
        [VMEM] * 13,
        [VMEM] * 4,
        [shape((TOK, CB), BF)] * 4,
        flops=US,
        after=(attended,),
    )
    from_x2 = lax.ppermute(to_x2, "head", X_SWAP)
    from_z2 = [along_z(to_z2[d - 1], d) for d in (1, 2, 3)]
    kept = call(
        keep_kernel,
        info,
        (*gated, weights, *from_z, from_x),
        [VMEM] * 13,
        VMEM,
        shape((TOK, ROWS), F32),
        flops=US,
        after=(to_x2,),
    )
    attended = earlier(2, 2, (to_x2,), attended)
    summed = call(
        finish_kernel,
        info,
        (kept, from_x2, *from_z2),
        [full((TOK, ROWS))] + [full((TOK, CB))] * 4,
        full((TOK, ROWS)),
        shape((TOK, ROWS), BF),
        flops=US,
        after=(attended,),
    )
    return (attended, summed, final_states)


def solution(mesh):
    placed = (
        P("seq", "head"),
        P("seq", None),
        P("seq", None),
        P(),
        P("seq", None),
        P("seq", None),
        P("seq", "head"),
        P("seq", "head"),
        P("head", "seq"),
        P("head"),
        P("head"),
        P("head", None),
    )
    return jax.shard_map(
        body,
        mesh=mesh,
        in_specs=placed,
        out_specs=(P("seq", "head"), P("seq", "head"), P("head", "seq", None)),
        check_vma=False,
    )
```

time: 141 us -> 100 us (0.71)
  the two profiles are of different devices: /device:TPU:94 before, /device:TPU:0 now
where the time goes in v2:
time: 100 us; the launch traced here: 99.6 us
  waiting for transfers between devices  34 us (34%)
  Pallas kernels  32 us (32%)
  starting transfers between devices  28.7 us (29%)
  local copies, waits for them, and re-layouts  3.23 us (3%)
  between operations  1.62 us (2%)
    pallas_call x13, Pallas kernels, call(): pl.pallas_call(run, grid_spec=spec, out_shape=out_shape, input_output_ali...  32 us
    ppermute x6, waiting for transfers between devices, body(): along_z = lambda a, d: lax.ppermute(a, 'head', Z_MOVE[d])  23.8 us
    ppermute x6, starting transfers between devices, body(): along_z = lambda a, d: lax.ppermute(a, 'head', Z_MOVE[d])  11.4 us
    ppermute x6, starting transfers between devices, body(): along_y = lambda a, d: lax.ppermute(a, 'seq', Y_MOVE[d])  9.49 us
    ppermute x6, waiting for transfers between devices, body(): along_y = lambda a, d: lax.ppermute(a, 'seq', Y_MOVE[d])  4.52 us
    ppermute x10, waiting for transfers between devices, body(): core = lambda a: lax.ppermute(a, 'head', CORE_SWAP)  3.16 us
    unnamed x10, local copies, waits for them, and re-layouts  3.05 us
    ppermute x1, starting transfers between devices, body(): from_x = lax.ppermute(to_x, 'head', X_SWAP)  2.8 us
  transfers between devices with their start and end apart: 26, of which 10 were waited for; matrix products, arithmetic and copies ran while one was open for 0% of the time, Pallas kernels for 25%

profile of v2, /device:TPU:0, one launch (start us, length us, event | category | flops | bytes accessed | tf_op | source)
XLA Modules:
  0.0 99.6 jit_solution(13716602059748539701)
XLA Ops:
  0.6 0.1 collective-permute-start.4
  1.4 0.1 stack.82.refs_0_
  1.5 0.7 copy-done.2
  2.2 0.7 copy-done.3
  2.9 3.1 %shard_map.139 = (bf16[512,128]{1,0:T(8,128)(2,1)S(1)}, bf16[512,128]{1,0:T(8,128)(2,1)S(1)}, bf16[512,128]{1,0:T(8,128)(2,1)S(1)}, bf16[544,128]{1,0:T(8,128)(2...) custom-call(s32[8]{0:T(128)S(1)} %stack.82.refs_0_, ...), custom_call_target="tpu_custom_call" | custom-call | flops 100000 | tf_op jit(solution)/shard_map/pallas_call | solution.py:44
  6.0 1.7 %collective-permute-start.1 = (bf16[544,128]{1,0:T(8,128)(2,1)S(1)}, bf16[544,128]{1,0:T(8,128)(2,1)S(1)}, u32[]{:S(2)}, u32[]{:S(2)}) collective-permute-start(bf16[544,128]{1,0:T(8,128)(2,1)S(1)} %get-tuple-element.32.refs_1_), channel_id=1, source_target_pairs={{0,16},{16,32},{32,48},{48,0},{64,80},{80,96},{96,112},{112,64},{1... | collective-permute-start | bytes 417800 | tf_op jit(solution)/shard_map/ppermute | solution.py:396
  7.7 2.9 %collective-permute-start.2 = (bf16[544,128]{1,0:T(8,128)(2,1)S(1)}, bf16[544,128]{1,0:T(8,128)(2,1)S(1)}, u32[]{:S(2)}, u32[]{:S(2)}) collective-permute-start(bf16[544,128]{1,0:T(8,128)(2,1)S(1)} %get-tuple-element.32.refs_1_), channel_id=1, source_target_pairs={{0,32},{16,48},{32,0},{48,16},{64,96},{80,112},{96,64},{112,80},{1... | collective-permute-start | bytes 417800 | tf_op jit(solution)/shard_map/ppermute | solution.py:396
  10.6 1.3 %collective-permute-start.3 = (bf16[544,128]{1,0:T(8,128)(2,1)S(1)}, bf16[544,128]{1,0:T(8,128)(2,1)S(1)}, u32[]{:S(2)}, u32[]{:S(2)}) collective-permute-start(bf16[544,128]{1,0:T(8,128)(2,1)S(1)} %get-tuple-element.32.refs_1_), channel_id=1, source_target_pairs={{0,48},{16,0},{32,16},{48,32},{64,112},{80,64},{96,80},{112,96},{1... | collective-permute-start | bytes 417800 | tf_op jit(solution)/shard_map/ppermute | solution.py:396
  11.9 1.5 %collective-permute-start = (bf16[512,128]{1,0:T(8,128)(2,1)S(1)}, bf16[512,128]{1,0:T(8,128)(2,1)S(1)}, u32[]{:S(2)}, u32[]{:S(2)}) collective-permute-start(bf16[512,128]{1,0:T(8,128)(2,1)S(1)} %get-tuple-element.31.refs_5_.refs_1_), channel_id=1, source_target_pairs={{0,64},{16,80},{32,96},{48,112},{64,0},{80,16},{96,32},{112,48},{1... | collective-permute-start | bytes 393224 | tf_op jit(solution)/shard_map/ppermute | solution.py:395
  13.4 3.7 %shard_map.141 = (f32[8,8,256]{2,1,0:T(8,128)S(1)}, f32[8,144,256]{2,1,0:T(8,128)S(1)}) custom-call(s32[8]{0:T(128)S(1)} %stack.82.refs_0_, bf16[512,512]{1,0:T(8,128)(2,1)} %refs_1_.7, bf16[512,128]{1,0:T(8,128)(2,1)S(1)} %get-tuple-element.36.refs_2_, bf16[512,128]{1,0:T(8,128)(2,1)S(1)} %get-tuple-element.37.refs_3_), custom_call_target="tpu_custom_call" | custom-call | flops 100000 | tf_op jit(solution)/shard_map/pallas_call | solution.py:44
  17.2 0.0 copy-start.4
  17.2 0.6 copy-done.4
  17.8 3.3 %shard_map.140.refs_5_.refs_7_.refs_3_ = f32[512,512]{1,0:T(8,128)S(1)} custom-call(s32[8]{0:T(128)S(1)} %stack.82.refs_0_, f32[16,512]{1,0:T(8,128)S(1)} %get-tuple-element.33.refs_1_, bf16[512,512]{1,0:T(8,128)(2,1)} %refs_2_.7, bf16[512,128]{1,0:T(8,128)(2,1)S(1)} %get-tuple-element.34.refs_3_, bf16[512,128]{1,0:T(8,128)(2,1)S(1)} %get-tuple-element.35.refs_4_, ...), custom_call_target="tpu_custom_call" | custom-call | flops 100000 | tf_op jit(solution)/shard_map/pallas_call | solution.py:44
  21.3 0.1 stack.99.refs_1_
  21.4 0.0 collective-permute-done.4.refs_3_
  21.4 4.3 %shard_map.142.refs_9_ = bf16[16,1024,256]{2,1,0:T(8,128)(2,1)S(1)} custom-call(s32[8]{0:T(128)S(1)} %stack.82.refs_0_, s32[16]{0:T(128)S(1)} %stack.99.refs_1_, bf16[512,8192]{1,0:T(8,128)(2,1)} %refs_2_.6, bf16[512,8192]{1,0:T(8,128)(2,1)} %collective-permute-done.4.refs_3_, f32[8,144,256]{2,1,0:T(8,128)S(1)} %get-tuple-element.38.refs_4_.refs_8_.refs_5_, ...), custom_call_target="tpu_custom_call" | custom-call | flops 100000 | tf_op jit(solution)/shard_map/pallas_call | solution.py:44
  25.7 0.0 collective-permute-done.refs_6_.refs_2_
  25.7 0.0 collective-permute-done.1.refs_2_
  25.7 0.0 collective-permute-done.2.refs_3_
  25.7 0.8 shard_map.143
  26.5 0.7 collective-permute-start.5
  27.2 0.8 collective-permute-start.6
  28.0 0.5 collective-permute-start.13
  28.6 2.0 %collective-permute-start.7 = (bf16[1024,128]{1,0:T(8,128)(2,1)S(1)}, bf16[1024,128]{1,0:T(8,128)(2,1)S(1)}, u32[]{:S(2)}, u32[]{:S(2)}) collective-permute-start(bf16[1024,128]{1,0:T(8,128)(2,1)S(1)} %get-tuple-element.39), channel_id=1, source_target_pairs={{0,48},{16,0},{32,16},{48,32},{64,112},{80,64},{96,80},{112,96},{1... | collective-permute-start | bytes 786440 | tf_op jit(solution)/shard_map/ppermute | solution.py:396
  30.5 2.5 %collective-permute-done.13.refs_8_ = bf16[544,128]{1,0:T(8,128)(2,1)S(1)} collective-permute-done((bf16[544,128]{1,0:T(8,128)(2,1)S(1)}, bf16[544,128]{1,0:T(8,128)(2,1)S(1)}, u32[]{:S(2)}, u32[]{:S(2)}) %collective-permute-start.13) | collective-permute-done | bytes 139296 | tf_op jit(solution)/shard_map/ppermute | solution.py:395
  33.1 2.9 %shard_map.144 = (bf16[512,128]{1,0:T(8,128)(2,1)S(1)}, bf16[512,128]{1,0:T(8,128)(2,1)S(1)}, bf16[512,128]{1,0:T(8,128)(2,1)S(1)}, bf16[512,128]{1,0:T(8,128)(2,1)S(1)}, f32[4,16,128]{2,1,0:T(8,128)}) custom-call(s32[8]{0:T(128)S(1)} %stack.82.refs_0_, f32[16,512]{1,0:T(8,128)S(1)} %get-tuple-element.33.refs_1_, bf16[512,512]{1,0:T(8,128)(2,1)} %refs_2_.7, ...), custom_call_target="tpu_custom_call" | custom-call | flops 100000 | tf_op jit(solution)/shard_map/pallas_call | solution.py:44
  36.0 0.5 collective-permute-start.15
  36.5 4.4 %collective-permute-done.5.refs_10_.refs_3_ = bf16[1024,128]{1,0:T(8,128)(2,1)S(1)} collective-permute-done((bf16[1024,128]{1,0:T(8,128)(2,1)S(1)}, bf16[1024,128]{1,0:T(8,128)(2,1)S(1)}, u32[]{:S(2)}, u32[]{:S(2)}) %collective-permute-start.5) | collective-permute-done | bytes 262176 | tf_op jit(solution)/shard_map/ppermute | solution.py:396
  40.9 0.5 collective-permute-start.17
  41.5 0.1 collective-permute-done.7.refs_12_.refs_5_
  41.6 0.0 collective-permute-done.15.refs_6_
  41.6 0.7 collective-permute-done.16.refs_7_
  42.3 0.2 collective-permute-done.17.refs_8_
  42.5 3.4 %shard_map.145 = (bf16[4,512,256]{2,1,0:T(8,128)(2,1)S(1)}, bf16[2,512,256]{2,1,0:T(8,128)(2,1)S(1)}, bf16[2,512,256]{2,1,0:T(8,128)(2,1)S(1)}, bf16[2,512,256]{2,1,0:T(8,128)(2,1)S(1)}) custom-call(s32[8]{0:T(128)S(1)} %stack.82.refs_0_, bf16[512,128]{1,0:T(8,128)(2,1)S(1)} %get-tuple-element.43.refs_1_, bf16[512,128]{1,0:T(8,128)(2,1)S(1)} %get-tuple-element.44.refs_2_, ...), custom_call_target="tpu_custom_call" | custom-call | flops 100000 | tf_op jit(solution)/shard_map/pallas_call | solution.py:44
  45.9 2.8 %collective-permute-start.21 = (bf16[4,512,256]{2,1,0:T(8,128)(2,1)S(1)}, bf16[4,512,256]{2,1,0:T(8,128)(2,1)S(1)}, u32[]{:S(2)}, u32[]{:S(2)}) collective-permute-start(bf16[4,512,256]{2,1,0:T(8,128)(2,1)S(1)} %get-tuple-element.53), channel_id=1, source_target_pairs={{0,2},{1,3},{2,0},{3,1},{4,6},{5,7},{6,4},{7,5},{8,10},{9,11},{10,... | collective-permute-start | bytes 3145736 | tf_op jit(solution)/shard_map/ppermute | solution.py:496
  48.7 0.0 collective-permute-start.10
  48.7 0.5 collective-permute-start.8
  49.2 0.0 collective-permute-start.9
  49.3 0.5 collective-permute-start.11
  49.7 0.7 collective-permute-done.8.refs_6_
  50.4 1.9 %collective-permute-start.18 = (bf16[2,512,256]{2,1,0:T(8,128)(2,1)S(1)}, bf16[2,512,256]{2,1,0:T(8,128)(2,1)S(1)}, u32[]{:S(2)}, u32[]{:S(2)}) collective-permute-start(bf16[2,512,256]{2,1,0:T(8,128)(2,1)S(1)} %get-tuple-element.47.refs_11_.refs_6_), channel_id=1, source_target_pairs={{0,4},{1,5},{2,6},{3,7},{4,8},{5,9},{6,10},{7,11},{8,12},{9,13},{1... | collective-permute-start | bytes 1572872 | tf_op jit(solution)/shard_map/ppermute | solution.py:397
  52.3 0.0 collective-permute-done.9.refs_7_
  52.3 3.6 %collective-permute-start.19 = (bf16[2,512,256]{2,1,0:T(8,128)(2,1)S(1)}, bf16[2,512,256]{2,1,0:T(8,128)(2,1)S(1)}, u32[]{:S(2)}, u32[]{:S(2)}) collective-permute-start(bf16[2,512,256]{2,1,0:T(8,128)(2,1)S(1)} %get-tuple-element.51), channel_id=1, source_target_pairs={{0,8},{1,9},{2,10},{3,11},{4,12},{5,13},{6,14},{7,15},{8,0},{9,1},... | collective-permute-start | bytes 1572872 | tf_op jit(solution)/shard_map/ppermute | solution.py:397
  55.9 1.0 %collective-permute-start.20 = (bf16[2,512,256]{2,1,0:T(8,128)(2,1)S(1)}, bf16[2,512,256]{2,1,0:T(8,128)(2,1)S(1)}, u32[]{:S(2)}, u32[]{:S(2)}) collective-permute-start(bf16[2,512,256]{2,1,0:T(8,128)(2,1)S(1)} %get-tuple-element.52), channel_id=1, source_target_pairs={{0,12},{1,13},{2,14},{3,15},{4,0},{5,1},{6,2},{7,3},{8,4},{9,5},{1... | collective-permute-start | bytes 1572872 | tf_op jit(solution)/shard_map/ppermute | solution.py:397
  56.9 0.0 collective-permute-done.11.refs_9_
  56.9 0.0 collective-permute-start.12
  56.9 1.5 %collective-permute-done.12.refs_10_ = bf16[1024,128]{1,0:T(8,128)(2,1)S(1)} collective-permute-done((bf16[1024,128]{1,0:T(8,128)(2,1)S(1)}, bf16[1024,128]{1,0:T(8,128)(2,1)S(1)}, u32[]{:S(2)}, u32[]{:S(2)}) %collective-permute-start.12) | collective-permute-done | bytes 262176 | tf_op jit(solution)/shard_map/ppermute | solution.py:394
  58.5 1.0 %shard_map.146 = (bf16[4096,128]{1,0:T(8,128)(2,1)S(1)}, bf16[4096,128]{1,0:T(8,128)(2,1)S(1)}) custom-call(s32[8]{0:T(128)S(1)} %stack.82.refs_0_, bf16[512,128]{1,0:T(8,128)(2,1)S(1)} %get-tuple-element.31.refs_5_.refs_1_, bf16[512,128]{1,0:T(8,128)(2,1)S(1)} %collective-permute-done.refs_6_.refs_2_, ...), custom_call_target="tpu_custom_call" | custom-call | flops 100000 | tf_op jit(solution)/shard_map/pallas_call | solution.py:44
  59.5 2.5 %shard_map.147.refs_14_.refs_6_ = bf16[512,512]{1,0:T(8,128)(2,1)} custom-call(s32[8]{0:T(128)S(1)} %stack.82.refs_0_, bf16[512,512]{1,0:T(8,128)(2,1)} %refs_1_.7, bf16[4096,128]{1,0:T(8,128)(2,1)S(1)} %get-tuple-element.48.refs_2_, bf16[4096,128]{1,0:T(8,128)(2,1)S(1)} %get-tuple-element.49.refs_3_, f32[8,8,256]{2,1,0:T(8,128)S(1)} %get-tuple-element.50.refs_4_, ...), custom_call_target="tpu_custom_call" | custom-call | flops 100000 | tf_op jit(solution)/shard_map/pallas_call | solution.py:44
  62.0 4.7 %collective-permute-done.18.refs_10_ = bf16[2,512,256]{2,1,0:T(8,128)(2,1)S(1)} collective-permute-done((bf16[2,512,256]{2,1,0:T(8,128)(2,1)S(1)}, bf16[2,512,256]{2,1,0:T(8,128)(2,1)S(1)}, u32[]{:S(2)}, u32[]{:S(2)}) %collective-permute-start.18) | collective-permute-done | bytes 524320 | tf_op jit(solution)/shard_map/ppermute | solution.py:397
  66.7 12.4 %collective-permute-done.19.refs_11_ = bf16[2,512,256]{2,1,0:T(8,128)(2,1)S(1)} collective-permute-done((bf16[2,512,256]{2,1,0:T(8,128)(2,1)S(1)}, bf16[2,512,256]{2,1,0:T(8,128)(2,1)S(1)}, u32[]{:S(2)}, u32[]{:S(2)}) %collective-permute-start.19) | collective-permute-done | bytes 524320 | tf_op jit(solution)/shard_map/ppermute | solution.py:397
  79.1 0.0 collective-permute-done.20.refs_12_
  79.1 0.0 collective-permute-done.21.refs_13_
  79.1 1.0 %copy-done = bf16[512,512]{1,0:T(8,128)(2,1)S(1)} copy-done((bf16[512,512]{1,0:T(8,128)(2,1)S(1)}, bf16[512,512]{1,0:T(8,128)(2,1)}, u32[]{:S(2)}) %copy-start) | copy-done | bytes 524312
  80.2 1.8 %shard_map.148 = (bf16[512,256]{1,0:T(8,128)(2,1)S(1)}, bf16[512,256]{1,0:T(8,128)(2,1)S(1)}, bf16[512,256]{1,0:T(8,128)(2,1)S(1)}, bf16[512,256]{1,0:T(8,128)(2,1)S(1)}) custom-call(s32[8]{0:T(128)S(1)} %stack.82.refs_0_, bf16[512,128]{1,0:T(8,128)(2,1)S(1)} %get-tuple-element.43.refs_1_, bf16[512,128]{1,0:T(8,128)(2,1)S(1)} %get-tuple-element.44.refs_2_, ...), custom_call_target="tpu_custom_call" | custom-call | flops 100000 | tf_op jit(solution)/shard_map/pallas_call | solution.py:44
  82.0 0.9 collective-permute-start.22
  82.9 1.3 %collective-permute-start.23 = (bf16[512,256]{1,0:T(8,128)(2,1)S(1)}, bf16[512,256]{1,0:T(8,128)(2,1)S(1)}, u32[]{:S(2)}, u32[]{:S(2)}) collective-permute-start(bf16[512,256]{1,0:T(8,128)(2,1)S(1)} %get-tuple-element.55), channel_id=1, source_target_pairs={{0,4},{1,5},{2,6},{3,7},{4,8},{5,9},{6,10},{7,11},{8,12},{9,13},{1... | collective-permute-start | bytes 786440 | tf_op jit(solution)/shard_map/ppermute | solution.py:397
  84.2 2.4 %collective-permute-start.24 = (bf16[512,256]{1,0:T(8,128)(2,1)S(1)}, bf16[512,256]{1,0:T(8,128)(2,1)S(1)}, u32[]{:S(2)}, u32[]{:S(2)}) collective-permute-start(bf16[512,256]{1,0:T(8,128)(2,1)S(1)} %get-tuple-element.56), channel_id=1, source_target_pairs={{0,8},{1,9},{2,10},{3,11},{4,12},{5,13},{6,14},{7,15},{8,0},{9,1},... | collective-permute-start | bytes 786440 | tf_op jit(solution)/shard_map/ppermute | solution.py:397
  86.6 1.2 %collective-permute-start.25 = (bf16[512,256]{1,0:T(8,128)(2,1)S(1)}, bf16[512,256]{1,0:T(8,128)(2,1)S(1)}, u32[]{:S(2)}, u32[]{:S(2)}) collective-permute-start(bf16[512,256]{1,0:T(8,128)(2,1)S(1)} %get-tuple-element.57), channel_id=1, source_target_pairs={{0,12},{1,13},{2,14},{3,15},{4,0},{5,1},{6,2},{7,3},{8,4},{9,5},{1... | collective-permute-start | bytes 786440 | tf_op jit(solution)/shard_map/ppermute | solution.py:397
  87.7 2.4 %shard_map.149.refs_6_ = bf16[512,512]{1,0:T(8,128)(2,1)} custom-call(s32[8]{0:T(128)S(1)} %stack.82.refs_0_, bf16[512,512]{1,0:T(8,128)(2,1)} %refs_1_.7, bf16[4096,128]{1,0:T(8,128)(2,1)S(1)} %get-tuple-element.48.refs_2_, bf16[4096,128]{1,0:T(8,128)(2,1)S(1)} %get-tuple-element.49.refs_3_, ...), custom_call_target="tpu_custom_call", output_to_operand_aliasing={{}: (6, {})} | custom-call | flops 100000 | tf_op jit(solution)/shard_map/pallas_call | solution.py:44
  90.2 1.2 %shard_map.150.refs_1_ = f32[512,512]{1,0:T(8,128)S(1)} custom-call(s32[8]{0:T(128)S(1)} %stack.82.refs_0_, bf16[512,128]{1,0:T(8,128)(2,1)S(1)} %get-tuple-element.43.refs_1_, bf16[512,128]{1,0:T(8,128)(2,1)S(1)} %get-tuple-element.44.refs_2_, bf16[512,128]{1,0:T(8,128)(2,1)S(1)} %get-tuple-element.45.refs_3_, ...), custom_call_target="tpu_custom_call" | custom-call | flops 100000 | tf_op jit(solution)/shard_map/pallas_call | solution.py:44
  91.5 0.0 collective-permute-done.23.refs_3_
  91.5 6.7 %collective-permute-done.24.refs_4_ = bf16[512,256]{1,0:T(8,128)(2,1)S(1)} collective-permute-done((bf16[512,256]{1,0:T(8,128)(2,1)S(1)}, bf16[512,256]{1,0:T(8,128)(2,1)S(1)}, u32[]{:S(2)}, u32[]{:S(2)}) %collective-permute-start.24) | collective-permute-done | bytes 262176 | tf_op jit(solution)/shard_map/ppermute | solution.py:397
  98.1 1.5 %shard_map.151 = bf16[512,512]{1,0:T(8,128)(2,1)} custom-call(s32[8]{0:T(128)S(1)} %stack.82.refs_0_, f32[512,512]{1,0:T(8,128)S(1)} %shard_map.150.refs_1_, bf16[512,256]{1,0:T(8,128)(2,1)S(1)} %collective-permute-done.22.refs_2_, bf16[512,256]{1,0:T(8,128)(2,1)S(1)} %collective-permute-done.23.refs_3_, ...), custom_call_target="tpu_custom_call" | custom-call | flops 100000 | tf_op jit(solution)/shard_map/pallas_call | solution.py:44
  (13 shorter events, 0.0 us)
Async XLA Ops:
  0.6 20.7 %collective-permute-start.4 = (bf16[512,8192]{1,0:T(8,128)(2,1)}, bf16[512,8192]{1,0:T(8,128)(2,1)}, u32[]{:S(2)}, u32[]{:S(2)}) collective-permute-start(bf16[512,8192]{1,0:T(8,128)(2,1)} %refs_2_.6), channel_id=1, source_target_pairs={{0,1},{1,0},{2,3},{3,2},{4,5},{5,4},{6,7},{7,6},{8,9},{9,8},{10,11... | collective-permute-start | bytes 25165832 | tf_op jit(solution)/shard_map/ppermute | solution.py:394
  1.5 0.7 copy-start.2
  2.2 0.7 copy-start.3
  6.0 19.7 %collective-permute-start.1 = (bf16[544,128]{1,0:T(8,128)(2,1)S(1)}, bf16[544,128]{1,0:T(8,128)(2,1)S(1)}, u32[]{:S(2)}, u32[]{:S(2)}) collective-permute-start(bf16[544,128]{1,0:T(8,128)(2,1)S(1)} %get-tuple-element.32.refs_1_), channel_id=1, source_target_pairs={{0,16},{16,32},{32,48},{48,0},{64,80},{80,96},{96,112},{112,64},{1... | collective-permute-start | bytes 417800 | tf_op jit(solution)/shard_map/ppermute | solution.py:396
  7.7 18.0 %collective-permute-start.2 = (bf16[544,128]{1,0:T(8,128)(2,1)S(1)}, bf16[544,128]{1,0:T(8,128)(2,1)S(1)}, u32[]{:S(2)}, u32[]{:S(2)}) collective-permute-start(bf16[544,128]{1,0:T(8,128)(2,1)S(1)} %get-tuple-element.32.refs_1_), channel_id=1, source_target_pairs={{0,32},{16,48},{32,0},{48,16},{64,96},{80,112},{96,64},{112,80},{1... | collective-permute-start | bytes 417800 | tf_op jit(solution)/shard_map/ppermute | solution.py:396
  10.6 15.1 %collective-permute-start.3 = (bf16[544,128]{1,0:T(8,128)(2,1)S(1)}, bf16[544,128]{1,0:T(8,128)(2,1)S(1)}, u32[]{:S(2)}, u32[]{:S(2)}) collective-permute-start(bf16[544,128]{1,0:T(8,128)(2,1)S(1)} %get-tuple-element.32.refs_1_), channel_id=1, source_target_pairs={{0,48},{16,0},{32,16},{48,32},{64,112},{80,64},{96,80},{112,96},{1... | collective-permute-start | bytes 417800 | tf_op jit(solution)/shard_map/ppermute | solution.py:396
  11.9 13.8 %collective-permute-start = (bf16[512,128]{1,0:T(8,128)(2,1)S(1)}, bf16[512,128]{1,0:T(8,128)(2,1)S(1)}, u32[]{:S(2)}, u32[]{:S(2)}) collective-permute-start(bf16[512,128]{1,0:T(8,128)(2,1)S(1)} %get-tuple-element.31.refs_5_.refs_1_), channel_id=1, source_target_pairs={{0,64},{16,80},{32,96},{48,112},{64,0},{80,16},{96,32},{112,48},{1... | collective-permute-start | bytes 393224 | tf_op jit(solution)/shard_map/ppermute | solution.py:395
  17.2 0.7 copy-start.4
  26.5 14.4 %collective-permute-start.5 = (bf16[1024,128]{1,0:T(8,128)(2,1)S(1)}, bf16[1024,128]{1,0:T(8,128)(2,1)S(1)}, u32[]{:S(2)}, u32[]{:S(2)}) collective-permute-start(bf16[1024,128]{1,0:T(8,128)(2,1)S(1)} %get-tuple-element.39), channel_id=1, source_target_pairs={{0,16},{16,32},{32,48},{48,0},{64,80},{80,96},{96,112},{112,64},{1... | collective-permute-start | bytes 786440 | tf_op jit(solution)/shard_map/ppermute | solution.py:396
  27.2 13.7 %collective-permute-start.6 = (bf16[1024,128]{1,0:T(8,128)(2,1)S(1)}, bf16[1024,128]{1,0:T(8,128)(2,1)S(1)}, u32[]{:S(2)}, u32[]{:S(2)}) collective-permute-start(bf16[1024,128]{1,0:T(8,128)(2,1)S(1)} %get-tuple-element.39), channel_id=1, source_target_pairs={{0,32},{16,48},{32,0},{48,16},{64,96},{80,112},{96,64},{112,80},{1... | collective-permute-start | bytes 786440 | tf_op jit(solution)/shard_map/ppermute | solution.py:396
  28.0 5.1 %collective-permute-start.13 = (bf16[544,128]{1,0:T(8,128)(2,1)S(1)}, bf16[544,128]{1,0:T(8,128)(2,1)S(1)}, u32[]{:S(2)}, u32[]{:S(2)}) collective-permute-start(bf16[544,128]{1,0:T(8,128)(2,1)S(1)} %get-tuple-element.42.refs_7_), channel_id=1, source_target_pairs={{0,64},{16,80},{32,96},{48,112},{64,0},{80,16},{96,32},{112,48},{1... | collective-permute-start | bytes 417800 | tf_op jit(solution)/shard_map/ppermute | solution.py:395
  28.6 13.0 %collective-permute-start.7 = (bf16[1024,128]{1,0:T(8,128)(2,1)S(1)}, bf16[1024,128]{1,0:T(8,128)(2,1)S(1)}, u32[]{:S(2)}, u32[]{:S(2)}) collective-permute-start(bf16[1024,128]{1,0:T(8,128)(2,1)S(1)} %get-tuple-element.39), channel_id=1, source_target_pairs={{0,48},{16,0},{32,16},{48,32},{64,112},{80,64},{96,80},{112,96},{1... | collective-permute-start | bytes 786440 | tf_op jit(solution)/shard_map/ppermute | solution.py:396
  36.0 5.5 %collective-permute-start.14 = (bf16[512,128]{1,0:T(8,128)(2,1)S(1)}, bf16[512,128]{1,0:T(8,128)(2,1)S(1)}, u32[]{:S(2)}, u32[]{:S(2)}) collective-permute-start(bf16[512,128]{1,0:T(8,128)(2,1)S(1)} %get-tuple-element.43.refs_1_), channel_id=1, source_target_pairs={{0,1},{1,0},{2,3},{3,2},{4,5},{5,4},{6,7},{7,6},{8,9},{9,8},{10,11... | collective-permute-start | bytes 393224 | tf_op jit(solution)/shard_map/ppermute | solution.py:394
  36.0 5.5 %collective-permute-start.15 = (bf16[512,128]{1,0:T(8,128)(2,1)S(1)}, bf16[512,128]{1,0:T(8,128)(2,1)S(1)}, u32[]{:S(2)}, u32[]{:S(2)}) collective-permute-start(bf16[512,128]{1,0:T(8,128)(2,1)S(1)} %get-tuple-element.44.refs_2_), channel_id=1, source_target_pairs={{0,1},{1,0},{2,3},{3,2},{4,5},{5,4},{6,7},{7,6},{8,9},{9,8},{10,11... | collective-permute-start | bytes 393224 | tf_op jit(solution)/shard_map/ppermute | solution.py:394
  40.9 1.3 %collective-permute-start.16 = (bf16[512,128]{1,0:T(8,128)(2,1)S(1)}, bf16[512,128]{1,0:T(8,128)(2,1)S(1)}, u32[]{:S(2)}, u32[]{:S(2)}) collective-permute-start(bf16[512,128]{1,0:T(8,128)(2,1)S(1)} %get-tuple-element.45.refs_3_), channel_id=1, source_target_pairs={{0,1},{1,0},{2,3},{3,2},{4,5},{5,4},{6,7},{7,6},{8,9},{9,8},{10,11... | collective-permute-start | bytes 393224 | tf_op jit(solution)/shard_map/ppermute | solution.py:394
  40.9 1.5 %collective-permute-start.17 = (bf16[512,128]{1,0:T(8,128)(2,1)S(1)}, bf16[512,128]{1,0:T(8,128)(2,1)S(1)}, u32[]{:S(2)}, u32[]{:S(2)}) collective-permute-start(bf16[512,128]{1,0:T(8,128)(2,1)S(1)} %get-tuple-element.46.refs_4_), channel_id=1, source_target_pairs={{0,1},{1,0},{2,3},{3,2},{4,5},{5,4},{6,7},{7,6},{8,9},{9,8},{10,11... | collective-permute-start | bytes 393224 | tf_op jit(solution)/shard_map/ppermute | solution.py:394
  45.9 33.2 %collective-permute-start.21 = (bf16[4,512,256]{2,1,0:T(8,128)(2,1)S(1)}, bf16[4,512,256]{2,1,0:T(8,128)(2,1)S(1)}, u32[]{:S(2)}, u32[]{:S(2)}) collective-permute-start(bf16[4,512,256]{2,1,0:T(8,128)(2,1)S(1)} %get-tuple-element.53), channel_id=1, source_target_pairs={{0,2},{1,3},{2,0},{3,1},{4,6},{5,7},{6,4},{7,5},{8,10},{9,11},{10,... | collective-permute-start | bytes 3145736 | tf_op jit(solution)/shard_map/ppermute | solution.py:496
  48.7 7.2 %collective-permute-start.10 = (bf16[1024,128]{1,0:T(8,128)(2,1)S(1)}, bf16[1024,128]{1,0:T(8,128)(2,1)S(1)}, u32[]{:S(2)}, u32[]{:S(2)}) collective-permute-start(bf16[1024,128]{1,0:T(8,128)(2,1)S(1)} %collective-permute-done.5.refs_10_.refs_3_), channel_id=1, source_target_pairs={{0,1},{1,0},{2,3},{3,2},{4,5},{5,4},{6,7},{7,6},{8,9},{9,8},{10,11... | collective-permute-start | bytes 786440 | tf_op jit(solution)/shard_map/ppermute | solution.py:394
  48.7 1.7 %collective-permute-start.8 = (bf16[512,128]{1,0:T(8,128)(2,1)S(1)}, bf16[512,128]{1,0:T(8,128)(2,1)S(1)}, u32[]{:S(2)}, u32[]{:S(2)}) collective-permute-start(bf16[512,128]{1,0:T(8,128)(2,1)S(1)} %get-tuple-element.31.refs_5_.refs_1_), channel_id=1, source_target_pairs={{0,1},{1,0},{2,3},{3,2},{4,5},{5,4},{6,7},{7,6},{8,9},{9,8},{10,11... | collective-permute-start | bytes 393224 | tf_op jit(solution)/shard_map/ppermute | solution.py:394
  49.2 3.1 %collective-permute-start.9 = (bf16[512,128]{1,0:T(8,128)(2,1)S(1)}, bf16[512,128]{1,0:T(8,128)(2,1)S(1)}, u32[]{:S(2)}, u32[]{:S(2)}) collective-permute-start(bf16[512,128]{1,0:T(8,128)(2,1)S(1)} %collective-permute-done.refs_6_.refs_2_), channel_id=1, source_target_pairs={{0,1},{1,0},{2,3},{3,2},{4,5},{5,4},{6,7},{7,6},{8,9},{9,8},{10,11... | collective-permute-start | bytes 393224 | tf_op jit(solution)/shard_map/ppermute | solution.py:394
  49.3 7.7 %collective-permute-start.11 = (bf16[1024,128]{1,0:T(8,128)(2,1)S(1)}, bf16[1024,128]{1,0:T(8,128)(2,1)S(1)}, u32[]{:S(2)}, u32[]{:S(2)}) collective-permute-start(bf16[1024,128]{1,0:T(8,128)(2,1)S(1)} %collective-permute-done.6.refs_11_.refs_4_), channel_id=1, source_target_pairs={{0,1},{1,0},{2,3},{3,2},{4,5},{5,4},{6,7},{7,6},{8,9},{9,8},{10,11... | collective-permute-start | bytes 786440 | tf_op jit(solution)/shard_map/ppermute | solution.py:394
  50.4 16.3 %collective-permute-start.18 = (bf16[2,512,256]{2,1,0:T(8,128)(2,1)S(1)}, bf16[2,512,256]{2,1,0:T(8,128)(2,1)S(1)}, u32[]{:S(2)}, u32[]{:S(2)}) collective-permute-start(bf16[2,512,256]{2,1,0:T(8,128)(2,1)S(1)} %get-tuple-element.47.refs_11_.refs_6_), channel_id=1, source_target_pairs={{0,4},{1,5},{2,6},{3,7},{4,8},{5,9},{6,10},{7,11},{8,12},{9,13},{1... | collective-permute-start | bytes 1572872 | tf_op jit(solution)/shard_map/ppermute | solution.py:397
  52.3 26.8 %collective-permute-start.19 = (bf16[2,512,256]{2,1,0:T(8,128)(2,1)S(1)}, bf16[2,512,256]{2,1,0:T(8,128)(2,1)S(1)}, u32[]{:S(2)}, u32[]{:S(2)}) collective-permute-start(bf16[2,512,256]{2,1,0:T(8,128)(2,1)S(1)} %get-tuple-element.51), channel_id=1, source_target_pairs={{0,8},{1,9},{2,10},{3,11},{4,12},{5,13},{6,14},{7,15},{8,0},{9,1},... | collective-permute-start | bytes 1572872 | tf_op jit(solution)/shard_map/ppermute | solution.py:397
  55.9 23.2 %collective-permute-start.20 = (bf16[2,512,256]{2,1,0:T(8,128)(2,1)S(1)}, bf16[2,512,256]{2,1,0:T(8,128)(2,1)S(1)}, u32[]{:S(2)}, u32[]{:S(2)}) collective-permute-start(bf16[2,512,256]{2,1,0:T(8,128)(2,1)S(1)} %get-tuple-element.52), channel_id=1, source_target_pairs={{0,12},{1,13},{2,14},{3,15},{4,0},{5,1},{6,2},{7,3},{8,4},{9,5},{1... | collective-permute-start | bytes 1572872 | tf_op jit(solution)/shard_map/ppermute | solution.py:397
  56.9 1.5 %collective-permute-start.12 = (bf16[1024,128]{1,0:T(8,128)(2,1)S(1)}, bf16[1024,128]{1,0:T(8,128)(2,1)S(1)}, u32[]{:S(2)}, u32[]{:S(2)}) collective-permute-start(bf16[1024,128]{1,0:T(8,128)(2,1)S(1)} %collective-permute-done.7.refs_12_.refs_5_), channel_id=1, source_target_pairs={{0,1},{1,0},{2,3},{3,2},{4,5},{5,4},{6,7},{7,6},{8,9},{9,8},{10,11... | collective-permute-start | bytes 786440 | tf_op jit(solution)/shard_map/ppermute | solution.py:394
  79.1 1.0 %copy-start = (bf16[512,512]{1,0:T(8,128)(2,1)S(1)}, bf16[512,512]{1,0:T(8,128)(2,1)}, u32[]{:S(2)}) copy-start(bf16[512,512]{1,0:T(8,128)(2,1)} %shard_map.147.refs_14_.refs_6_) | copy-start | bytes 1572868
  82.0 9.5 %collective-permute-start.22 = (bf16[512,256]{1,0:T(8,128)(2,1)S(1)}, bf16[512,256]{1,0:T(8,128)(2,1)S(1)}, u32[]{:S(2)}, u32[]{:S(2)}) collective-permute-start(bf16[512,256]{1,0:T(8,128)(2,1)S(1)} %get-tuple-element.54.refs_7_.refs_14_), channel_id=1, source_target_pairs={{0,2},{1,3},{2,0},{3,1},{4,6},{5,7},{6,4},{7,5},{8,10},{9,11},{10,... | collective-permute-start | bytes 786440 | tf_op jit(solution)/shard_map/ppermute | solution.py:540
  82.9 8.6 %collective-permute-start.23 = (bf16[512,256]{1,0:T(8,128)(2,1)S(1)}, bf16[512,256]{1,0:T(8,128)(2,1)S(1)}, u32[]{:S(2)}, u32[]{:S(2)}) collective-permute-start(bf16[512,256]{1,0:T(8,128)(2,1)S(1)} %get-tuple-element.55), channel_id=1, source_target_pairs={{0,4},{1,5},{2,6},{3,7},{4,8},{5,9},{6,10},{7,11},{8,12},{9,13},{1... | collective-permute-start | bytes 786440 | tf_op jit(solution)/shard_map/ppermute | solution.py:397
  84.2 13.9 %collective-permute-start.24 = (bf16[512,256]{1,0:T(8,128)(2,1)S(1)}, bf16[512,256]{1,0:T(8,128)(2,1)S(1)}, u32[]{:S(2)}, u32[]{:S(2)}) collective-permute-start(bf16[512,256]{1,0:T(8,128)(2,1)S(1)} %get-tuple-element.56), channel_id=1, source_target_pairs={{0,8},{1,9},{2,10},{3,11},{4,12},{5,13},{6,14},{7,15},{8,0},{9,1},... | collective-permute-start | bytes 786440 | tf_op jit(solution)/shard_map/ppermute | solution.py:397
  86.6 11.5 %collective-permute-start.25 = (bf16[512,256]{1,0:T(8,128)(2,1)S(1)}, bf16[512,256]{1,0:T(8,128)(2,1)S(1)}, u32[]{:S(2)}, u32[]{:S(2)}) collective-permute-start(bf16[512,256]{1,0:T(8,128)(2,1)S(1)} %get-tuple-element.57), channel_id=1, source_target_pairs={{0,12},{1,13},{2,14},{3,15},{4,0},{5,1},{6,2},{7,3},{8,4},{9,5},{1... | collective-permute-start | bytes 786440 | tf_op jit(solution)/shard_map/ppermute | solution.py:397
  90.2 7.9 %copy-start.1 = (bf16[512,512]{1,0:T(8,128)(2,1)S(1)}, bf16[512,512]{1,0:T(8,128)(2,1)}, u32[]{:S(2)}) copy-start(bf16[512,512]{1,0:T(8,128)(2,1)} %shard_map.149.refs_6_) | copy-start | bytes 1572868

commit v3 on v2

--- a/solution.py
+++ b/solution.py
@@ -20,9 +20,9 @@
 F32 = jnp.float32
 US = 10**5
 NT = (((1,), (1,)), ((), ()))
-VMEM_LIMIT = 28 * 1024 * 1024
-
-SEQ, CORE, GROUP, LENGTH, YPOS, XLO, ZPOS, XHI = range(8)
+VMEM_LIMIT = 16 * 1024 * 1024
+
+SEQ, CORE, GROUP, LENGTH, YPOS, XLO, ZPOS, XHI, COLUMNS = range(9)
 
 
 def call(kernel, info, args, in_specs, out_specs, out_shape, grid=(1,), scratch=(), flops=0, nbytes=0, trans=0, extra=(), after=(), limit=VMEM_LIMIT, alias=None):
@@ -67,6 +67,10 @@
 
 def shape(dims, kind):
     return jax.ShapeDtypeStruct(dims, kind)
+
+
+def kept_shape(dims, kind):
+    return pltpu.VMEM(dims, kind)
 
 
 def split2(a):
@@ -187,7 +191,7 @@
             y_ref[here, part] = y + skip_ref[h] * mv_ref[here, :].astype(F32)
 
 
-def gate_kernel(info, cum_ref, c_ref, y_ref, g_ref, prefix_ref, pdec_ref, own_ref, got_ref, out0, out1, out2, out3, fin_ref):
+def gate_kernel(info, cum_ref, c_ref, y_ref, g_ref, prefix_ref, pdec_ref, own_ref, got_ref, out0, out1, fin_ref):
     second = info[XLO] == 1
     ecols = jnp.exp(cum_ref[0:8, :]).T
     for h in range(HEADS):
@@ -201,7 +205,7 @@
         )
         y = y_ref[:, part] + ecols[:, h : h + 1] * carried
         g = g_ref[:, part].astype(F32)
-        (out0, out1, out2, out3)[h][...] = (y * (g / (1.0 + jnp.exp(-g)))).astype(BF)
+        (out0, out1)[h // 2][:, (h % 2) * HD : (h % 2 + 1) * HD] = (y * (g / (1.0 + jnp.exp(-g)))).astype(BF)
     own_log = log_of(own_ref)
     got_log = log_of(got_ref)
     later = jnp.exp(jnp.where(second, own_log, got_log))
@@ -214,25 +218,6 @@
         fin_ref[h] = last + later[h : h + 1, :] * first
 
 
-def place_kernel(info, *refs):
-    mine, other, (k_ref, v_ref) = refs[0:5], refs[5:10], refs[10:12]
-    zero = info[CORE] == 0
-    y, x = info[YPOS], info[XLO]
-
-    def put(a, b, where):
-        rows = pl.ds(pl.multiple_of(where * TOK, TOK), TOK)
-        a, b = a.astype(F32), b.astype(F32)
-        k_ref[rows, :] = jnp.where(zero, a, b).astype(BF)
-        v_ref[rows, :] = jnp.where(zero, b, a).astype(BF)
-
-    put(mine[0][...], other[0][...], x * 4 + y)
-    put(mine[1][...], other[1][...], (1 - x) * 4 + y)
-    for d in range(1, 4):
-        ypos = lax.rem(y - d + 4, 4)
-        put(mine[d + 1][0:TOK, :], other[d + 1][0:TOK, :], x * 4 + ypos)
-        put(mine[d + 1][TOK : 2 * TOK, :], other[d + 1][TOK : 2 * TOK, :], (1 - x) * 4 + ypos)
-
-
 SCALE = math.log2(math.e) / math.sqrt(HD)
 HALF = TOK // 2
 UNITS = [(h, i) for h in range(HEADS) for i in range(2)]
@@ -244,13 +229,36 @@
     return jnp.concatenate([vt, jnp.ones((16, vt.shape[1]), BF)], axis=0)
 
 
+def split_pair(info, mine, other):
+    zero = jnp.broadcast_to(info[CORE], mine.shape) == 0
+    a, b = mine.astype(F32), other.astype(F32)
+    return jnp.where(zero, a, b).astype(BF), jnp.where(zero, b, a).astype(BF)
+
+
+def pieces(q_ref):
+    return [q_ref[i * HALF : (i + 1) * HALF, h * HD : (h + 1) * HD] for h, i in UNITS]
+
+
+def add_block(queries, k, v, state):
+    vt = with_ones([v[i * HD : (i + 1) * HD] for i in range(TOK // HD)])
+    scores = [lax.dot_general(k, q, NT, preferred_element_type=F32) for q in queries]
+    new = []
+    for u in range(len(UNITS)):
+        best, summed = state[2 * u], state[2 * u + 1]
+        top = jnp.maximum(best, jnp.max(scores[u], axis=0, keepdims=True))
+        weights = jnp.exp2((scores[u] - top) * SCALE).astype(BF)
+        shrink = jnp.exp2((best - top) * SCALE)
+        new += [top, summed * shrink + jnp.dot(vt, weights, preferred_element_type=F32)]
+    return tuple(new)
+
+
 def diagonal_kernel(info, q_ref, k_ref, v_ref, best_ref, acc_ref):
     limit = info[LENGTH] - info[SEQ] * TOK
     vt = with_ones([v_ref[i * HD : (i + 1) * HD, :] for i in range(TOK // HD)])
+    queries = pieces(q_ref)
     for u, (h, i) in enumerate(UNITS):
         wide = (i + 1) * HALF
-        q = q_ref[i * HALF : (i + 1) * HALF, h * HD : (h + 1) * HD]
-        scores = lax.dot_general(k_ref[0:wide, :], q, NT, preferred_element_type=F32)
+        scores = lax.dot_general(k_ref[0:wide, :], queries[u], NT, preferred_element_type=F32)
         s = lax.broadcasted_iota(jnp.int32, (wide, HALF), 0)
         t = i * HALF + lax.broadcasted_iota(jnp.int32, (wide, HALF), 1)
         keep = jnp.logical_and(s <= t, s < limit)
@@ -261,37 +269,30 @@
         acc_ref[u] = jnp.dot(vt[:, 0:wide], weights, preferred_element_type=F32)
 
 
-def earlier_kernel(heads, info, q_ref, k_ref, v_ref, best_ref, acc_ref, out_ref):
-    units = [(h, i) for h in range(heads) for i in range(2)]
-    queries = [q_ref[i * HALF : (i + 1) * HALF, h * HD : (h + 1) * HD] for h, i in units]
-
-    def one(j, state):
-        base = pl.multiple_of(j * TOK, TOK)
-        k = k_ref[pl.ds(base, TOK), :]
-        vt = with_ones([v_ref[pl.ds(base + i * HD, HD), :] for i in range(TOK // HD)])
-        scores = [lax.dot_general(k, q, NT, preferred_element_type=F32) for q in queries]
-        new = []
-        for u in range(len(units)):
-            best, summed = state[2 * u], state[2 * u + 1]
-            top = jnp.maximum(best, jnp.max(scores[u], axis=0, keepdims=True))
-            weights = jnp.exp2((scores[u] - top) * SCALE).astype(BF)
-            shrink = jnp.exp2((best - top) * SCALE)
-            new += [top, summed * shrink + jnp.dot(vt, weights, preferred_element_type=F32)]
-        return tuple(new)
-
+def earlier_kernel(info, q_ref, far, far_other, mine, other, best_ref, acc_ref, out_ref, k_all, v_all):
+    y, x = info[YPOS], info[XLO]
+    place = (1 - x) * 4 + y
+    k_all[place], v_all[place] = split_pair(info, far[...], far_other[...])
+    for d in (1, 2, 3):
+        for plane, rows in ((x, slice(0, TOK)), (1 - x, slice(TOK, 2 * TOK))):
+            place = plane * 4 + lax.rem(y - d + 4, 4)
+            k_all[place], v_all[place] = split_pair(info, mine[d - 1, rows, :], other[d - 1, rows, :])
+    queries = pieces(q_ref)
     start = []
-    for u in range(len(units)):
+    for u in range(len(UNITS)):
         start += [best_ref[u, 0:1, :], acc_ref[u]]
-    state = lax.fori_loop(0, info[SEQ], one, tuple(start))
-    for u, (h, i) in enumerate(units):
+    state = lax.fori_loop(
+        0, info[SEQ], lambda j, state: add_block(queries, k_all[j], v_all[j], state), tuple(start)
+    )
+    for u, (h, i) in enumerate(UNITS):
         summed = state[2 * u + 1]
         out = summed[0:HD] * (1.0 / summed[HD : HD + 1])
         out_ref[i * HALF : (i + 1) * HALF, h * HD : (h + 1) * HD] = out.T.astype(BF)
 
 
-def weights_kernel(info, columns, near, far, out_ref, sems):
+def weights_kernel(info, near, far, out_ref, sems):
     def copies(k):
-        part = pl.ds(pl.multiple_of(columns[k] * CB, CB), CB)
+        part = pl.ds(pl.multiple_of(info[COLUMNS + k] * CB, CB), CB)
         return (
             pltpu.make_async_copy(near.at[:, part], out_ref.at[k, 0:TOK, :], sems.at[0, k]),
             pltpu.make_async_copy(far.at[:, part], out_ref.at[k, TOK : 2 * TOK, :], sems.at[1, k]),
@@ -312,7 +313,9 @@
 
 
 def first_kernel(info, *refs):
-    gated, weights, to_x, to_z = refs[0:8], refs[8], refs[9], refs[10:13]
+    gated, weights, got, to_x, to_z, bundle = refs[0:4], refs[4], refs[5:8], refs[8], refs[9:12], refs[12]
+    for d in range(3):
+        bundle[d] = got[d][...]
     for i in range(2):
         acc = product(gated, weights, 2 * i, 2).astype(BF)
         to_x[2 * i] = acc[:, 0:CB]
@@ -324,7 +327,7 @@
 
 
 def second_kernel(info, *refs):
-    gated, (weights, z1, z2, z3, x, to_x), to_z = refs[0:8], refs[8:14], refs[14:17]
+    gated, (weights, z1, z2, z3, x, to_x), to_z = refs[0:4], refs[4:10], refs[10:13]
     acc = product(gated, weights, 10, 2)
     total = acc[:, 0:CB]
     for r in (z1, z2, z3):
@@ -339,7 +342,7 @@
 
 
 def keep_kernel(info, *refs):
-    gated, (weights, z1, z2, z3, x, out_ref) = refs[0:8], refs[8:14]
+    gated, (weights, z1, z2, z3, x, out_ref) = refs[0:4], refs[4:10]
     acc = product(gated, weights, 14, 2)
     total = acc[:, 0:CB]
     for r in (z1, z2, z3):
@@ -390,66 +393,56 @@
     seq = lax.axis_index("seq")
     head = lax.axis_index("head")
     z, x, c = head // 4, (head // 2) % 2, head % 2
-    info = jnp.stack([seq, c, head // 2, length[0], seq % 4, seq // 4, z, x]).astype(jnp.int32)
-    core = lambda a: lax.ppermute(a, "head", CORE_SWAP)
-    lo = lambda a: lax.ppermute(a, "seq", LO_SWAP)
-    along_y = lambda a, d: lax.ppermute(a, "seq", Y_MOVE[d])
-    along_z = lambda a, d: lax.ppermute(a, "head", Z_MOVE[d])
-
-    far_weight = core(out_weight)
-    keys, values, mixer_values, mixer_keys = hbm(keys), hbm(values), hbm(mixer_values), hbm(mixer_keys)
-    queries, mixer_queries, gate_values = hbm(queries), hbm(mixer_queries), hbm(gate_values)
-
-    k_own, vt_own, kv, msg, cum, mv, mk = call(
-        prep_kernel,
-        info,
-        (keys, values, mixer_values, mixer_keys, step_size, decay_rate),
-        [HBM, HBM, HBM, HBM, full((HEADS, TOK)), SMEM],
-        [full((TOK, HD))] * 3 + [full((MSG, HD)), full((16, TOK))] + [full((TOK, HD))] * 2,
-        [shape((TOK, HD), BF)] * 3 + [shape((MSG, HD), BF), shape((16, TOK), F32)] + [shape((TOK, HD), BF)] * 2,
-        scratch=[pltpu.VMEM((TOK, HD), BF), pltpu.SemaphoreType.DMA((4,))],
-        flops=US,
-    )
-    msgs = [msg] + [along_y(msg, d) for d in (1, 2, 3)]
-    kv_far = lo(kv)
-
-    y_in = call(
-        intra_kernel,
-        info,
-        (cum, mixer_queries, mk, mv, skip_gain),
-        [full((16, TOK)), full((TOK, ROWS)), full((TOK, HD)), full((TOK, HD)), SMEM],
-        full((TOK, ROWS)),
-        shape((TOK, ROWS), F32),
-        flops=US,
-    )
-    best, acc = call(
-        diagonal_kernel,
-        info,
-        (queries, k_own, vt_own),
-        [full((TOK, ROWS)), full((TOK, HD)), full((TOK, HD))],
-        [full((8, 8, HALF)), full((8, ACC, HALF))],
-        [shape((8, 8, HALF), F32), shape((8, ACC, HALF), F32)],
-        flops=US,
-    )
     block = lambda zz, xx, half: ((zz % 4) * 4 + (xx % 2) * 2 + c) * 2 + half
-    columns = jnp.stack(
+    columns = (
         [block(i, x + 1, 1) for i in range(4)]
         + [block(z + d, i, 0) for d in (1, 2, 3) for i in range(2)]
         + [block(z, x + 1, 0)]
         + [block(z + d, x, 1) for d in (1, 2, 3)]
         + [block(z, x, 0), block(z, x, 1)]
-    ).astype(jnp.int32)
-    weights = call(
-        weights_kernel,
-        info,
-        (hbm(out_weight), hbm(far_weight)),
-        [HBM, HBM],
-        VMEM,
-        pltpu.VMEM((16, 2 * TOK, CB), BF),
-        scratch=[pltpu.SemaphoreType.DMA((2, 16))],
-        flops=US,
-        extra=(columns,),
-        after=(acc, y_in),
+    )
+    info = jnp.stack([seq, c, head // 2, length[0], seq % 4, seq // 4, z, x, *columns]).astype(jnp.int32)
+    core = lambda a: lax.ppermute(a, "head", CORE_SWAP)
+    lo = lambda a: lax.ppermute(a, "seq", LO_SWAP)
+    along_y = lambda a, d: lax.ppermute(a, "seq", Y_MOVE[d])
+    along_z = lambda a, d: lax.ppermute(a, "head", Z_MOVE[d])
+
+    far_weight = core(out_weight)
+    keys, values, mixer_values, mixer_keys = hbm(keys), hbm(values), hbm(mixer_values), hbm(mixer_keys)
+    step_size, decay_rate, skip_gain = hbm(step_size), hbm(decay_rate), hbm(skip_gain)
+
+    k_own, vt_own, kv, msg, cum, mv, mk = call(
+        prep_kernel,
+        info,
+        (keys, values, mixer_values, mixer_keys, step_size, decay_rate),
+        [HBM, HBM, HBM, HBM, full((HEADS, TOK)), SMEM],
+        [full((TOK, HD))] * 3 + [full((MSG, HD)), full((16, TOK))] + [full((TOK, HD))] * 2,
+        [kept_shape((TOK, HD), BF)] * 3 + [kept_shape((MSG, HD), BF), kept_shape((16, TOK), F32)] + [kept_shape((TOK, HD), BF)] * 2,
+        scratch=[pltpu.VMEM((TOK, HD), BF), pltpu.SemaphoreType.DMA((4,))],
+        flops=US,
+    )
+    from_1, from_3, from_2 = [along_y(msg, d) for d in (1, 3, 2)]
+    msgs = [msg, from_1, from_2, from_3]
+    kv_far = lo(kv)
+    kv_far_other = core(kv_far)
+
+    y_in = call(
+        intra_kernel,
+        info,
+        (cum, hbm(mixer_queries), mk, mv, skip_gain),
+        [full((16, TOK)), full((TOK, ROWS)), full((TOK, HD)), full((TOK, HD)), SMEM],
+        full((TOK, ROWS)),
+        kept_shape((TOK, ROWS), F32),
+        flops=US,
+    )
+    best, acc = call(
+        diagonal_kernel,
+        info,
+        (hbm(queries), k_own, vt_own),
+        [full((TOK, ROWS)), full((TOK, HD)), full((TOK, HD))],
+        [full((8, 8, HALF)), full((8, ACC, HALF))],
+        [kept_shape((8, 8, HALF), F32), kept_shape((8, ACC, HALF), F32)],
+        flops=US,
     )
     prefix, pdec, total, kv_pair = call(
         combine_kernel,
@@ -457,12 +450,13 @@
         (*msgs, kv, kv_far),
         [full((MSG, HD))] * 4 + [full((TOK, HD))] * 2,
         [full((ROWS, HD)), full((8, HD)), full((MSG, HD)), full((2 * TOK, HD))],
-        [shape((ROWS, HD), F32), shape((8, HD), F32), shape((MSG, HD), BF), shape((2 * TOK, HD), BF)],
-        flops=US,
-        after=(y_in, acc, weights),
+        [kept_shape((ROWS, HD), F32), kept_shape((8, HD), F32), kept_shape((MSG, HD), BF), kept_shape((2 * TOK, HD), BF)],
+        flops=US,
+        after=(y_in, acc),
     )
     total_far = lo(total)
-    from_y = [along_y(kv_pair, d) for d in (1, 2, 3)]
+    from_1, from_3, from_2 = [along_y(kv_pair, d) for d in (1, 3, 2)]
+    from_y = [from_1, from_2, from_3]
     *gated, final_states = call(
         gate_kernel,
         info,
@@ -477,79 +471,72 @@
             full((MSG, HD)),
             full((MSG, HD)),
         ],
-        [full((TOK, HD))] * 4 + [full((HEADS, HD // 8, NST))],
-        [shape((TOK, HD), BF)] * 4 + [shape((HEADS, HD // 8, NST), F32)],
-        flops=US,
+        [full((TOK, 2 * HD))] * 2 + [full((HEADS, HD // 8, NST))],
+        [shape((TOK, 2 * HD), BF)] * 2 + [shape((HEADS, HD // 8, NST), F32)],
+        flops=US,
+    )
+    weights = call(
+        weights_kernel,
+        info,
+        (hbm(out_weight), hbm(far_weight)),
+        [HBM, HBM],
+        VMEM,
+        pltpu.VMEM((16, 2 * TOK, CB), BF),
+        scratch=[pltpu.SemaphoreType.DMA((2, 16))],
+        flops=10**10,
+        after=(gated[0],),
     )
     gated += [core(a) for a in gated]
 
-    to_x, *to_z = call(
+    to_x, *to_z, bundle = call(
         first_kernel,
         info,
-        (*gated, weights),
+        (*gated, weights, *from_y),
+        [VMEM] * 8,
+        [VMEM] * 5,
+        [shape((4, TOK, CB), BF)] + [shape((2, TOK, CB), BF)] * 3 + [shape((3, 2 * TOK, HD), BF)],
+        flops=US,
+    )
+    from_x = lax.ppermute(to_x, "head", X_SWAP)
+    from_1, from_3, from_2 = [along_z(to_z[d - 1], d) for d in (1, 3, 2)]
+    from_z = [from_1, from_2, from_3]
+
+    attended = call(
+        earlier_kernel,
+        info,
+        (queries, kv_far, kv_far_other, bundle, core(bundle), best, acc),
+        [full((TOK, ROWS))] + [full((TOK, HD))] * 2 + [full((3, 2 * TOK, HD))] * 2 + [full((8, 8, HALF)), full((8, ACC, HALF))],
+        full((TOK, ROWS)),
+        shape((TOK, ROWS), BF),
+        scratch=[pltpu.VMEM((8, TOK, HD), BF)] * 2,
+        flops=US,
+        limit=28 * 1024 * 1024,
+        after=(to_z[0],),
+    )
+
+    to_x2, *to_z2 = call(
+        second_kernel,
+        info,
+        (*gated, weights, *from_z, from_x),
         [VMEM] * 9,
         [VMEM] * 4,
-        [shape((4, TOK, CB), BF)] + [shape((2, TOK, CB), BF)] * 3,
-        flops=US,
-        after=from_y,
-    )
-    from_x = lax.ppermute(to_x, "head", X_SWAP)
-    from_z = [along_z(to_z[d - 1], d) for d in (1, 2, 3)]
-
-    mine = [kv, kv_far] + from_y
-    other = [core(a) for a in mine]
-    pieces = [full((TOK, HD))] * 2 + [full((2 * TOK, HD))] * 3
-    k_all, v_all = call(
-        place_kernel,
-        info,
-        (*mine, *other),
-        pieces * 2,
-        [full((8 * TOK, HD))] * 2,
-        [shape((8 * TOK, HD), BF)] * 2,
-        flops=US,
-        after=(to_z[0],),
-    )
-
-    def earlier(heads, first, after, prior=None):
-        part = lambda *dims: pl.BlockSpec((2 * heads, *dims), lambda i, info: (first // heads, 0, 0))
-        column = pl.BlockSpec((TOK, heads * HD), lambda i, info: (0, first // heads))
-        return call(
-            lambda *refs: earlier_kernel(heads, *refs),
-            info,
-            (queries, k_all, v_all, best, acc),
-            [column, full((8 * TOK, HD)), full((8 * TOK, HD)), part(8, HALF), part(ACC, HALF)],
-            column,
-            shape((TOK, ROWS), BF),
-            flops=US,
-            after=after if prior is None else (prior, *after),
-            alias=None if prior is None else 0,
-        )
-
-    attended = earlier(2, 0, (to_z[0],))
-
-    to_x2, *to_z2 = call(
-        second_kernel,
-        info,
-        (*gated, weights, *from_z, from_x),
-        [VMEM] * 13,
-        [VMEM] * 4,
         [shape((TOK, CB), BF)] * 4,
         flops=US,
-        after=(attended,),
-    )
+        after=(hbm(attended),),
+    )
+    from_1, from_3, from_2 = [along_z(to_z2[d - 1], d) for d in (1, 3, 2)]
+    from_z2 = [from_1, from_2, from_3]
     from_x2 = lax.ppermute(to_x2, "head", X_SWAP)
-    from_z2 = [along_z(to_z2[d - 1], d) for d in (1, 2, 3)]
     kept = call(
         keep_kernel,
         info,
         (*gated, weights, *from_z, from_x),
-        [VMEM] * 13,
+        [VMEM] * 9,
         VMEM,
         shape((TOK, ROWS), F32),
         flops=US,
         after=(to_x2,),
     )
-    attended = earlier(2, 2, (to_x2,), attended)
     summed = call(
         finish_kernel,
         info,
@@ -558,7 +545,6 @@
         full((TOK, ROWS)),
         shape((TOK, ROWS), BF),
         flops=US,
-        after=(attended,),
     )
     return (attended, summed, final_states)
 

time: 100 us -> 90.1 us (0.901)
  Pallas kernels: 32 us -> 27.4 us
  local copies, waits for them, and re-layouts: 3.23 us -> 0.12 us
  starting transfers between devices: 28.7 us -> 27.6 us
    pallas_call x13 -> x11, Pallas kernels: 32 us -> 27.4 us  [call(): pl.pallas_call(run, grid_spec=spec, out_shape=out_shape, input_output_ali...]
    ppermute x10 -> x5, waiting for transfers between devices: 3.16 us -> 0.01 us  [body(): core = lambda a: lax.ppermute(a, 'head', CORE_SWAP)]
    unnamed x10 -> x6, local copies, waits for them, and re-layouts: 3.05 us -> 0.02 us
    ppermute x6, waiting for transfers between devices: 23.8 us -> 26.6 us  [body(): along_z = lambda a, d: lax.ppermute(a, 'head', Z_MOVE[d])]
    ppermute x1, waiting for transfers between devices: 0.01 us -> 2.24 us  [body(): from_x2 = lax.ppermute(to_x2, 'head', X_SWAP)]
    ppermute x6, waiting for transfers between devices: 4.52 us -> 3.09 us  [body(): along_y = lambda a, d: lax.ppermute(a, 'seq', Y_MOVE[d])]
    ppermute x2, waiting for transfers between devices: 2.54 us -> 1.17 us  [body(): lo = lambda a: lax.ppermute(a, 'seq', LO_SWAP)]
    ppermute x10 -> x5, starting transfers between devices: 2.13 us -> 1.11 us  [body(): core = lambda a: lax.ppermute(a, 'head', CORE_SWAP)]
  transfers between devices with their start and end apart: 26 -> 21, of which waited for: 10 -> 7; matrix products, arithmetic and copies ran while one was open for 0% -> 0% of each run, Pallas kernels for 25% -> 23%
where the time goes in v3:
time: 90.1 us; the launch traced here: 89.9 us
  waiting for transfers between devices  33.1 us (37%)
  starting transfers between devices  27.6 us (31%)
  Pallas kernels  27.4 us (30%)
  between operations  1.64 us (2%)
    pallas_call x11, Pallas kernels, call(): pl.pallas_call(run, grid_spec=spec, out_shape=out_shape, input_output_ali...  27.4 us
    ppermute x6, waiting for transfers between devices, body(): along_z = lambda a, d: lax.ppermute(a, 'head', Z_MOVE[d])  26.6 us
    ppermute x6, starting transfers between devices, body(): along_z = lambda a, d: lax.ppermute(a, 'head', Z_MOVE[d])  11.4 us
    ppermute x6, starting transfers between devices, body(): along_y = lambda a, d: lax.ppermute(a, 'seq', Y_MOVE[d])  9.33 us
    ppermute x1, starting transfers between devices, body(): from_x = lax.ppermute(to_x, 'head', X_SWAP)  3.1 us
    ppermute x6, waiting for transfers between devices, body(): along_y = lambda a, d: lax.ppermute(a, 'seq', Y_MOVE[d])  3.09 us
    ppermute x1, waiting for transfers between devices, body(): from_x2 = lax.ppermute(to_x2, 'head', X_SWAP)  2.24 us
    ppermute x2, starting transfers between devices, body(): lo = lambda a: lax.ppermute(a, 'seq', LO_SWAP)  2.1 us
  transfers between devices with their start and end apart: 21, of which 7 were waited for; matrix products, arithmetic and copies ran while one was open for 0% of the time, Pallas kernels for 23%

profile of v3, /device:TPU:0, one launch (start us, length us, event | category | flops | bytes accessed | tf_op | source)
XLA Modules:
  0.0 89.9 jit_solution(9196220754079282376)
XLA Ops:
  0.6 0.0 copy-start.1
  0.6 0.0 copy-start.2
  0.7 0.1 collective-permute-start.8
  1.6 0.1 stack.95.refs_0_
  1.7 3.3 %shard_map.139 = (bf16[512,128]{1,0:T(8,128)(2,1)S(1)}, bf16[512,128]{1,0:T(8,128)(2,1)S(1)}, bf16[512,128]{1,0:T(8,128)(2,1)S(1)}, bf16[544,128]{1,0:T(8,128)(2...) custom-call(s32[24]{0:T(128)S(1)} %stack.95.refs_0_, ...), custom_call_target="tpu_custom_call" | custom-call | flops 100000 | tf_op jit(solution)/shard_map/pallas_call | solution.py:44
  5.1 1.7 %collective-permute-start.2 = (bf16[544,128]{1,0:T(8,128)(2,1)S(1)}, bf16[544,128]{1,0:T(8,128)(2,1)S(1)}, u32[]{:S(2)}, u32[]{:S(2)}) collective-permute-start(bf16[544,128]{1,0:T(8,128)(2,1)S(1)} %get-tuple-element.32.refs_1_), channel_id=1, source_target_pairs={{0,16},{16,32},{32,48},{48,0},{64,80},{80,96},{96,112},{112,64},{1... | collective-permute-start | bytes 417800 | tf_op jit(solution)/shard_map/ppermute | solution.py:407
  6.8 2.9 %collective-permute-start.3 = (bf16[544,128]{1,0:T(8,128)(2,1)S(1)}, bf16[544,128]{1,0:T(8,128)(2,1)S(1)}, u32[]{:S(2)}, u32[]{:S(2)}) collective-permute-start(bf16[544,128]{1,0:T(8,128)(2,1)S(1)} %get-tuple-element.32.refs_1_), channel_id=1, source_target_pairs={{0,32},{16,48},{32,0},{48,16},{64,96},{80,112},{96,64},{112,80},{1... | collective-permute-start | bytes 417800 | tf_op jit(solution)/shard_map/ppermute | solution.py:407
  9.7 1.3 %collective-permute-start.4 = (bf16[544,128]{1,0:T(8,128)(2,1)S(1)}, bf16[544,128]{1,0:T(8,128)(2,1)S(1)}, u32[]{:S(2)}, u32[]{:S(2)}) collective-permute-start(bf16[544,128]{1,0:T(8,128)(2,1)S(1)} %get-tuple-element.32.refs_1_), channel_id=1, source_target_pairs={{0,48},{16,0},{32,16},{48,32},{64,112},{80,64},{96,80},{112,96},{1... | collective-permute-start | bytes 417800 | tf_op jit(solution)/shard_map/ppermute | solution.py:407
  11.0 1.5 %collective-permute-start = (bf16[512,128]{1,0:T(8,128)(2,1)S(1)}, bf16[512,128]{1,0:T(8,128)(2,1)S(1)}, u32[]{:S(2)}, u32[]{:S(2)}) collective-permute-start(bf16[512,128]{1,0:T(8,128)(2,1)S(1)} %get-tuple-element.28.refs_5_), channel_id=1, source_target_pairs={{0,64},{16,80},{32,96},{48,112},{64,0},{80,16},{96,32},{112,48},{1... | collective-permute-start | bytes 393224 | tf_op jit(solution)/shard_map/ppermute | solution.py:406
  12.5 3.8 %shard_map.141 = (f32[8,8,256]{2,1,0:T(8,128)S(1)}, f32[8,144,256]{2,1,0:T(8,128)S(1)}) custom-call(s32[24]{0:T(128)S(1)} %stack.95.refs_0_, bf16[512,512]{1,0:T(8,128)(2,1)} %refs_1_.7, bf16[512,128]{1,0:T(8,128)(2,1)S(1)} %get-tuple-element.33.refs_2_, bf16[512,128]{1,0:T(8,128)(2,1)S(1)} %get-tuple-element.34.refs_3_), custom_call_target="tpu_custom_call" | custom-call | flops 100000 | tf_op jit(solution)/shard_map/pallas_call | solution.py:44
  16.3 3.3 %shard_map.140.refs_7_.refs_3_ = f32[512,512]{1,0:T(8,128)S(1)} custom-call(s32[24]{0:T(128)S(1)} %stack.95.refs_0_, f32[16,512]{1,0:T(8,128)S(1)} %get-tuple-element.29.refs_1_, bf16[512,512]{1,0:T(8,128)(2,1)} %refs_2_.5, bf16[512,128]{1,0:T(8,128)(2,1)S(1)} %get-tuple-element.30.refs_3_, bf16[512,128]{1,0:T(8,128)(2,1)S(1)} %get-tuple-element.31.refs_4_, ...), custom_call_target="tpu_custom_call" | custom-call | flops 100000 | tf_op jit(solution)/shard_map/pallas_call | solution.py:44
  19.6 0.0 collective-permute-done.refs_6_.refs_2_
  19.6 0.0 collective-permute-done.2.refs_2_
  19.6 0.0 collective-permute-done.3.refs_3_
  19.6 0.0 collective-permute-done.4.refs_4_
  19.7 0.8 shard_map.142
  20.4 0.6 collective-permute-start.5
  21.0 0.4 collective-permute-start.10
  21.4 2.9 %collective-permute-start.11 = (bf16[1024,128]{1,0:T(8,128)(2,1)S(1)}, bf16[1024,128]{1,0:T(8,128)(2,1)S(1)}, u32[]{:S(2)}, u32[]{:S(2)}) collective-permute-start(bf16[1024,128]{1,0:T(8,128)(2,1)S(1)} %get-tuple-element.41), channel_id=1, source_target_pairs={{0,48},{16,0},{32,16},{48,32},{64,112},{80,64},{96,80},{112,96},{1... | collective-permute-start | bytes 786440 | tf_op jit(solution)/shard_map/ppermute | solution.py:407
  24.4 0.0 collective-permute-start.9
  24.4 1.2 %collective-permute-done.5.refs_8_ = bf16[544,128]{1,0:T(8,128)(2,1)S(1)} collective-permute-done((bf16[544,128]{1,0:T(8,128)(2,1)S(1)}, bf16[544,128]{1,0:T(8,128)(2,1)S(1)}, u32[]{:S(2)}, u32[]{:S(2)}) %collective-permute-start.5) | collective-permute-done | bytes 139296 | tf_op jit(solution)/shard_map/ppermute | solution.py:406
  25.5 0.0 copy-done.1
  25.5 0.0 copy-done.2
  25.5 1.8 %shard_map.143 = (bf16[512,256]{1,0:T(8,128)(2,1)S(1)}, bf16[512,256]{1,0:T(8,128)(2,1)S(1)}, f32[4,16,128]{2,1,0:T(8,128)}) custom-call(s32[24]{0:T(128)S(1)} %stack.95.refs_0_, f32[16,512]{1,0:T(8,128)S(1)} %get-tuple-element.29.refs_1_, bf16[512,512]{1,0:T(8,128)(2,1)S(1)} %copy-done.1, f32[512,512]{1,0:T(8,128)S(1)} %shard_map.140.refs_7_.refs_3_, ...), custom_call_target="tpu_custom_call" | custom-call | flops 100000 | tf_op jit(solution)/shard_map/pallas_call | solution.py:44
  27.3 0.0 collective-permute-start.6
  27.3 0.0 collective-permute-done.8.refs_2_
  27.3 0.5 collective-permute-start.7
  27.8 4.3 %shard_map.144.refs_5_ = bf16[16,1024,256]{2,1,0:T(8,128)(2,1)S(1)} custom-call(s32[24]{0:T(128)S(1)} %stack.95.refs_0_, bf16[512,8192]{1,0:T(8,128)(2,1)} %refs_1_.6, bf16[512,8192]{1,0:T(8,128)(2,1)} %collective-permute-done.8.refs_2_, bf16[512,256]{1,0:T(8,128)(2,1)S(1)} %get-tuple-element.39.refs_3_.refs_1_), custom_call_target="tpu_custom_call" | custom-call | flops 10000000000 | tf_op jit(solution)/shard_map/pallas_call | solution.py:44
  32.1 0.0 copy-start
  32.2 0.0 collective-permute-done.10.refs_7_
  32.2 0.9 collective-permute-done.11.refs_8_
  33.0 2.2 %collective-permute-done.9.refs_6_ = bf16[1024,128]{1,0:T(8,128)(2,1)S(1)} collective-permute-done((bf16[1024,128]{1,0:T(8,128)(2,1)S(1)}, bf16[1024,128]{1,0:T(8,128)(2,1)S(1)}, u32[]{:S(2)}, u32[]{:S(2)}) %collective-permute-start.9) | collective-permute-done | bytes 262176 | tf_op jit(solution)/shard_map/ppermute | solution.py:407
  35.2 0.0 collective-permute-done.6.refs_3_
  35.2 0.0 collective-permute-done.7.refs_4_
  35.3 3.5 %shard_map.145 = (bf16[4,512,256]{2,1,0:T(8,128)(2,1)S(1)}, bf16[2,512,256]{2,1,0:T(8,128)(2,1)S(1)}, bf16[2,512,256]{2,1,0:T(8,128)(2,1)S(1)}, bf16[2,512,256]{...) custom-call(s32[24]{0:T(128)S(1)} %stack.95.refs_0_, bf16[512,256]{1,0:T(8,128)(2,1)S(1)} %get-tuple-element.39.refs_3_.refs_1_, ...), custom_call_target="tpu_custom_call" | custom-call | flops 100000 | tf_op jit(solution)/shard_map/pallas_call | solution.py:44
  38.7 3.1 %collective-permute-start.16 = (bf16[4,512,256]{2,1,0:T(8,128)(2,1)S(1)}, bf16[4,512,256]{2,1,0:T(8,128)(2,1)S(1)}, u32[]{:S(2)}, u32[]{:S(2)}) collective-permute-start(bf16[4,512,256]{2,1,0:T(8,128)(2,1)S(1)} %get-tuple-element.47), channel_id=1, source_target_pairs={{0,2},{1,3},{2,0},{3,1},{4,6},{5,7},{6,4},{7,5},{8,10},{9,11},{10,... | collective-permute-start | bytes 3145736 | tf_op jit(solution)/shard_map/ppermute | solution.py:500
  41.8 0.0 collective-permute-start.12
  41.8 0.5 collective-permute-start.1
  42.3 1.9 %collective-permute-start.13 = (bf16[2,512,256]{2,1,0:T(8,128)(2,1)S(1)}, bf16[2,512,256]{2,1,0:T(8,128)(2,1)S(1)}, u32[]{:S(2)}, u32[]{:S(2)}) collective-permute-start(bf16[2,512,256]{2,1,0:T(8,128)(2,1)S(1)} %get-tuple-element.44.refs_8_), channel_id=1, source_target_pairs={{0,4},{1,5},{2,6},{3,7},{4,8},{5,9},{6,10},{7,11},{8,12},{9,13},{1... | collective-permute-start | bytes 1572872 | tf_op jit(solution)/shard_map/ppermute | solution.py:408
  44.3 3.6 %collective-permute-start.14 = (bf16[2,512,256]{2,1,0:T(8,128)(2,1)S(1)}, bf16[2,512,256]{2,1,0:T(8,128)(2,1)S(1)}, u32[]{:S(2)}, u32[]{:S(2)}) collective-permute-start(bf16[2,512,256]{2,1,0:T(8,128)(2,1)S(1)} %get-tuple-element.45), channel_id=1, source_target_pairs={{0,8},{1,9},{2,10},{3,11},{4,12},{5,13},{6,14},{7,15},{8,0},{9,1},... | collective-permute-start | bytes 1572872 | tf_op jit(solution)/shard_map/ppermute | solution.py:408
  47.8 0.0 collective-permute-done.1.refs_3_
  47.8 1.0 %collective-permute-start.15 = (bf16[2,512,256]{2,1,0:T(8,128)(2,1)S(1)}, bf16[2,512,256]{2,1,0:T(8,128)(2,1)S(1)}, u32[]{:S(2)}, u32[]{:S(2)}) collective-permute-start(bf16[2,512,256]{2,1,0:T(8,128)(2,1)S(1)} %get-tuple-element.46), channel_id=1, source_target_pairs={{0,12},{1,13},{2,14},{3,15},{4,0},{5,1},{6,2},{7,3},{8,4},{9,5},{1... | collective-permute-start | bytes 1572872 | tf_op jit(solution)/shard_map/ppermute | solution.py:408
  48.9 0.0 collective-permute-done.12.refs_5_
  48.9 0.0 copy-done
  48.9 2.2 %shard_map.146.refs_10_ = bf16[512,512]{1,0:T(8,128)(2,1)} custom-call(s32[24]{0:T(128)S(1)} %stack.95.refs_0_, bf16[512,512]{1,0:T(8,128)(2,1)S(1)} %copy-done, bf16[512,128]{1,0:T(8,128)(2,1)S(1)} %collective-permute-done.refs_6_.refs_2_, bf16[512,128]{1,0:T(8,128)(2,1)S(1)} %collective-permute-done.1.refs_3_, ...), custom_call_target="tpu_custom_call" | custom-call | flops 100000 | tf_op jit(solution)/shard_map/pallas_call | solution.py:44
  51.0 7.4 %collective-permute-done.13.refs_6_ = bf16[2,512,256]{2,1,0:T(8,128)(2,1)S(1)} collective-permute-done((bf16[2,512,256]{2,1,0:T(8,128)(2,1)S(1)}, bf16[2,512,256]{2,1,0:T(8,128)(2,1)S(1)}, u32[]{:S(2)}, u32[]{:S(2)}) %collective-permute-start.13) | collective-permute-done | bytes 524320 | tf_op jit(solution)/shard_map/ppermute | solution.py:408
  58.5 12.4 %collective-permute-done.14.refs_7_ = bf16[2,512,256]{2,1,0:T(8,128)(2,1)S(1)} collective-permute-done((bf16[2,512,256]{2,1,0:T(8,128)(2,1)S(1)}, bf16[2,512,256]{2,1,0:T(8,128)(2,1)S(1)}, u32[]{:S(2)}, u32[]{:S(2)}) %collective-permute-start.14) | collective-permute-done | bytes 524320 | tf_op jit(solution)/shard_map/ppermute | solution.py:408
  70.9 0.0 collective-permute-done.15.refs_8_
  70.9 0.0 collective-permute-done.16.refs_9_
  70.9 1.8 %shard_map.147 = (bf16[512,256]{1,0:T(8,128)(2,1)S(1)}, bf16[512,256]{1,0:T(8,128)(2,1)S(1)}, bf16[512,256]{1,0:T(8,128)(2,1)S(1)}, bf16[512,256]{1,0:T(8,128)(2,1)S(1)}) custom-call(s32[24]{0:T(128)S(1)} %stack.95.refs_0_, bf16[512,256]{1,0:T(8,128)(2,1)S(1)} %get-tuple-element.39.refs_3_.refs_1_, bf16[512,256]{1,0:T(8,128)(2,1)S(1)} %get-tuple-element.40.refs_2_, ...), custom_call_target="tpu_custom_call" | custom-call | flops 100000 | tf_op jit(solution)/shard_map/pallas_call | solution.py:44
  72.7 0.6 collective-permute-start.17
  73.3 1.1 %collective-permute-start.18 = (bf16[512,256]{1,0:T(8,128)(2,1)S(1)}, bf16[512,256]{1,0:T(8,128)(2,1)S(1)}, u32[]{:S(2)}, u32[]{:S(2)}) collective-permute-start(bf16[512,256]{1,0:T(8,128)(2,1)S(1)} %get-tuple-element.49), channel_id=1, source_target_pairs={{0,4},{1,5},{2,6},{3,7},{4,8},{5,9},{6,10},{7,11},{8,12},{9,13},{1... | collective-permute-start | bytes 786440 | tf_op jit(solution)/shard_map/ppermute | solution.py:408
  74.5 2.4 %collective-permute-start.19 = (bf16[512,256]{1,0:T(8,128)(2,1)S(1)}, bf16[512,256]{1,0:T(8,128)(2,1)S(1)}, u32[]{:S(2)}, u32[]{:S(2)}) collective-permute-start(bf16[512,256]{1,0:T(8,128)(2,1)S(1)} %get-tuple-element.50), channel_id=1, source_target_pairs={{0,8},{1,9},{2,10},{3,11},{4,12},{5,13},{6,14},{7,15},{8,0},{9,1},... | collective-permute-start | bytes 786440 | tf_op jit(solution)/shard_map/ppermute | solution.py:408
  76.8 1.3 %collective-permute-start.20 = (bf16[512,256]{1,0:T(8,128)(2,1)S(1)}, bf16[512,256]{1,0:T(8,128)(2,1)S(1)}, u32[]{:S(2)}, u32[]{:S(2)}) collective-permute-start(bf16[512,256]{1,0:T(8,128)(2,1)S(1)} %get-tuple-element.51), channel_id=1, source_target_pairs={{0,12},{1,13},{2,14},{3,15},{4,0},{5,1},{6,2},{7,3},{8,4},{9,5},{1... | collective-permute-start | bytes 786440 | tf_op jit(solution)/shard_map/ppermute | solution.py:408
  78.2 1.2 %shard_map.148.refs_1_ = f32[512,512]{1,0:T(8,128)S(1)} custom-call(s32[24]{0:T(128)S(1)} %stack.95.refs_0_, bf16[512,256]{1,0:T(8,128)(2,1)S(1)} %get-tuple-element.39.refs_3_.refs_1_, bf16[512,256]{1,0:T(8,128)(2,1)S(1)} %get-tuple-element.40.refs_2_, bf16[512,256]{1,0:T(8,128)(2,1)S(1)} %collective-permute-done.6.refs_3_, ...), custom_call_target="tpu_custom_call" | custom-call | flops 100000 | tf_op jit(solution)/shard_map/pallas_call | solution.py:44
  79.4 2.2 %collective-permute-done.17.refs_2_ = bf16[512,256]{1,0:T(8,128)(2,1)S(1)} collective-permute-done((bf16[512,256]{1,0:T(8,128)(2,1)S(1)}, bf16[512,256]{1,0:T(8,128)(2,1)S(1)}, u32[]{:S(2)}, u32[]{:S(2)}) %collective-permute-start.17) | collective-permute-done | bytes 262176 | tf_op jit(solution)/shard_map/ppermute | solution.py:529
  81.7 0.0 collective-permute-done.18.refs_3_
  81.7 6.7 %collective-permute-done.19.refs_4_ = bf16[512,256]{1,0:T(8,128)(2,1)S(1)} collective-permute-done((bf16[512,256]{1,0:T(8,128)(2,1)S(1)}, bf16[512,256]{1,0:T(8,128)(2,1)S(1)}, u32[]{:S(2)}, u32[]{:S(2)}) %collective-permute-start.19) | collective-permute-done | bytes 262176 | tf_op jit(solution)/shard_map/ppermute | solution.py:408
  88.4 0.0 collective-permute-done.20.refs_5_
  88.4 1.5 %shard_map.149 = bf16[512,512]{1,0:T(8,128)(2,1)} custom-call(s32[24]{0:T(128)S(1)} %stack.95.refs_0_, f32[512,512]{1,0:T(8,128)S(1)} %shard_map.148.refs_1_, bf16[512,256]{1,0:T(8,128)(2,1)S(1)} %collective-permute-done.17.refs_2_, bf16[512,256]{1,0:T(8,128)(2,1)S(1)} %collective-permute-done.18.refs_3_, ...), custom_call_target="tpu_custom_call" | custom-call | flops 100000 | tf_op jit(solution)/shard_map/pallas_call | solution.py:44
Async XLA Ops:
  0.6 24.9 %copy-start.1 = (bf16[512,512]{1,0:T(8,128)(2,1)S(1)}, bf16[512,512]{1,0:T(8,128)(2,1)}, u32[]{:S(2)}) copy-start(bf16[512,512]{1,0:T(8,128)(2,1)} %refs_2_.5) | copy-start | bytes 1572868
  0.6 24.9 %copy-start.2 = (bf16[512,512]{1,0:T(8,128)(2,1)S(1)}, bf16[512,512]{1,0:T(8,128)(2,1)}, u32[]{:S(2)}) copy-start(bf16[512,512]{1,0:T(8,128)(2,1)} %refs_4_.3) | copy-start | bytes 1572868
  0.7 26.7 %collective-permute-start.8 = (bf16[512,8192]{1,0:T(8,128)(2,1)}, bf16[512,8192]{1,0:T(8,128)(2,1)}, u32[]{:S(2)}, u32[]{:S(2)}) collective-permute-start(bf16[512,8192]{1,0:T(8,128)(2,1)} %refs_1_.6), channel_id=1, source_target_pairs={{0,1},{1,0},{2,3},{3,2},{4,5},{5,4},{6,7},{7,6},{8,9},{9,8},{10,11... | collective-permute-start | bytes 25165832 | tf_op jit(solution)/shard_map/ppermute | solution.py:405
  5.1 14.6 %collective-permute-start.2 = (bf16[544,128]{1,0:T(8,128)(2,1)S(1)}, bf16[544,128]{1,0:T(8,128)(2,1)S(1)}, u32[]{:S(2)}, u32[]{:S(2)}) collective-permute-start(bf16[544,128]{1,0:T(8,128)(2,1)S(1)} %get-tuple-element.32.refs_1_), channel_id=1, source_target_pairs={{0,16},{16,32},{32,48},{48,0},{64,80},{80,96},{96,112},{112,64},{1... | collective-permute-start | bytes 417800 | tf_op jit(solution)/shard_map/ppermute | solution.py:407
  6.8 12.8 %collective-permute-start.3 = (bf16[544,128]{1,0:T(8,128)(2,1)S(1)}, bf16[544,128]{1,0:T(8,128)(2,1)S(1)}, u32[]{:S(2)}, u32[]{:S(2)}) collective-permute-start(bf16[544,128]{1,0:T(8,128)(2,1)S(1)} %get-tuple-element.32.refs_1_), channel_id=1, source_target_pairs={{0,32},{16,48},{32,0},{48,16},{64,96},{80,112},{96,64},{112,80},{1... | collective-permute-start | bytes 417800 | tf_op jit(solution)/shard_map/ppermute | solution.py:407
  9.7 10.0 %collective-permute-start.4 = (bf16[544,128]{1,0:T(8,128)(2,1)S(1)}, bf16[544,128]{1,0:T(8,128)(2,1)S(1)}, u32[]{:S(2)}, u32[]{:S(2)}) collective-permute-start(bf16[544,128]{1,0:T(8,128)(2,1)S(1)} %get-tuple-element.32.refs_1_), channel_id=1, source_target_pairs={{0,48},{16,0},{32,16},{48,32},{64,112},{80,64},{96,80},{112,96},{1... | collective-permute-start | bytes 417800 | tf_op jit(solution)/shard_map/ppermute | solution.py:407
  11.0 8.6 %collective-permute-start = (bf16[512,128]{1,0:T(8,128)(2,1)S(1)}, bf16[512,128]{1,0:T(8,128)(2,1)S(1)}, u32[]{:S(2)}, u32[]{:S(2)}) collective-permute-start(bf16[512,128]{1,0:T(8,128)(2,1)S(1)} %get-tuple-element.28.refs_5_), channel_id=1, source_target_pairs={{0,64},{16,80},{32,96},{48,112},{64,0},{80,16},{96,32},{112,48},{1... | collective-permute-start | bytes 393224 | tf_op jit(solution)/shard_map/ppermute | solution.py:406
  20.4 5.1 %collective-permute-start.5 = (bf16[544,128]{1,0:T(8,128)(2,1)S(1)}, bf16[544,128]{1,0:T(8,128)(2,1)S(1)}, u32[]{:S(2)}, u32[]{:S(2)}) collective-permute-start(bf16[544,128]{1,0:T(8,128)(2,1)S(1)} %get-tuple-element.38.refs_7_), channel_id=1, source_target_pairs={{0,64},{16,80},{32,96},{48,112},{64,0},{80,16},{96,32},{112,48},{1... | collective-permute-start | bytes 417800 | tf_op jit(solution)/shard_map/ppermute | solution.py:406
  21.0 11.1 %collective-permute-start.10 = (bf16[1024,128]{1,0:T(8,128)(2,1)S(1)}, bf16[1024,128]{1,0:T(8,128)(2,1)S(1)}, u32[]{:S(2)}, u32[]{:S(2)}) collective-permute-start(bf16[1024,128]{1,0:T(8,128)(2,1)S(1)} %get-tuple-element.41), channel_id=1, source_target_pairs={{0,32},{16,48},{32,0},{48,16},{64,96},{80,112},{96,64},{112,80},{1... | collective-permute-start | bytes 786440 | tf_op jit(solution)/shard_map/ppermute | solution.py:407
  21.4 11.6 %collective-permute-start.11 = (bf16[1024,128]{1,0:T(8,128)(2,1)S(1)}, bf16[1024,128]{1,0:T(8,128)(2,1)S(1)}, u32[]{:S(2)}, u32[]{:S(2)}) collective-permute-start(bf16[1024,128]{1,0:T(8,128)(2,1)S(1)} %get-tuple-element.41), channel_id=1, source_target_pairs={{0,48},{16,0},{32,16},{48,32},{64,112},{80,64},{96,80},{112,96},{1... | collective-permute-start | bytes 786440 | tf_op jit(solution)/shard_map/ppermute | solution.py:407
  24.4 10.9 %collective-permute-start.9 = (bf16[1024,128]{1,0:T(8,128)(2,1)S(1)}, bf16[1024,128]{1,0:T(8,128)(2,1)S(1)}, u32[]{:S(2)}, u32[]{:S(2)}) collective-permute-start(bf16[1024,128]{1,0:T(8,128)(2,1)S(1)} %get-tuple-element.41), channel_id=1, source_target_pairs={{0,16},{16,32},{32,48},{48,0},{64,80},{80,96},{96,112},{112,64},{1... | collective-permute-start | bytes 786440 | tf_op jit(solution)/shard_map/ppermute | solution.py:407
  27.3 7.9 %collective-permute-start.6 = (bf16[512,256]{1,0:T(8,128)(2,1)S(1)}, bf16[512,256]{1,0:T(8,128)(2,1)S(1)}, u32[]{:S(2)}, u32[]{:S(2)}) collective-permute-start(bf16[512,256]{1,0:T(8,128)(2,1)S(1)} %get-tuple-element.39.refs_3_.refs_1_), channel_id=1, source_target_pairs={{0,1},{1,0},{2,3},{3,2},{4,5},{5,4},{6,7},{7,6},{8,9},{9,8},{10,11... | collective-permute-start | bytes 786440 | tf_op jit(solution)/shard_map/ppermute | solution.py:405
  27.3 7.9 %collective-permute-start.7 = (bf16[512,256]{1,0:T(8,128)(2,1)S(1)}, bf16[512,256]{1,0:T(8,128)(2,1)S(1)}, u32[]{:S(2)}, u32[]{:S(2)}) collective-permute-start(bf16[512,256]{1,0:T(8,128)(2,1)S(1)} %get-tuple-element.40.refs_2_), channel_id=1, source_target_pairs={{0,1},{1,0},{2,3},{3,2},{4,5},{5,4},{6,7},{7,6},{8,9},{9,8},{10,11... | collective-permute-start | bytes 786440 | tf_op jit(solution)/shard_map/ppermute | solution.py:405
  32.1 16.7 %copy-start = (bf16[512,512]{1,0:T(8,128)(2,1)S(1)}, bf16[512,512]{1,0:T(8,128)(2,1)}, u32[]{:S(2)}) copy-start(bf16[512,512]{1,0:T(8,128)(2,1)} %refs_1_.7) | copy-start | bytes 1572868
  38.7 32.2 %collective-permute-start.16 = (bf16[4,512,256]{2,1,0:T(8,128)(2,1)S(1)}, bf16[4,512,256]{2,1,0:T(8,128)(2,1)S(1)}, u32[]{:S(2)}, u32[]{:S(2)}) collective-permute-start(bf16[4,512,256]{2,1,0:T(8,128)(2,1)S(1)} %get-tuple-element.47), channel_id=1, source_target_pairs={{0,2},{1,3},{2,0},{3,1},{4,6},{5,7},{6,4},{7,5},{8,10},{9,11},{10,... | collective-permute-start | bytes 3145736 | tf_op jit(solution)/shard_map/ppermute | solution.py:500
  41.8 7.0 %collective-permute-start.12 = (bf16[3,1024,128]{2,1,0:T(8,128)(2,1)S(1)}, bf16[3,1024,128]{2,1,0:T(8,128)(2,1)S(1)}, u32[]{:S(2)}, u32[]{:S(2)}) collective-permute-start(bf16[3,1024,128]{2,1,0:T(8,128)(2,1)S(1)} %get-tuple-element.42.refs_4_), channel_id=1, source_target_pairs={{0,1},{1,0},{2,3},{3,2},{4,5},{5,4},{6,7},{7,6},{8,9},{9,8},{10,11... | collective-permute-start | bytes 2359304 | tf_op jit(solution)/shard_map/ppermute | solution.py:405
  41.8 6.0 %collective-permute-start.1 = (bf16[512,128]{1,0:T(8,128)(2,1)S(1)}, bf16[512,128]{1,0:T(8,128)(2,1)S(1)}, u32[]{:S(2)}, u32[]{:S(2)}) collective-permute-start(bf16[512,128]{1,0:T(8,128)(2,1)S(1)} %collective-permute-done.refs_6_.refs_2_), channel_id=1, source_target_pairs={{0,1},{1,0},{2,3},{3,2},{4,5},{5,4},{6,7},{7,6},{8,9},{9,8},{10,11... | collective-permute-start | bytes 393224 | tf_op jit(solution)/shard_map/ppermute | solution.py:405
  42.3 16.1 %collective-permute-start.13 = (bf16[2,512,256]{2,1,0:T(8,128)(2,1)S(1)}, bf16[2,512,256]{2,1,0:T(8,128)(2,1)S(1)}, u32[]{:S(2)}, u32[]{:S(2)}) collective-permute-start(bf16[2,512,256]{2,1,0:T(8,128)(2,1)S(1)} %get-tuple-element.44.refs_8_), channel_id=1, source_target_pairs={{0,4},{1,5},{2,6},{3,7},{4,8},{5,9},{6,10},{7,11},{8,12},{9,13},{1... | collective-permute-start | bytes 1572872 | tf_op jit(solution)/shard_map/ppermute | solution.py:408
  44.3 26.6 %collective-permute-start.14 = (bf16[2,512,256]{2,1,0:T(8,128)(2,1)S(1)}, bf16[2,512,256]{2,1,0:T(8,128)(2,1)S(1)}, u32[]{:S(2)}, u32[]{:S(2)}) collective-permute-start(bf16[2,512,256]{2,1,0:T(8,128)(2,1)S(1)} %get-tuple-element.45), channel_id=1, source_target_pairs={{0,8},{1,9},{2,10},{3,11},{4,12},{5,13},{6,14},{7,15},{8,0},{9,1},... | collective-permute-start | bytes 1572872 | tf_op jit(solution)/shard_map/ppermute | solution.py:408
  47.8 23.0 %collective-permute-start.15 = (bf16[2,512,256]{2,1,0:T(8,128)(2,1)S(1)}, bf16[2,512,256]{2,1,0:T(8,128)(2,1)S(1)}, u32[]{:S(2)}, u32[]{:S(2)}) collective-permute-start(bf16[2,512,256]{2,1,0:T(8,128)(2,1)S(1)} %get-tuple-element.46), channel_id=1, source_target_pairs={{0,12},{1,13},{2,14},{3,15},{4,0},{5,1},{6,2},{7,3},{8,4},{9,5},{1... | collective-permute-start | bytes 1572872 | tf_op jit(solution)/shard_map/ppermute | solution.py:408
  72.7 8.9 %collective-permute-start.17 = (bf16[512,256]{1,0:T(8,128)(2,1)S(1)}, bf16[512,256]{1,0:T(8,128)(2,1)S(1)}, u32[]{:S(2)}, u32[]{:S(2)}) collective-permute-start(bf16[512,256]{1,0:T(8,128)(2,1)S(1)} %get-tuple-element.48.refs_10_), channel_id=1, source_target_pairs={{0,2},{1,3},{2,0},{3,1},{4,6},{5,7},{6,4},{7,5},{8,10},{9,11},{10,... | collective-permute-start | bytes 786440 | tf_op jit(solution)/shard_map/ppermute | solution.py:529
  73.3 8.4 %collective-permute-start.18 = (bf16[512,256]{1,0:T(8,128)(2,1)S(1)}, bf16[512,256]{1,0:T(8,128)(2,1)S(1)}, u32[]{:S(2)}, u32[]{:S(2)}) collective-permute-start(bf16[512,256]{1,0:T(8,128)(2,1)S(1)} %get-tuple-element.49), channel_id=1, source_target_pairs={{0,4},{1,5},{2,6},{3,7},{4,8},{5,9},{6,10},{7,11},{8,12},{9,13},{1... | collective-permute-start | bytes 786440 | tf_op jit(solution)/shard_map/ppermute | solution.py:408
  74.5 13.9 %collective-permute-start.19 = (bf16[512,256]{1,0:T(8,128)(2,1)S(1)}, bf16[512,256]{1,0:T(8,128)(2,1)S(1)}, u32[]{:S(2)}, u32[]{:S(2)}) collective-permute-start(bf16[512,256]{1,0:T(8,128)(2,1)S(1)} %get-tuple-element.50), channel_id=1, source_target_pairs={{0,8},{1,9},{2,10},{3,11},{4,12},{5,13},{6,14},{7,15},{8,0},{9,1},... | collective-permute-start | bytes 786440 | tf_op jit(solution)/shard_map/ppermute | solution.py:408
  76.8 11.5 %collective-permute-start.20 = (bf16[512,256]{1,0:T(8,128)(2,1)S(1)}, bf16[512,256]{1,0:T(8,128)(2,1)S(1)}, u32[]{:S(2)}, u32[]{:S(2)}) collective-permute-start(bf16[512,256]{1,0:T(8,128)(2,1)S(1)} %get-tuple-element.51), channel_id=1, source_target_pairs={{0,12},{1,13},{2,14},{3,15},{4,0},{5,1},{6,2},{7,3},{8,4},{9,5},{1... | collective-permute-start | bytes 786440 | tf_op jit(solution)/shard_map/ppermute | solution.py:408

commit v4 on v3

--- a/solution.py
+++ b/solution.py
@@ -16,6 +16,7 @@
 ROWS = HEADS * HD
 MSG = ROWS + 32
 CB = 256
+Z_ORDER = (2, 1, 3)
 BF = jnp.bfloat16
 F32 = jnp.float32
 US = 10**5
@@ -252,7 +253,25 @@
     return tuple(new)
 
 
-def diagonal_kernel(info, q_ref, k_ref, v_ref, best_ref, acc_ref):
+def earlier_kernel(info, q_ref, far, far_other, mine, other, best_ref, acc_ref, k_all, v_all):
+    y, x = info[YPOS], info[XLO]
+    place = (1 - x) * 4 + y
+    k_all[place], v_all[place] = split_pair(info, far[...], far_other[...])
+    for d in (1, 2, 3):
+        for plane, rows in ((x, slice(0, TOK)), (1 - x, slice(TOK, 2 * TOK))):
+            place = plane * 4 + lax.rem(y - d + 4, 4)
+            k_all[place], v_all[place] = split_pair(info, mine[d - 1, rows, :], other[d - 1, rows, :])
+    queries = pieces(q_ref)
+    start = (jnp.full((1, HALF), -1e30, F32), jnp.zeros((ACC, HALF), F32)) * len(UNITS)
+    state = lax.fori_loop(
+        0, info[SEQ], lambda j, state: add_block(queries, k_all[j], v_all[j], state), start
+    )
+    for u in range(len(UNITS)):
+        best_ref[u] = jnp.broadcast_to(state[2 * u], (8, HALF))
+        acc_ref[u] = state[2 * u + 1]
+
+
+def own_kernel(info, q_ref, k_ref, v_ref, best_ref, acc_ref, out_ref):
     limit = info[LENGTH] - info[SEQ] * TOK
     vt = with_ones([v_ref[i * HD : (i + 1) * HD, :] for i in range(TOK // HD)])
     queries = pieces(q_ref)
@@ -263,29 +282,11 @@
         t = i * HALF + lax.broadcasted_iota(jnp.int32, (wide, HALF), 1)
         keep = jnp.logical_and(s <= t, s < limit)
         scores = jnp.where(keep, scores, -jnp.inf)
-        best = jnp.max(scores, axis=0, keepdims=True)
-        weights = jnp.exp2((scores - best) * SCALE).astype(BF)
-        best_ref[u] = jnp.broadcast_to(best, (8, HALF))
-        acc_ref[u] = jnp.dot(vt[:, 0:wide], weights, preferred_element_type=F32)
-
-
-def earlier_kernel(info, q_ref, far, far_other, mine, other, best_ref, acc_ref, out_ref, k_all, v_all):
-    y, x = info[YPOS], info[XLO]
-    place = (1 - x) * 4 + y
-    k_all[place], v_all[place] = split_pair(info, far[...], far_other[...])
-    for d in (1, 2, 3):
-        for plane, rows in ((x, slice(0, TOK)), (1 - x, slice(TOK, 2 * TOK))):
-            place = plane * 4 + lax.rem(y - d + 4, 4)
-            k_all[place], v_all[place] = split_pair(info, mine[d - 1, rows, :], other[d - 1, rows, :])
-    queries = pieces(q_ref)
-    start = []
-    for u in range(len(UNITS)):
-        start += [best_ref[u, 0:1, :], acc_ref[u]]
-    state = lax.fori_loop(
-        0, info[SEQ], lambda j, state: add_block(queries, k_all[j], v_all[j], state), tuple(start)
-    )
-    for u, (h, i) in enumerate(UNITS):
-        summed = state[2 * u + 1]
+        best = best_ref[u, 0:1, :]
+        top = jnp.maximum(best, jnp.max(scores, axis=0, keepdims=True))
+        weights = jnp.exp2((scores - top) * SCALE).astype(BF)
+        shrink = jnp.exp2((best - top) * SCALE)
+        summed = acc_ref[u] * shrink + jnp.dot(vt[:, 0:wide], weights, preferred_element_type=F32)
         out = summed[0:HD] * (1.0 / summed[HD : HD + 1])
         out_ref[i * HALF : (i + 1) * HALF, h * HD : (h + 1) * HD] = out.T.astype(BF)
 
@@ -312,33 +313,39 @@
     return jnp.dot(g, w, preferred_element_type=F32)
 
 
-def first_kernel(info, *refs):
-    gated, weights, got, to_x, to_z, bundle = refs[0:4], refs[4], refs[5:8], refs[8], refs[9:12], refs[12]
-    for d in range(3):
-        bundle[d] = got[d][...]
+def first_x_kernel(info, *refs):
+    gated, weights, got, to_x, bundle = refs[0:4], refs[4], refs[5:8], refs[8], refs[9]
     for i in range(2):
         acc = product(gated, weights, 2 * i, 2).astype(BF)
         to_x[2 * i] = acc[:, 0:CB]
         to_x[2 * i + 1] = acc[:, CB : 2 * CB]
     for d in range(3):
-        acc = product(gated, weights, 4 + 2 * d, 2).astype(BF)
-        to_z[d][0] = acc[:, 0:CB]
-        to_z[d][1] = acc[:, CB : 2 * CB]
-
-
-def second_kernel(info, *refs):
-    gated, (weights, z1, z2, z3, x, to_x), to_z = refs[0:4], refs[4:10], refs[10:13]
-    acc = product(gated, weights, 10, 2)
-    total = acc[:, 0:CB]
+        bundle[d] = got[d][...]
+
+
+def first_z_kernel(info, *refs):
+    gated, weights, to_z = refs[0:4], refs[4], refs[5:8]
+    for out, d in zip(to_z, Z_ORDER):
+        acc = product(gated, weights, 2 + 2 * d, 2).astype(BF)
+        out[0] = acc[:, 0:CB]
+        out[1] = acc[:, CB : 2 * CB]
+
+
+def second_z_kernel(info, *refs):
+    gated, (weights, x), to_z = refs[0:4], refs[4:6], refs[6:9]
+    acc = product(gated, weights, 11, 3)
+    for out, d in zip(to_z, Z_ORDER):
+        part = acc[:, (d - 1) * CB : d * CB]
+        out[...] = (part + x[lax.rem(info[ZPOS] + d, 4)].astype(F32)).astype(BF)
+
+
+def second_x_kernel(info, *refs):
+    gated, (weights, z1, z2, z3), to_x = refs[0:4], refs[4:8], refs[8:10]
+    total = product(gated, weights, 10, 1)
     for r in (z1, z2, z3):
         total = total + r[1 - info[XHI]].astype(F32)
-    to_x[...] = total.astype(BF)
-    part = acc[:, CB : 2 * CB]
-    to_z[0][...] = (part + x[lax.rem(info[ZPOS] + 1, 4)].astype(F32)).astype(BF)
-    acc = product(gated, weights, 12, 2)
-    for d in (1, 2):
-        part = acc[:, (d - 1) * CB : d * CB]
-        to_z[d][...] = (part + x[lax.rem(info[ZPOS] + d + 1, 4)].astype(F32)).astype(BF)
+    for i in range(2):
+        to_x[i][...] = total[i * HALF : (i + 1) * HALF].astype(BF)
 
 
 def keep_kernel(info, *refs):
@@ -351,8 +358,10 @@
     out_ref[:, CB : 2 * CB] = acc[:, CB : 2 * CB] + x[info[ZPOS]].astype(F32)
 
 
-def finish_kernel(info, kept, x, z1, z2, z3, out_ref):
-    out_ref[:, 0:CB] = (kept[:, 0:CB] + x[...].astype(F32)).astype(BF)
+def finish_kernel(info, kept, x0, x1, z1, z2, z3, out_ref):
+    for i, x in enumerate((x0, x1)):
+        rows = slice(i * HALF, (i + 1) * HALF)
+        out_ref[rows, 0:CB] = (kept[rows, 0:CB] + x[...].astype(F32)).astype(BF)
     total = kept[:, CB : 2 * CB]
     for r in (z1, z2, z3):
         total = total + r[...].astype(F32)
@@ -416,7 +425,7 @@
         info,
         (keys, values, mixer_values, mixer_keys, step_size, decay_rate),
         [HBM, HBM, HBM, HBM, full((HEADS, TOK)), SMEM],
-        [full((TOK, HD))] * 3 + [full((MSG, HD)), full((16, TOK))] + [full((TOK, HD))] * 2,
+        [VMEM] * 7,
         [kept_shape((TOK, HD), BF)] * 3 + [kept_shape((MSG, HD), BF), kept_shape((16, TOK), F32)] + [kept_shape((TOK, HD), BF)] * 2,
         scratch=[pltpu.VMEM((TOK, HD), BF), pltpu.SemaphoreType.DMA((4,))],
         flops=US,
@@ -430,29 +439,20 @@
         intra_kernel,
         info,
         (cum, hbm(mixer_queries), mk, mv, skip_gain),
-        [full((16, TOK)), full((TOK, ROWS)), full((TOK, HD)), full((TOK, HD)), SMEM],
-        full((TOK, ROWS)),
+        [VMEM, full((TOK, ROWS)), VMEM, VMEM, SMEM],
+        VMEM,
         kept_shape((TOK, ROWS), F32),
-        flops=US,
-    )
-    best, acc = call(
-        diagonal_kernel,
-        info,
-        (hbm(queries), k_own, vt_own),
-        [full((TOK, ROWS)), full((TOK, HD)), full((TOK, HD))],
-        [full((8, 8, HALF)), full((8, ACC, HALF))],
-        [kept_shape((8, 8, HALF), F32), kept_shape((8, ACC, HALF), F32)],
         flops=US,
     )
     prefix, pdec, total, kv_pair = call(
         combine_kernel,
         info,
         (*msgs, kv, kv_far),
-        [full((MSG, HD))] * 4 + [full((TOK, HD))] * 2,
-        [full((ROWS, HD)), full((8, HD)), full((MSG, HD)), full((2 * TOK, HD))],
+        [VMEM] * 6,
+        [VMEM] * 4,
         [kept_shape((ROWS, HD), F32), kept_shape((8, HD), F32), kept_shape((MSG, HD), BF), kept_shape((2 * TOK, HD), BF)],
         flops=US,
-        after=(y_in, acc),
+        after=(y_in,),
     )
     total_far = lo(total)
     from_1, from_3, from_2 = [along_y(kv_pair, d) for d in (1, 3, 2)]
@@ -461,17 +461,8 @@
         gate_kernel,
         info,
         (cum, mixer_queries, y_in, gate_values, prefix, pdec, total, total_far),
-        [
-            full((16, TOK)),
-            full((TOK, ROWS)),
-            full((TOK, ROWS)),
-            full((TOK, ROWS)),
-            full((ROWS, HD)),
-            full((8, HD)),
-            full((MSG, HD)),
-            full((MSG, HD)),
-        ],
-        [full((TOK, 2 * HD))] * 2 + [full((HEADS, HD // 8, NST))],
+        [VMEM] * 8,
+        [VMEM] * 2 + [full((HEADS, HD // 8, NST))],
         [shape((TOK, 2 * HD), BF)] * 2 + [shape((HEADS, HD // 8, NST), F32)],
         flops=US,
     )
@@ -488,45 +479,63 @@
     )
     gated += [core(a) for a in gated]
 
-    to_x, *to_z, bundle = call(
-        first_kernel,
+    to_x, bundle = call(
+        first_x_kernel,
         info,
         (*gated, weights, *from_y),
         [VMEM] * 8,
+        [VMEM] * 2,
+        [shape((4, TOK, CB), BF), shape((3, 2 * TOK, HD), BF)],
+        flops=US,
+    )
+    from_x = lax.ppermute(to_x, "head", X_SWAP)
+    to_z = call(
+        first_z_kernel,
+        info,
+        (*gated, weights),
         [VMEM] * 5,
-        [shape((4, TOK, CB), BF)] + [shape((2, TOK, CB), BF)] * 3 + [shape((3, 2 * TOK, HD), BF)],
-        flops=US,
-    )
-    from_x = lax.ppermute(to_x, "head", X_SWAP)
-    from_1, from_3, from_2 = [along_z(to_z[d - 1], d) for d in (1, 3, 2)]
-    from_z = [from_1, from_2, from_3]
-
-    attended = call(
+        [VMEM] * 3,
+        [shape((2, TOK, CB), BF)] * 3,
+        flops=US,
+        after=(to_x,),
+    )
+    from_z = [along_z(a, d) for a, d in zip(to_z, Z_ORDER)]
+
+    best, acc = call(
         earlier_kernel,
         info,
-        (queries, kv_far, kv_far_other, bundle, core(bundle), best, acc),
-        [full((TOK, ROWS))] + [full((TOK, HD))] * 2 + [full((3, 2 * TOK, HD))] * 2 + [full((8, 8, HALF)), full((8, ACC, HALF))],
-        full((TOK, ROWS)),
-        shape((TOK, ROWS), BF),
+        (queries, kv_far, kv_far_other, bundle, core(bundle)),
+        [VMEM] * 5,
+        [VMEM] * 2,
+        [kept_shape((8, 8, HALF), F32), kept_shape((8, ACC, HALF), F32)],
         scratch=[pltpu.VMEM((8, TOK, HD), BF)] * 2,
         flops=US,
         limit=28 * 1024 * 1024,
         after=(to_z[0],),
     )
 
-    to_x2, *to_z2 = call(
-        second_kernel,
-        info,
-        (*gated, weights, *from_z, from_x),
-        [VMEM] * 9,
-        [VMEM] * 4,
-        [shape((TOK, CB), BF)] * 4,
-        flops=US,
-        after=(hbm(attended),),
-    )
-    from_1, from_3, from_2 = [along_z(to_z2[d - 1], d) for d in (1, 3, 2)]
-    from_z2 = [from_1, from_2, from_3]
-    from_x2 = lax.ppermute(to_x2, "head", X_SWAP)
+    to_z2 = call(
+        second_z_kernel,
+        info,
+        (*gated, weights, from_x),
+        [VMEM] * 6,
+        [VMEM] * 3,
+        [shape((TOK, CB), BF)] * 3,
+        flops=US,
+        after=(best,),
+    )
+    from_z2 = [along_z(a, d) for a, d in zip(to_z2, Z_ORDER)]
+    to_x2 = call(
+        second_x_kernel,
+        info,
+        (*gated, weights, *from_z),
+        [VMEM] * 8,
+        [VMEM] * 2,
+        [shape((HALF, CB), BF)] * 2,
+        flops=US,
+        after=(to_z2[0],),
+    )
+    from_x2 = [lax.ppermute(a, "head", X_SWAP) for a in to_x2]
     kept = call(
         keep_kernel,
         info,
@@ -535,16 +544,27 @@
         VMEM,
         shape((TOK, ROWS), F32),
         flops=US,
-        after=(to_x2,),
+        after=(to_x2[0],),
+    )
+    attended = call(
+        own_kernel,
+        info,
+        (queries, k_own, vt_own, best, acc),
+        [VMEM] * 5,
+        full((TOK, ROWS)),
+        shape((TOK, ROWS), BF),
+        flops=US,
+        after=(kept,),
     )
     summed = call(
         finish_kernel,
         info,
-        (kept, from_x2, *from_z2),
-        [full((TOK, ROWS))] + [full((TOK, CB))] * 4,
+        (kept, *from_x2, *from_z2),
+        [VMEM] * 6,
         full((TOK, ROWS)),
         shape((TOK, ROWS), BF),
         flops=US,
+        after=(hbm(attended),),
     )
     return (attended, summed, final_states)
 

time: 90.1 us -> 82 us (0.910)
  waiting for transfers between devices: 33.1 us -> 16.4 us
  starting transfers between devices: 27.6 us -> 35.6 us
    ppermute x6, waiting for transfers between devices: 26.6 us -> 0.14 us  [body(): along_z = lambda a, d: lax.ppermute(a, 'head', Z_MOVE[d])]
    ppermute x1, waiting for transfers between devices: 0.01 us -> 11.6 us  [body(): from_x = lax.ppermute(to_x, 'head', X_SWAP)]
    ppermute x1 -> x2, starting transfers between devices: 0.59 us -> 3.61 us  [body(): from_x2 = [lax.ppermute(a, 'head', X_SWAP) for a in to_x2]]
    ppermute x6, starting transfers between devices: 11.4 us -> 14.4 us  [body(): along_z = lambda a, d: lax.ppermute(a, 'head', Z_MOVE[d])]
    ppermute x1 -> x2, waiting for transfers between devices: 2.24 us -> 0.65 us  [body(): from_x2 = [lax.ppermute(a, 'head', X_SWAP) for a in to_x2]]
    ppermute x6, starting transfers between devices: 9.33 us -> 10.6 us  [body(): along_y = lambda a, d: lax.ppermute(a, 'seq', Y_MOVE[d])]
    ppermute x2, waiting for transfers between devices: 1.17 us -> 0.18 us  [body(): lo = lambda a: lax.ppermute(a, 'seq', LO_SWAP)]
    ppermute x2, starting transfers between devices: 2.1 us -> 3.06 us  [body(): lo = lambda a: lax.ppermute(a, 'seq', LO_SWAP)]
  transfers between devices with their start and end apart: 21 -> 22, of which waited for: 7 -> 7; matrix products, arithmetic and copies ran while one was open for 0% -> 0% of each run, Pallas kernels for 23% -> 30%
where the time goes in v4:
time: 82 us; the launch traced here: 81.7 us
  starting transfers between devices  35.6 us (43%)
  Pallas kernels  27.9 us (34%)
  waiting for transfers between devices  16.4 us (20%)
  between operations  1.63 us (2%)
    pallas_call x13, Pallas kernels, call(): pl.pallas_call(run, grid_spec=spec, out_shape=out_shape, input_output_ali...  27.9 us
    ppermute x6, starting transfers between devices, body(): along_z = lambda a, d: lax.ppermute(a, 'head', Z_MOVE[d])  14.4 us
    ppermute x1, waiting for transfers between devices, body(): from_x = lax.ppermute(to_x, 'head', X_SWAP)  11.6 us
    ppermute x6, starting transfers between devices, body(): along_y = lambda a, d: lax.ppermute(a, 'seq', Y_MOVE[d])  10.6 us
    ppermute x6, waiting for transfers between devices, body(): along_y = lambda a, d: lax.ppermute(a, 'seq', Y_MOVE[d])  3.8 us
    ppermute x2, starting transfers between devices, body(): from_x2 = [lax.ppermute(a, 'head', X_SWAP) for a in to_x2]  3.61 us
    ppermute x2, starting transfers between devices, body(): lo = lambda a: lax.ppermute(a, 'seq', LO_SWAP)  3.06 us
    ppermute x1, starting transfers between devices, body(): from_x = lax.ppermute(to_x, 'head', X_SWAP)  2.82 us
  transfers between devices with their start and end apart: 22, of which 7 were waited for; matrix products, arithmetic and copies ran while one was open for 0% of the time, Pallas kernels for 30%

profile of v4, /device:TPU:0, one launch (start us, length us, event | category | flops | bytes accessed | tf_op | source)
XLA Modules:
  0.0 81.7 jit_solution(11128396211377053542)
XLA Ops:
  0.6 0.0 copy-start
  0.6 0.0 copy-start.2
  0.7 0.1 collective-permute-start.8
  1.6 0.1 stack.95.refs_0_
  1.7 3.3 %shard_map.139 = (bf16[512,128]{1,0:T(8,128)(2,1)S(1)}, bf16[512,128]{1,0:T(8,128)(2,1)S(1)}, bf16[512,128]{1,0:T(8,128)(2,1)S(1)}, bf16[544,128]{1,0:T(8,128)(2...) custom-call(s32[24]{0:T(128)S(1)} %stack.95.refs_0_, ...), custom_call_target="tpu_custom_call" | custom-call | flops 100000 | tf_op jit(solution)/shard_map/pallas_call | solution.py:45
  5.1 1.7 %collective-permute-start.2 = (bf16[544,128]{1,0:T(8,128)(2,1)S(1)}, bf16[544,128]{1,0:T(8,128)(2,1)S(1)}, u32[]{:S(2)}, u32[]{:S(2)}) collective-permute-start(bf16[544,128]{1,0:T(8,128)(2,1)S(1)} %get-tuple-element.35.refs_1_), channel_id=1, source_target_pairs={{0,16},{16,32},{32,48},{48,0},{64,80},{80,96},{96,112},{112,64},{1... | collective-permute-start | bytes 417800 | tf_op jit(solution)/shard_map/ppermute | solution.py:416
  6.8 2.9 %collective-permute-start.3 = (bf16[544,128]{1,0:T(8,128)(2,1)S(1)}, bf16[544,128]{1,0:T(8,128)(2,1)S(1)}, u32[]{:S(2)}, u32[]{:S(2)}) collective-permute-start(bf16[544,128]{1,0:T(8,128)(2,1)S(1)} %get-tuple-element.35.refs_1_), channel_id=1, source_target_pairs={{0,32},{16,48},{32,0},{48,16},{64,96},{80,112},{96,64},{112,80},{1... | collective-permute-start | bytes 417800 | tf_op jit(solution)/shard_map/ppermute | solution.py:416
  9.7 1.3 %collective-permute-start.4 = (bf16[544,128]{1,0:T(8,128)(2,1)S(1)}, bf16[544,128]{1,0:T(8,128)(2,1)S(1)}, u32[]{:S(2)}, u32[]{:S(2)}) collective-permute-start(bf16[544,128]{1,0:T(8,128)(2,1)S(1)} %get-tuple-element.35.refs_1_), channel_id=1, source_target_pairs={{0,48},{16,0},{32,16},{48,32},{64,112},{80,64},{96,80},{112,96},{1... | collective-permute-start | bytes 417800 | tf_op jit(solution)/shard_map/ppermute | solution.py:416
  11.0 1.5 %collective-permute-start = (bf16[512,128]{1,0:T(8,128)(2,1)S(1)}, bf16[512,128]{1,0:T(8,128)(2,1)S(1)}, u32[]{:S(2)}, u32[]{:S(2)}) collective-permute-start(bf16[512,128]{1,0:T(8,128)(2,1)S(1)} %get-tuple-element.31.refs_5_), channel_id=1, source_target_pairs={{0,64},{16,80},{32,96},{48,112},{64,0},{80,16},{96,32},{112,48},{1... | collective-permute-start | bytes 393224 | tf_op jit(solution)/shard_map/ppermute | solution.py:415
  12.5 3.3 %shard_map.140.refs_7_.refs_3_ = f32[512,512]{1,0:T(8,128)S(1)} custom-call(s32[24]{0:T(128)S(1)} %stack.95.refs_0_, f32[16,512]{1,0:T(8,128)S(1)} %get-tuple-element.32.refs_1_, bf16[512,512]{1,0:T(8,128)(2,1)} %refs_2_.5, bf16[512,128]{1,0:T(8,128)(2,1)S(1)} %get-tuple-element.33.refs_3_, bf16[512,128]{1,0:T(8,128)(2,1)S(1)} %get-tuple-element.34.refs_4_, ...), custom_call_target="tpu_custom_call" | custom-call | flops 100000 | tf_op jit(solution)/shard_map/pallas_call | solution.py:45
  15.8 0.2 collective-permute-done.refs_6_.refs_2_
  16.0 0.0 collective-permute-done.2.refs_2_
  16.0 0.5 collective-permute-done.3.refs_3_
  16.5 0.0 collective-permute-done.4.refs_4_
  16.5 0.7 shard_map.141
  17.3 1.6 %collective-permute-start.5 = (bf16[544,128]{1,0:T(8,128)(2,1)S(1)}, bf16[544,128]{1,0:T(8,128)(2,1)S(1)}, u32[]{:S(2)}, u32[]{:S(2)}) collective-permute-start(bf16[544,128]{1,0:T(8,128)(2,1)S(1)} %get-tuple-element.38.refs_7_), channel_id=1, source_target_pairs={{0,64},{16,80},{32,96},{48,112},{64,0},{80,16},{96,32},{112,48},{1... | collective-permute-start | bytes 417800 | tf_op jit(solution)/shard_map/ppermute | solution.py:415
  18.8 2.6 %collective-permute-start.10 = (bf16[1024,128]{1,0:T(8,128)(2,1)S(1)}, bf16[1024,128]{1,0:T(8,128)(2,1)S(1)}, u32[]{:S(2)}, u32[]{:S(2)}) collective-permute-start(bf16[1024,128]{1,0:T(8,128)(2,1)S(1)} %get-tuple-element.41), channel_id=1, source_target_pairs={{0,32},{16,48},{32,0},{48,16},{64,96},{80,112},{96,64},{112,80},{1... | collective-permute-start | bytes 786440 | tf_op jit(solution)/shard_map/ppermute | solution.py:416
  21.4 1.3 %collective-permute-start.11 = (bf16[1024,128]{1,0:T(8,128)(2,1)S(1)}, bf16[1024,128]{1,0:T(8,128)(2,1)S(1)}, u32[]{:S(2)}, u32[]{:S(2)}) collective-permute-start(bf16[1024,128]{1,0:T(8,128)(2,1)S(1)} %get-tuple-element.41), channel_id=1, source_target_pairs={{0,48},{16,0},{32,16},{48,32},{64,112},{80,64},{96,80},{112,96},{1... | collective-permute-start | bytes 786440 | tf_op jit(solution)/shard_map/ppermute | solution.py:416
  22.8 0.7 collective-permute-start.9
  23.4 0.0 collective-permute-done.5.refs_8_
  23.5 0.0 copy-done
  23.5 0.0 copy-done.2
  23.5 1.8 %shard_map.142 = (bf16[512,256]{1,0:T(8,128)(2,1)S(1)}, bf16[512,256]{1,0:T(8,128)(2,1)S(1)}, f32[4,16,128]{2,1,0:T(8,128)}) custom-call(s32[24]{0:T(128)S(1)} %stack.95.refs_0_, f32[16,512]{1,0:T(8,128)S(1)} %get-tuple-element.32.refs_1_, bf16[512,512]{1,0:T(8,128)(2,1)S(1)} %copy-done, f32[512,512]{1,0:T(8,128)S(1)} %shard_map.140.refs_7_.refs_3_, ...), custom_call_target="tpu_custom_call" | custom-call | flops 100000 | tf_op jit(solution)/shard_map/pallas_call | solution.py:45
  25.2 0.0 collective-permute-start.6
  25.2 0.0 collective-permute-done.8.refs_2_
  25.3 0.5 collective-permute-start.7
  25.8 4.3 %shard_map.143.refs_5_ = bf16[16,1024,256]{2,1,0:T(8,128)(2,1)S(1)} custom-call(s32[24]{0:T(128)S(1)} %stack.95.refs_0_, bf16[512,8192]{1,0:T(8,128)(2,1)} %refs_1_.5, bf16[512,8192]{1,0:T(8,128)(2,1)} %collective-permute-done.8.refs_2_, bf16[512,256]{1,0:T(8,128)(2,1)S(1)} %get-tuple-element.39.refs_3_.refs_1_), custom_call_target="tpu_custom_call" | custom-call | flops 10000000000 | tf_op jit(solution)/shard_map/pallas_call | solution.py:45
  30.1 0.0 copy-start.1
  30.1 0.0 collective-permute-done.10.refs_7_
  30.1 3.0 %collective-permute-done.11.refs_8_ = bf16[1024,128]{1,0:T(8,128)(2,1)S(1)} collective-permute-done((bf16[1024,128]{1,0:T(8,128)(2,1)S(1)}, bf16[1024,128]{1,0:T(8,128)(2,1)S(1)}, u32[]{:S(2)}, u32[]{:S(2)}) %collective-permute-start.11) | collective-permute-done | bytes 262176 | tf_op jit(solution)/shard_map/ppermute | solution.py:416
  33.1 0.3 collective-permute-done.9.refs_6_
  33.4 0.0 collective-permute-done.6.refs_3_
  33.4 0.0 collective-permute-done.7.refs_4_
  33.4 1.8 %shard_map.144 = (bf16[4,512,256]{2,1,0:T(8,128)(2,1)S(1)}, bf16[3,1024,128]{2,1,0:T(8,128)(2,1)S(1)}) custom-call(s32[24]{0:T(128)S(1)} %stack.95.refs_0_, bf16[512,256]{1,0:T(8,128)(2,1)S(1)} %get-tuple-element.39.refs_3_.refs_1_, bf16[512,256]{1,0:T(8,128)(2,1)S(1)} %get-tuple-element.40.refs_2_, bf16[512,256]{1,0:T(8,128)(2,1)S(1)} %collective-permute-done.6.refs_3_, ...), custom_call_target="tpu_custom_call" | custom-call | flops 100000 | tf_op jit(solution)/shard_map/pallas_call | solution.py:45
  35.2 2.8 %collective-permute-start.16 = (bf16[4,512,256]{2,1,0:T(8,128)(2,1)S(1)}, bf16[4,512,256]{2,1,0:T(8,128)(2,1)S(1)}, u32[]{:S(2)}, u32[]{:S(2)}) collective-permute-start(bf16[4,512,256]{2,1,0:T(8,128)(2,1)S(1)} %get-tuple-element.43.refs_6_), channel_id=1, source_target_pairs={{0,2},{1,3},{2,0},{3,1},{4,6},{5,7},{6,4},{7,5},{8,10},{9,11},{10,... | collective-permute-start | bytes 3145736 | tf_op jit(solution)/shard_map/ppermute | solution.py:491
  38.0 0.0 collective-permute-start.12
  38.0 0.5 collective-permute-start.1
  38.5 2.3 %shard_map.145 = (bf16[2,512,256]{2,1,0:T(8,128)(2,1)S(1)}, bf16[2,512,256]{2,1,0:T(8,128)(2,1)S(1)}, bf16[2,512,256]{2,1,0:T(8,128)(2,1)S(1)}) custom-call(s32[24]{0:T(128)S(1)} %stack.95.refs_0_, bf16[512,256]{1,0:T(8,128)(2,1)S(1)} %get-tuple-element.39.refs_3_.refs_1_, bf16[512,256]{1,0:T(8,128)(2,1)S(1)} %get-tuple-element.40.refs_2_, ...), custom_call_target="tpu_custom_call" | custom-call | flops 100000 | tf_op jit(solution)/shard_map/pallas_call | solution.py:45
  40.9 3.9 %collective-permute-start.13 = (bf16[2,512,256]{2,1,0:T(8,128)(2,1)S(1)}, bf16[2,512,256]{2,1,0:T(8,128)(2,1)S(1)}, u32[]{:S(2)}, u32[]{:S(2)}) collective-permute-start(bf16[2,512,256]{2,1,0:T(8,128)(2,1)S(1)} %get-tuple-element.44.refs_6_), channel_id=1, source_target_pairs={{0,8},{1,9},{2,10},{3,11},{4,12},{5,13},{6,14},{7,15},{8,0},{9,1},... | collective-permute-start | bytes 1572872 | tf_op jit(solution)/shard_map/ppermute | solution.py:417
  44.8 1.0 %collective-permute-start.14 = (bf16[2,512,256]{2,1,0:T(8,128)(2,1)S(1)}, bf16[2,512,256]{2,1,0:T(8,128)(2,1)S(1)}, u32[]{:S(2)}, u32[]{:S(2)}) collective-permute-start(bf16[2,512,256]{2,1,0:T(8,128)(2,1)S(1)} %get-tuple-element.47), channel_id=1, source_target_pairs={{0,4},{1,5},{2,6},{3,7},{4,8},{5,9},{6,10},{7,11},{8,12},{9,13},{1... | collective-permute-start | bytes 1572872 | tf_op jit(solution)/shard_map/ppermute | solution.py:417
  45.8 0.0 collective-permute-done.1.refs_3_
  45.8 2.2 %collective-permute-start.15 = (bf16[2,512,256]{2,1,0:T(8,128)(2,1)S(1)}, bf16[2,512,256]{2,1,0:T(8,128)(2,1)S(1)}, u32[]{:S(2)}, u32[]{:S(2)}) collective-permute-start(bf16[2,512,256]{2,1,0:T(8,128)(2,1)S(1)} %get-tuple-element.48), channel_id=1, source_target_pairs={{0,12},{1,13},{2,14},{3,15},{4,0},{5,1},{6,2},{7,3},{8,4},{9,5},{1... | collective-permute-start | bytes 1572872 | tf_op jit(solution)/shard_map/ppermute | solution.py:417
  48.0 0.0 collective-permute-done.12.refs_5_
  48.0 0.0 copy-done.1
  48.0 1.4 %shard_map.146 = (f32[8,8,256]{2,1,0:T(8,128)S(1)}, f32[8,144,256]{2,1,0:T(8,128)S(1)}) custom-call(s32[24]{0:T(128)S(1)} %stack.95.refs_0_, bf16[512,512]{1,0:T(8,128)(2,1)S(1)} %copy-done.1, bf16[512,128]{1,0:T(8,128)(2,1)S(1)} %collective-permute-done.refs_6_.refs_2_, bf16[512,128]{1,0:T(8,128)(2,1)S(1)} %collective-permute-done.1.refs_3_, ...), custom_call_target="tpu_custom_call" | custom-call | flops 100000 | tf_op jit(solution)/shard_map/pallas_call | solution.py:45
  49.5 11.6 %collective-permute-done.16.refs_6_.refs_9_ = bf16[4,512,256]{2,1,0:T(8,128)(2,1)S(1)} collective-permute-done((bf16[4,512,256]{2,1,0:T(8,128)(2,1)S(1)}, bf16[4,512,256]{2,1,0:T(8,128)(2,1)S(1)}, u32[]{:S(2)}, u32[]{:S(2)}) %collective-permute-start.16) | collective-permute-done | bytes 1048608 | tf_op jit(solution)/shard_map/ppermute | solution.py:491
  61.1 1.5 %shard_map.147 = (bf16[512,256]{1,0:T(8,128)(2,1)S(1)}, bf16[512,256]{1,0:T(8,128)(2,1)S(1)}, bf16[512,256]{1,0:T(8,128)(2,1)S(1)}) custom-call(s32[24]{0:T(128)S(1)} %stack.95.refs_0_, bf16[512,256]{1,0:T(8,128)(2,1)S(1)} %get-tuple-element.39.refs_3_.refs_1_, bf16[512,256]{1,0:T(8,128)(2,1)S(1)} %get-tuple-element.40.refs_2_, ...), custom_call_target="tpu_custom_call" | custom-call | flops 100000 | tf_op jit(solution)/shard_map/pallas_call | solution.py:45
  62.6 4.0 %collective-permute-start.19 = (bf16[512,256]{1,0:T(8,128)(2,1)S(1)}, bf16[512,256]{1,0:T(8,128)(2,1)S(1)}, u32[]{:S(2)}, u32[]{:S(2)}) collective-permute-start(bf16[512,256]{1,0:T(8,128)(2,1)S(1)} %get-tuple-element.49.refs_9_), channel_id=1, source_target_pairs={{0,8},{1,9},{2,10},{3,11},{4,12},{5,13},{6,14},{7,15},{8,0},{9,1},... | collective-permute-start | bytes 786440 | tf_op jit(solution)/shard_map/ppermute | solution.py:417
  66.6 1.0 %collective-permute-start.20 = (bf16[512,256]{1,0:T(8,128)(2,1)S(1)}, bf16[512,256]{1,0:T(8,128)(2,1)S(1)}, u32[]{:S(2)}, u32[]{:S(2)}) collective-permute-start(bf16[512,256]{1,0:T(8,128)(2,1)S(1)} %get-tuple-element.52), channel_id=1, source_target_pairs={{0,4},{1,5},{2,6},{3,7},{4,8},{5,9},{6,10},{7,11},{8,12},{9,13},{1... | collective-permute-start | bytes 786440 | tf_op jit(solution)/shard_map/ppermute | solution.py:417
  67.6 0.0 collective-permute-done.13.refs_6_
  67.6 2.2 %collective-permute-start.21 = (bf16[512,256]{1,0:T(8,128)(2,1)S(1)}, bf16[512,256]{1,0:T(8,128)(2,1)S(1)}, u32[]{:S(2)}, u32[]{:S(2)}) collective-permute-start(bf16[512,256]{1,0:T(8,128)(2,1)S(1)} %get-tuple-element.53), channel_id=1, source_target_pairs={{0,12},{1,13},{2,14},{3,15},{4,0},{5,1},{6,2},{7,3},{8,4},{9,5},{1... | collective-permute-start | bytes 786440 | tf_op jit(solution)/shard_map/ppermute | solution.py:417
  69.8 0.0 collective-permute-done.14.refs_7_
  69.8 0.0 collective-permute-done.15.refs_8_
  69.9 1.0 %shard_map.148 = (bf16[256,256]{1,0:T(8,128)(2,1)S(1)}, bf16[256,256]{1,0:T(8,128)(2,1)S(1)}) custom-call(s32[24]{0:T(128)S(1)} %stack.95.refs_0_, bf16[512,256]{1,0:T(8,128)(2,1)S(1)} %get-tuple-element.39.refs_3_.refs_1_, bf16[512,256]{1,0:T(8,128)(2,1)S(1)} %get-tuple-element.40.refs_2_, bf16[512,256]{1,0:T(8,128)(2,1)S(1)} %collective-permute-done.6.refs_3_, ...), custom_call_target="tpu_custom_call" | custom-call | flops 100000 | tf_op jit(solution)/shard_map/pallas_call | solution.py:45
  70.9 2.8 %collective-permute-start.17 = (bf16[256,256]{1,0:T(8,128)(2,1)S(1)}, bf16[256,256]{1,0:T(8,128)(2,1)S(1)}, u32[]{:S(2)}, u32[]{:S(2)}) collective-permute-start(bf16[256,256]{1,0:T(8,128)(2,1)S(1)} %get-tuple-element.50.refs_10_), channel_id=1, source_target_pairs={{0,2},{1,3},{2,0},{3,1},{4,6},{5,7},{6,4},{7,5},{8,10},{9,11},{10,... | collective-permute-start | bytes 393224 | tf_op jit(solution)/shard_map/ppermute | solution.py:538
  73.6 0.8 %collective-permute-start.18 = (bf16[256,256]{1,0:T(8,128)(2,1)S(1)}, bf16[256,256]{1,0:T(8,128)(2,1)S(1)}, u32[]{:S(2)}, u32[]{:S(2)}) collective-permute-start(bf16[256,256]{1,0:T(8,128)(2,1)S(1)} %get-tuple-element.51), channel_id=1, source_target_pairs={{0,2},{1,3},{2,0},{3,1},{4,6},{5,7},{6,4},{7,5},{8,10},{9,11},{10,... | collective-permute-start | bytes 393224 | tf_op jit(solution)/shard_map/ppermute | solution.py:538
  74.5 1.2 %shard_map.149.refs_6_.refs_1_ = f32[512,512]{1,0:T(8,128)S(1)} custom-call(s32[24]{0:T(128)S(1)} %stack.95.refs_0_, bf16[512,256]{1,0:T(8,128)(2,1)S(1)} %get-tuple-element.39.refs_3_.refs_1_, bf16[512,256]{1,0:T(8,128)(2,1)S(1)} %get-tuple-element.40.refs_2_, bf16[512,256]{1,0:T(8,128)(2,1)S(1)} %collective-permute-done.6.refs_3_, ...), custom_call_target="tpu_custom_call" | custom-call | flops 100000 | tf_op jit(solution)/shard_map/pallas_call | solution.py:45
  75.7 3.7 %shard_map.150.refs_7_ = bf16[512,512]{1,0:T(8,128)(2,1)} custom-call(s32[24]{0:T(128)S(1)} %stack.95.refs_0_, bf16[512,512]{1,0:T(8,128)(2,1)S(1)} %copy-done.1, bf16[512,128]{1,0:T(8,128)(2,1)S(1)} %get-tuple-element.29.refs_2_, bf16[512,128]{1,0:T(8,128)(2,1)S(1)} %get-tuple-element.30.refs_3_, f32[8,8,256]{2,1,0:T(8,128)S(1)} %get-tuple-element.45.refs_7_.refs_4_, ...), custom_call_target="tpu_custom_call" | custom-call | flops 100000 | tf_op jit(solution)/shard_map/pallas_call | solution.py:45
  79.4 0.0 collective-permute-done.17.refs_2_
  79.4 0.6 collective-permute-done.18.refs_3_
  80.1 0.0 collective-permute-done.19.refs_4_
  80.1 0.0 collective-permute-done.20.refs_5_
  80.1 0.1 collective-permute-done.21.refs_6_
  80.2 1.5 %shard_map.151 = bf16[512,512]{1,0:T(8,128)(2,1)} custom-call(s32[24]{0:T(128)S(1)} %stack.95.refs_0_, f32[512,512]{1,0:T(8,128)S(1)} %shard_map.149.refs_6_.refs_1_, bf16[256,256]{1,0:T(8,128)(2,1)S(1)} %collective-permute-done.17.refs_2_, bf16[256,256]{1,0:T(8,128)(2,1)S(1)} %collective-permute-done.18.refs_3_, ...), custom_call_target="tpu_custom_call" | custom-call | flops 100000 | tf_op jit(solution)/shard_map/pallas_call | solution.py:45
Async XLA Ops:
  0.6 22.8 %copy-start = (bf16[512,512]{1,0:T(8,128)(2,1)S(1)}, bf16[512,512]{1,0:T(8,128)(2,1)}, u32[]{:S(2)}) copy-start(bf16[512,512]{1,0:T(8,128)(2,1)} %refs_2_.5) | copy-start | bytes 1572868
  0.6 22.8 %copy-start.2 = (bf16[512,512]{1,0:T(8,128)(2,1)S(1)}, bf16[512,512]{1,0:T(8,128)(2,1)}, u32[]{:S(2)}) copy-start(bf16[512,512]{1,0:T(8,128)(2,1)} %refs_4_.3) | copy-start | bytes 1572868
  0.7 24.6 %collective-permute-start.8 = (bf16[512,8192]{1,0:T(8,128)(2,1)}, bf16[512,8192]{1,0:T(8,128)(2,1)}, u32[]{:S(2)}, u32[]{:S(2)}) collective-permute-start(bf16[512,8192]{1,0:T(8,128)(2,1)} %refs_1_.5), channel_id=1, source_target_pairs={{0,1},{1,0},{2,3},{3,2},{4,5},{5,4},{6,7},{7,6},{8,9},{9,8},{10,11... | collective-permute-start | bytes 25165832 | tf_op jit(solution)/shard_map/ppermute | solution.py:414
  5.1 11.0 %collective-permute-start.2 = (bf16[544,128]{1,0:T(8,128)(2,1)S(1)}, bf16[544,128]{1,0:T(8,128)(2,1)S(1)}, u32[]{:S(2)}, u32[]{:S(2)}) collective-permute-start(bf16[544,128]{1,0:T(8,128)(2,1)S(1)} %get-tuple-element.35.refs_1_), channel_id=1, source_target_pairs={{0,16},{16,32},{32,48},{48,0},{64,80},{80,96},{96,112},{112,64},{1... | collective-permute-start | bytes 417800 | tf_op jit(solution)/shard_map/ppermute | solution.py:416
  6.8 9.7 %collective-permute-start.3 = (bf16[544,128]{1,0:T(8,128)(2,1)S(1)}, bf16[544,128]{1,0:T(8,128)(2,1)S(1)}, u32[]{:S(2)}, u32[]{:S(2)}) collective-permute-start(bf16[544,128]{1,0:T(8,128)(2,1)S(1)} %get-tuple-element.35.refs_1_), channel_id=1, source_target_pairs={{0,32},{16,48},{32,0},{48,16},{64,96},{80,112},{96,64},{112,80},{1... | collective-permute-start | bytes 417800 | tf_op jit(solution)/shard_map/ppermute | solution.py:416
  9.7 6.8 %collective-permute-start.4 = (bf16[544,128]{1,0:T(8,128)(2,1)S(1)}, bf16[544,128]{1,0:T(8,128)(2,1)S(1)}, u32[]{:S(2)}, u32[]{:S(2)}) collective-permute-start(bf16[544,128]{1,0:T(8,128)(2,1)S(1)} %get-tuple-element.35.refs_1_), channel_id=1, source_target_pairs={{0,48},{16,0},{32,16},{48,32},{64,112},{80,64},{96,80},{112,96},{1... | collective-permute-start | bytes 417800 | tf_op jit(solution)/shard_map/ppermute | solution.py:416
  11.0 5.0 %collective-permute-start = (bf16[512,128]{1,0:T(8,128)(2,1)S(1)}, bf16[512,128]{1,0:T(8,128)(2,1)S(1)}, u32[]{:S(2)}, u32[]{:S(2)}) collective-permute-start(bf16[512,128]{1,0:T(8,128)(2,1)S(1)} %get-tuple-element.31.refs_5_), channel_id=1, source_target_pairs={{0,64},{16,80},{32,96},{48,112},{64,0},{80,16},{96,32},{112,48},{1... | collective-permute-start | bytes 393224 | tf_op jit(solution)/shard_map/ppermute | solution.py:415
  17.3 6.2 %collective-permute-start.5 = (bf16[544,128]{1,0:T(8,128)(2,1)S(1)}, bf16[544,128]{1,0:T(8,128)(2,1)S(1)}, u32[]{:S(2)}, u32[]{:S(2)}) collective-permute-start(bf16[544,128]{1,0:T(8,128)(2,1)S(1)} %get-tuple-element.38.refs_7_), channel_id=1, source_target_pairs={{0,64},{16,80},{32,96},{48,112},{64,0},{80,16},{96,32},{112,48},{1... | collective-permute-start | bytes 417800 | tf_op jit(solution)/shard_map/ppermute | solution.py:415
  18.8 11.2 %collective-permute-start.10 = (bf16[1024,128]{1,0:T(8,128)(2,1)S(1)}, bf16[1024,128]{1,0:T(8,128)(2,1)S(1)}, u32[]{:S(2)}, u32[]{:S(2)}) collective-permute-start(bf16[1024,128]{1,0:T(8,128)(2,1)S(1)} %get-tuple-element.41), channel_id=1, source_target_pairs={{0,32},{16,48},{32,0},{48,16},{64,96},{80,112},{96,64},{112,80},{1... | collective-permute-start | bytes 786440 | tf_op jit(solution)/shard_map/ppermute | solution.py:416
  21.4 11.6 %collective-permute-start.11 = (bf16[1024,128]{1,0:T(8,128)(2,1)S(1)}, bf16[1024,128]{1,0:T(8,128)(2,1)S(1)}, u32[]{:S(2)}, u32[]{:S(2)}) collective-permute-start(bf16[1024,128]{1,0:T(8,128)(2,1)S(1)} %get-tuple-element.41), channel_id=1, source_target_pairs={{0,48},{16,0},{32,16},{48,32},{64,112},{80,64},{96,80},{112,96},{1... | collective-permute-start | bytes 786440 | tf_op jit(solution)/shard_map/ppermute | solution.py:416
  22.8 10.6 %collective-permute-start.9 = (bf16[1024,128]{1,0:T(8,128)(2,1)S(1)}, bf16[1024,128]{1,0:T(8,128)(2,1)S(1)}, u32[]{:S(2)}, u32[]{:S(2)}) collective-permute-start(bf16[1024,128]{1,0:T(8,128)(2,1)S(1)} %get-tuple-element.41), channel_id=1, source_target_pairs={{0,16},{16,32},{32,48},{48,0},{64,80},{80,96},{96,112},{112,64},{1... | collective-permute-start | bytes 786440 | tf_op jit(solution)/shard_map/ppermute | solution.py:416
  25.2 8.1 %collective-permute-start.6 = (bf16[512,256]{1,0:T(8,128)(2,1)S(1)}, bf16[512,256]{1,0:T(8,128)(2,1)S(1)}, u32[]{:S(2)}, u32[]{:S(2)}) collective-permute-start(bf16[512,256]{1,0:T(8,128)(2,1)S(1)} %get-tuple-element.39.refs_3_.refs_1_), channel_id=1, source_target_pairs={{0,1},{1,0},{2,3},{3,2},{4,5},{5,4},{6,7},{7,6},{8,9},{9,8},{10,11... | collective-permute-start | bytes 786440 | tf_op jit(solution)/shard_map/ppermute | solution.py:414
  25.3 8.1 %collective-permute-start.7 = (bf16[512,256]{1,0:T(8,128)(2,1)S(1)}, bf16[512,256]{1,0:T(8,128)(2,1)S(1)}, u32[]{:S(2)}, u32[]{:S(2)}) collective-permute-start(bf16[512,256]{1,0:T(8,128)(2,1)S(1)} %get-tuple-element.40.refs_2_), channel_id=1, source_target_pairs={{0,1},{1,0},{2,3},{3,2},{4,5},{5,4},{6,7},{7,6},{8,9},{9,8},{10,11... | collective-permute-start | bytes 786440 | tf_op jit(solution)/shard_map/ppermute | solution.py:414
  30.1 18.0 %copy-start.1 = (bf16[512,512]{1,0:T(8,128)(2,1)S(1)}, bf16[512,512]{1,0:T(8,128)(2,1)}, u32[]{:S(2)}) copy-start(bf16[512,512]{1,0:T(8,128)(2,1)} %refs_1_.7) | copy-start | bytes 1572868
  35.2 25.9 %collective-permute-start.16 = (bf16[4,512,256]{2,1,0:T(8,128)(2,1)S(1)}, bf16[4,512,256]{2,1,0:T(8,128)(2,1)S(1)}, u32[]{:S(2)}, u32[]{:S(2)}) collective-permute-start(bf16[4,512,256]{2,1,0:T(8,128)(2,1)S(1)} %get-tuple-element.43.refs_6_), channel_id=1, source_target_pairs={{0,2},{1,3},{2,0},{3,1},{4,6},{5,7},{6,4},{7,5},{8,10},{9,11},{10,... | collective-permute-start | bytes 3145736 | tf_op jit(solution)/shard_map/ppermute | solution.py:491
  38.0 10.0 %collective-permute-start.12 = (bf16[3,1024,128]{2,1,0:T(8,128)(2,1)S(1)}, bf16[3,1024,128]{2,1,0:T(8,128)(2,1)S(1)}, u32[]{:S(2)}, u32[]{:S(2)}) collective-permute-start(bf16[3,1024,128]{2,1,0:T(8,128)(2,1)S(1)} %get-tuple-element.42.refs_4_), channel_id=1, source_target_pairs={{0,1},{1,0},{2,3},{3,2},{4,5},{5,4},{6,7},{7,6},{8,9},{9,8},{10,11... | collective-permute-start | bytes 2359304 | tf_op jit(solution)/shard_map/ppermute | solution.py:414
  38.0 7.8 %collective-permute-start.1 = (bf16[512,128]{1,0:T(8,128)(2,1)S(1)}, bf16[512,128]{1,0:T(8,128)(2,1)S(1)}, u32[]{:S(2)}, u32[]{:S(2)}) collective-permute-start(bf16[512,128]{1,0:T(8,128)(2,1)S(1)} %collective-permute-done.refs_6_.refs_2_), channel_id=1, source_target_pairs={{0,1},{1,0},{2,3},{3,2},{4,5},{5,4},{6,7},{7,6},{8,9},{9,8},{10,11... | collective-permute-start | bytes 393224 | tf_op jit(solution)/shard_map/ppermute | solution.py:414
  40.9 26.7 %collective-permute-start.13 = (bf16[2,512,256]{2,1,0:T(8,128)(2,1)S(1)}, bf16[2,512,256]{2,1,0:T(8,128)(2,1)S(1)}, u32[]{:S(2)}, u32[]{:S(2)}) collective-permute-start(bf16[2,512,256]{2,1,0:T(8,128)(2,1)S(1)} %get-tuple-element.44.refs_6_), channel_id=1, source_target_pairs={{0,8},{1,9},{2,10},{3,11},{4,12},{5,13},{6,14},{7,15},{8,0},{9,1},... | collective-permute-start | bytes 1572872 | tf_op jit(solution)/shard_map/ppermute | solution.py:417
  44.8 25.0 %collective-permute-start.14 = (bf16[2,512,256]{2,1,0:T(8,128)(2,1)S(1)}, bf16[2,512,256]{2,1,0:T(8,128)(2,1)S(1)}, u32[]{:S(2)}, u32[]{:S(2)}) collective-permute-start(bf16[2,512,256]{2,1,0:T(8,128)(2,1)S(1)} %get-tuple-element.47), channel_id=1, source_target_pairs={{0,4},{1,5},{2,6},{3,7},{4,8},{5,9},{6,10},{7,11},{8,12},{9,13},{1... | collective-permute-start | bytes 1572872 | tf_op jit(solution)/shard_map/ppermute | solution.py:417
  45.8 24.0 %collective-permute-start.15 = (bf16[2,512,256]{2,1,0:T(8,128)(2,1)S(1)}, bf16[2,512,256]{2,1,0:T(8,128)(2,1)S(1)}, u32[]{:S(2)}, u32[]{:S(2)}) collective-permute-start(bf16[2,512,256]{2,1,0:T(8,128)(2,1)S(1)} %get-tuple-element.48), channel_id=1, source_target_pairs={{0,12},{1,13},{2,14},{3,15},{4,0},{5,1},{6,2},{7,3},{8,4},{9,5},{1... | collective-permute-start | bytes 1572872 | tf_op jit(solution)/shard_map/ppermute | solution.py:417
  62.6 17.5 %collective-permute-start.19 = (bf16[512,256]{1,0:T(8,128)(2,1)S(1)}, bf16[512,256]{1,0:T(8,128)(2,1)S(1)}, u32[]{:S(2)}, u32[]{:S(2)}) collective-permute-start(bf16[512,256]{1,0:T(8,128)(2,1)S(1)} %get-tuple-element.49.refs_9_), channel_id=1, source_target_pairs={{0,8},{1,9},{2,10},{3,11},{4,12},{5,13},{6,14},{7,15},{8,0},{9,1},... | collective-permute-start | bytes 786440 | tf_op jit(solution)/shard_map/ppermute | solution.py:417
  66.6 13.5 %collective-permute-start.20 = (bf16[512,256]{1,0:T(8,128)(2,1)S(1)}, bf16[512,256]{1,0:T(8,128)(2,1)S(1)}, u32[]{:S(2)}, u32[]{:S(2)}) collective-permute-start(bf16[512,256]{1,0:T(8,128)(2,1)S(1)} %get-tuple-element.52), channel_id=1, source_target_pairs={{0,4},{1,5},{2,6},{3,7},{4,8},{5,9},{6,10},{7,11},{8,12},{9,13},{1... | collective-permute-start | bytes 786440 | tf_op jit(solution)/shard_map/ppermute | solution.py:417
  67.6 12.6 %collective-permute-start.21 = (bf16[512,256]{1,0:T(8,128)(2,1)S(1)}, bf16[512,256]{1,0:T(8,128)(2,1)S(1)}, u32[]{:S(2)}, u32[]{:S(2)}) collective-permute-start(bf16[512,256]{1,0:T(8,128)(2,1)S(1)} %get-tuple-element.53), channel_id=1, source_target_pairs={{0,12},{1,13},{2,14},{3,15},{4,0},{5,1},{6,2},{7,3},{8,4},{9,5},{1... | collective-permute-start | bytes 786440 | tf_op jit(solution)/shard_map/ppermute | solution.py:417
  70.9 8.6 %collective-permute-start.17 = (bf16[256,256]{1,0:T(8,128)(2,1)S(1)}, bf16[256,256]{1,0:T(8,128)(2,1)S(1)}, u32[]{:S(2)}, u32[]{:S(2)}) collective-permute-start(bf16[256,256]{1,0:T(8,128)(2,1)S(1)} %get-tuple-element.50.refs_10_), channel_id=1, source_target_pairs={{0,2},{1,3},{2,0},{3,1},{4,6},{5,7},{6,4},{7,5},{8,10},{9,11},{10,... | collective-permute-start | bytes 393224 | tf_op jit(solution)/shard_map/ppermute | solution.py:538
  73.6 6.5 %collective-permute-start.18 = (bf16[256,256]{1,0:T(8,128)(2,1)S(1)}, bf16[256,256]{1,0:T(8,128)(2,1)S(1)}, u32[]{:S(2)}, u32[]{:S(2)}) collective-permute-start(bf16[256,256]{1,0:T(8,128)(2,1)S(1)} %get-tuple-element.51), channel_id=1, source_target_pairs={{0,2},{1,3},{2,0},{3,1},{4,6},{5,7},{6,4},{7,5},{8,10},{9,11},{10,... | collective-permute-start | bytes 393224 | tf_op jit(solution)/shard_map/ppermute | solution.py:538

commit v5 on v4

--- a/solution.py
+++ b/solution.py
@@ -16,7 +16,10 @@
 ROWS = HEADS * HD
 MSG = ROWS + 32
 CB = 256
-Z_ORDER = (2, 1, 3)
+FIRST_BLOCKS = 10
+LATE_BLOCKS = 6
+Z_FIRST = (2, 1, 3)
+Z_SECOND = (2, 1, 3)
 BF = jnp.bfloat16
 F32 = jnp.float32
 US = 10**5
@@ -253,7 +256,13 @@
     return tuple(new)
 
 
-def earlier_kernel(info, q_ref, far, far_other, mine, other, best_ref, acc_ref, k_all, v_all):
+def attend_kernel(
+    info, q_ref, k_ref, v_ref, far, far_other, mine, other, g0, g1, g2, g3, near_w, far_w,
+    out_ref, late_ref, ready_ref, k_all, v_all, sems,
+):
+    copies = weight_copies(info, near_w, far_w, late_ref, sems, FIRST_BLOCKS, LATE_BLOCKS)
+    for copy in copies:
+        copy.start()
     y, x = info[YPOS], info[XLO]
     place = (1 - x) * 4 + y
     k_all[place], v_all[place] = split_pair(info, far[...], far_other[...])
@@ -261,20 +270,10 @@
         for plane, rows in ((x, slice(0, TOK)), (1 - x, slice(TOK, 2 * TOK))):
             place = plane * 4 + lax.rem(y - d + 4, 4)
             k_all[place], v_all[place] = split_pair(info, mine[d - 1, rows, :], other[d - 1, rows, :])
-    queries = pieces(q_ref)
-    start = (jnp.full((1, HALF), -1e30, F32), jnp.zeros((ACC, HALF), F32)) * len(UNITS)
-    state = lax.fori_loop(
-        0, info[SEQ], lambda j, state: add_block(queries, k_all[j], v_all[j], state), start
-    )
-    for u in range(len(UNITS)):
-        best_ref[u] = jnp.broadcast_to(state[2 * u], (8, HALF))
-        acc_ref[u] = state[2 * u + 1]
-
-
-def own_kernel(info, q_ref, k_ref, v_ref, best_ref, acc_ref, out_ref):
     limit = info[LENGTH] - info[SEQ] * TOK
     vt = with_ones([v_ref[i * HD : (i + 1) * HD, :] for i in range(TOK // HD)])
     queries = pieces(q_ref)
+    state = []
     for u, (h, i) in enumerate(UNITS):
         wide = (i + 1) * HALF
         scores = lax.dot_general(k_ref[0:wide, :], queries[u], NT, preferred_element_type=F32)
@@ -282,29 +281,41 @@
         t = i * HALF + lax.broadcasted_iota(jnp.int32, (wide, HALF), 1)
         keep = jnp.logical_and(s <= t, s < limit)
         scores = jnp.where(keep, scores, -jnp.inf)
-        best = best_ref[u, 0:1, :]
-        top = jnp.maximum(best, jnp.max(scores, axis=0, keepdims=True))
-        weights = jnp.exp2((scores - top) * SCALE).astype(BF)
-        shrink = jnp.exp2((best - top) * SCALE)
-        summed = acc_ref[u] * shrink + jnp.dot(vt[:, 0:wide], weights, preferred_element_type=F32)
+        best = jnp.max(scores, axis=0, keepdims=True)
+        weights = jnp.exp2((scores - best) * SCALE).astype(BF)
+        state += [best, jnp.dot(vt[:, 0:wide], weights, preferred_element_type=F32)]
+    state = lax.fori_loop(
+        0, info[SEQ], lambda j, state: add_block(queries, k_all[j], v_all[j], state), tuple(state)
+    )
+    for u, (h, i) in enumerate(UNITS):
+        summed = state[2 * u + 1]
         out = summed[0:HD] * (1.0 / summed[HD : HD + 1])
         out_ref[i * HALF : (i + 1) * HALF, h * HD : (h + 1) * HD] = out.T.astype(BF)
-
-
-def weights_kernel(info, near, far, out_ref, sems):
-    def copies(k):
-        part = pl.ds(pl.multiple_of(info[COLUMNS + k] * CB, CB), CB)
-        return (
+    for copy in copies:
+        copy.wait()
+    for i in range(2):
+        acc = product((g0, g1, g2, g3), late_ref, 2 * i, 2)
+        ready_ref[2 * i] = acc[:, 0:CB]
+        ready_ref[2 * i + 1] = acc[:, CB : 2 * CB]
+
+
+def weight_copies(info, near, far, out_ref, sems, first, n):
+    copies = []
+    for k in range(n):
+        part = pl.ds(pl.multiple_of(info[COLUMNS + first + k] * CB, CB), CB)
+        copies += [
             pltpu.make_async_copy(near.at[:, part], out_ref.at[k, 0:TOK, :], sems.at[0, k]),
             pltpu.make_async_copy(far.at[:, part], out_ref.at[k, TOK : 2 * TOK, :], sems.at[1, k]),
-        )
-
-    for k in range(16):
-        for copy in copies(k):
-            copy.start()
-    for k in range(16):
-        for copy in copies(k):
-            copy.wait()
+        ]
+    return copies
+
+
+def weights_kernel(info, near, far, out_ref, sems):
+    copies = weight_copies(info, near, far, out_ref, sems, 0, FIRST_BLOCKS)
+    for copy in copies:
+        copy.start()
+    for copy in copies:
+        copy.wait()
 
 
 def product(gated, weights, first, n):
@@ -313,44 +324,38 @@
     return jnp.dot(g, w, preferred_element_type=F32)
 
 
-def first_x_kernel(info, *refs):
-    gated, weights, got, to_x, bundle = refs[0:4], refs[4], refs[5:8], refs[8], refs[9]
+def first_kernel(info, *refs):
+    gated, weights, to_x, to_z = refs[0:4], refs[4], refs[5], refs[6:9]
     for i in range(2):
         acc = product(gated, weights, 2 * i, 2).astype(BF)
         to_x[2 * i] = acc[:, 0:CB]
         to_x[2 * i + 1] = acc[:, CB : 2 * CB]
-    for d in range(3):
-        bundle[d] = got[d][...]
-
-
-def first_z_kernel(info, *refs):
-    gated, weights, to_z = refs[0:4], refs[4], refs[5:8]
-    for out, d in zip(to_z, Z_ORDER):
+    for out, d in zip(to_z, Z_FIRST):
         acc = product(gated, weights, 2 + 2 * d, 2).astype(BF)
         out[0] = acc[:, 0:CB]
         out[1] = acc[:, CB : 2 * CB]
 
 
-def second_z_kernel(info, *refs):
-    gated, (weights, x), to_z = refs[0:4], refs[4:6], refs[6:9]
-    acc = product(gated, weights, 11, 3)
-    for out, d in zip(to_z, Z_ORDER):
-        part = acc[:, (d - 1) * CB : d * CB]
-        out[...] = (part + x[lax.rem(info[ZPOS] + d, 4)].astype(F32)).astype(BF)
-
-
-def second_x_kernel(info, *refs):
-    gated, (weights, z1, z2, z3), to_x = refs[0:4], refs[4:8], refs[8:10]
-    total = product(gated, weights, 10, 1)
+def bundle_kernel(info, y1, y2, y3, same_ref, bundle_ref):
+    for d, r in enumerate((y1, y2, y3)):
+        bundle_ref[d] = r[...]
+
+
+def second_z_kernel(info, ready, x, *to_z):
+    for out, d in zip(to_z, Z_SECOND):
+        out[...] = (ready[d] + x[lax.rem(info[ZPOS] + d, 4)].astype(F32)).astype(BF)
+
+
+def second_x_kernel(info, ready, z1, z2, z3, to_x):
+    total = ready[0]
     for r in (z1, z2, z3):
         total = total + r[1 - info[XHI]].astype(F32)
-    for i in range(2):
-        to_x[i][...] = total[i * HALF : (i + 1) * HALF].astype(BF)
+    to_x[...] = total.astype(BF)
 
 
 def keep_kernel(info, *refs):
     gated, (weights, z1, z2, z3, x, out_ref) = refs[0:4], refs[4:10]
-    acc = product(gated, weights, 14, 2)
+    acc = product(gated, weights, 4, 2)
     total = acc[:, 0:CB]
     for r in (z1, z2, z3):
         total = total + r[info[XHI]].astype(F32)
@@ -358,10 +363,8 @@
     out_ref[:, CB : 2 * CB] = acc[:, CB : 2 * CB] + x[info[ZPOS]].astype(F32)
 
 
-def finish_kernel(info, kept, x0, x1, z1, z2, z3, out_ref):
-    for i, x in enumerate((x0, x1)):
-        rows = slice(i * HALF, (i + 1) * HALF)
-        out_ref[rows, 0:CB] = (kept[rows, 0:CB] + x[...].astype(F32)).astype(BF)
+def finish_kernel(info, kept, x, z1, z2, z3, out_ref):
+    out_ref[:, 0:CB] = (kept[:, 0:CB] + x[...].astype(F32)).astype(BF)
     total = kept[:, CB : 2 * CB]
     for r in (z1, z2, z3):
         total = total + r[...].astype(F32)
@@ -472,99 +475,87 @@
         (hbm(out_weight), hbm(far_weight)),
         [HBM, HBM],
         VMEM,
-        pltpu.VMEM((16, 2 * TOK, CB), BF),
-        scratch=[pltpu.SemaphoreType.DMA((2, 16))],
+        kept_shape((FIRST_BLOCKS, 2 * TOK, CB), BF),
+        scratch=[pltpu.SemaphoreType.DMA((2, FIRST_BLOCKS))],
         flops=10**10,
         after=(gated[0],),
     )
     gated += [core(a) for a in gated]
 
-    to_x, bundle = call(
-        first_x_kernel,
-        info,
-        (*gated, weights, *from_y),
-        [VMEM] * 8,
-        [VMEM] * 2,
-        [shape((4, TOK, CB), BF), shape((3, 2 * TOK, HD), BF)],
-        flops=US,
-    )
-    from_x = lax.ppermute(to_x, "head", X_SWAP)
-    to_z = call(
-        first_z_kernel,
+    to_x, *to_z = call(
+        first_kernel,
         info,
         (*gated, weights),
         [VMEM] * 5,
+        [VMEM] * 4,
+        [kept_shape((4, TOK, CB), BF)] + [kept_shape((2, TOK, CB), BF)] * 3,
+        flops=US,
+    )
+    to_x, bundle = call(
+        bundle_kernel,
+        info,
+        from_y,
         [VMEM] * 3,
-        [shape((2, TOK, CB), BF)] * 3,
+        [ANY, VMEM],
+        [kept_shape((4, TOK, CB), BF), kept_shape((3, 2 * TOK, HD), BF)],
         flops=US,
         after=(to_x,),
-    )
-    from_z = [along_z(a, d) for a, d in zip(to_z, Z_ORDER)]
-
-    best, acc = call(
-        earlier_kernel,
-        info,
-        (queries, kv_far, kv_far_other, bundle, core(bundle)),
-        [VMEM] * 5,
-        [VMEM] * 2,
-        [kept_shape((8, 8, HALF), F32), kept_shape((8, ACC, HALF), F32)],
-        scratch=[pltpu.VMEM((8, TOK, HD), BF)] * 2,
+        alias=0,
+    )
+    from_x = lax.ppermute(to_x, "head", X_SWAP)
+    from_z = [along_z(a, d) for a, d in zip(to_z, Z_FIRST)]
+
+    attended, late, ready = call(
+        attend_kernel,
+        info,
+        (queries, k_own, vt_own, kv_far, kv_far_other, bundle, core(bundle), *gated, hbm(out_weight), hbm(far_weight)),
+        [VMEM] * 11 + [HBM] * 2,
+        [full((TOK, ROWS)), VMEM, VMEM],
+        [shape((TOK, ROWS), BF), kept_shape((LATE_BLOCKS, 2 * TOK, CB), BF), kept_shape((4, TOK, CB), F32)],
+        scratch=[pltpu.VMEM((8, TOK, HD), BF)] * 2 + [pltpu.SemaphoreType.DMA((2, LATE_BLOCKS))],
         flops=US,
         limit=28 * 1024 * 1024,
         after=(to_z[0],),
     )
-
     to_z2 = call(
         second_z_kernel,
         info,
-        (*gated, weights, from_x),
-        [VMEM] * 6,
+        (ready, from_x),
+        [VMEM] * 2,
         [VMEM] * 3,
         [shape((TOK, CB), BF)] * 3,
         flops=US,
-        after=(best,),
-    )
-    from_z2 = [along_z(a, d) for a, d in zip(to_z2, Z_ORDER)]
+    )
+    from_z2 = [along_z(a, d) for a, d in zip(to_z2, Z_SECOND)]
     to_x2 = call(
         second_x_kernel,
         info,
-        (*gated, weights, *from_z),
-        [VMEM] * 8,
-        [VMEM] * 2,
-        [shape((HALF, CB), BF)] * 2,
+        (ready, *from_z),
+        [VMEM] * 4,
+        VMEM,
+        shape((TOK, CB), BF),
         flops=US,
         after=(to_z2[0],),
     )
-    from_x2 = [lax.ppermute(a, "head", X_SWAP) for a in to_x2]
+    from_x2 = lax.ppermute(to_x2, "head", X_SWAP)
     kept = call(
         keep_kernel,
         info,
-        (*gated, weights, *from_z, from_x),
+        (*gated, late, *from_z, from_x),
         [VMEM] * 9,
         VMEM,
         shape((TOK, ROWS), F32),
         flops=US,
-        after=(to_x2[0],),
-    )
-    attended = call(
-        own_kernel,
-        info,
-        (queries, k_own, vt_own, best, acc),
+        after=(to_x2,),
+    )
+    summed = call(
+        finish_kernel,
+        info,
+        (kept, from_x2, *from_z2),
         [VMEM] * 5,
         full((TOK, ROWS)),
         shape((TOK, ROWS), BF),
         flops=US,
-        after=(kept,),
-    )
-    summed = call(
-        finish_kernel,
-        info,
-        (kept, *from_x2, *from_z2),
-        [VMEM] * 6,
-        full((TOK, ROWS)),
-        shape((TOK, ROWS), BF),
-        flops=US,
-        after=(hbm(attended),),
     )
     return (attended, summed, final_states)
 

time: 82 us -> 79.3 us (0.967)
  starting transfers between devices: 35.6 us -> 34.2 us
  waiting for transfers between devices: 16.4 us -> 15.3 us
  Pallas kernels: 27.9 us -> 27 us
    ppermute x6, waiting for transfers between devices: 3.8 us -> 1.14 us  [body(): along_y = lambda a, d: lax.ppermute(a, 'seq', Y_MOVE[d])]
    ppermute x1, waiting for transfers between devices: 11.6 us -> 9.07 us  [body(): from_x = lax.ppermute(to_x, 'head', X_SWAP)]
    ppermute x6, waiting for transfers between devices: 0.14 us -> 2.25 us  [body(): along_z = lambda a, d: lax.ppermute(a, 'head', Z_MOVE[d])]
    ppermute x2 -> x1, waiting for transfers between devices: 0.65 us -> 2.65 us  [body(): from_x2 = lax.ppermute(to_x2, 'head', X_SWAP)]
    ppermute x2 -> x1, starting transfers between devices: 3.61 us -> 1.79 us  [body(): from_x2 = lax.ppermute(to_x2, 'head', X_SWAP)]
    pallas_call x13 -> x12, Pallas kernels: 27.9 us -> 27 us  [call(): pl.pallas_call(run, grid_spec=spec, out_shape=out_shape, input_output_ali...]
  transfers between devices with their start and end apart: 22 -> 21, of which waited for: 7 -> 10; matrix products, arithmetic and copies ran while one was open for 0% -> 0% of each run, Pallas kernels for 30% -> 32%
where the time goes in v5:
time: 79.3 us; the launch traced here: 78.3 us
  starting transfers between devices  34.2 us (43%)
  Pallas kernels  27 us (34%)
  waiting for transfers between devices  15.3 us (19%)
  between operations  1.64 us (2%)
    pallas_call x12, Pallas kernels, call(): pl.pallas_call(run, grid_spec=spec, out_shape=out_shape, input_output_ali...  27 us
    ppermute x6, starting transfers between devices, body(): along_z = lambda a, d: lax.ppermute(a, 'head', Z_MOVE[d])  14.3 us
    ppermute x6, starting transfers between devices, body(): along_y = lambda a, d: lax.ppermute(a, 'seq', Y_MOVE[d])  11.2 us
    ppermute x1, waiting for transfers between devices, body(): from_x = lax.ppermute(to_x, 'head', X_SWAP)  9.07 us
    ppermute x2, starting transfers between devices, body(): lo = lambda a: lax.ppermute(a, 'seq', LO_SWAP)  3.07 us
    ppermute x1, starting transfers between devices, body(): from_x = lax.ppermute(to_x, 'head', X_SWAP)  2.8 us
    ppermute x1, waiting for transfers between devices, body(): from_x2 = lax.ppermute(to_x2, 'head', X_SWAP)  2.65 us
    ppermute x6, waiting for transfers between devices, body(): along_z = lambda a, d: lax.ppermute(a, 'head', Z_MOVE[d])  2.25 us
  transfers between devices with their start and end apart: 21, of which 10 were waited for; matrix products, arithmetic and copies ran while one was open for 0% of the time, Pallas kernels for 32%

profile of v5, /device:TPU:0, one launch (start us, length us, event | category | flops | bytes accessed | tf_op | source)
XLA Modules:
  0.0 78.3 jit_solution(17283015260969192442)
XLA Ops:
  0.6 0.0 copy-start
  0.6 0.0 copy-start.2
  0.7 0.1 collective-permute-start.11
  1.6 0.1 stack.95.refs_0_
  1.7 3.4 %shard_map.139 = (bf16[512,128]{1,0:T(8,128)(2,1)S(1)}, bf16[512,128]{1,0:T(8,128)(2,1)S(1)}, bf16[512,128]{1,0:T(8,128)(2,1)S(1)}, bf16[544,128]{1,0:T(8,128)(2...) custom-call(s32[24]{0:T(128)S(1)} %stack.95.refs_0_, ...), custom_call_target="tpu_custom_call" | custom-call | flops 100000 | tf_op jit(solution)/shard_map/pallas_call | solution.py:48
  5.1 1.7 %collective-permute-start.2 = (bf16[544,128]{1,0:T(8,128)(2,1)S(1)}, bf16[544,128]{1,0:T(8,128)(2,1)S(1)}, u32[]{:S(2)}, u32[]{:S(2)}) collective-permute-start(bf16[544,128]{1,0:T(8,128)(2,1)S(1)} %get-tuple-element.32.refs_1_), channel_id=1, source_target_pairs={{0,16},{16,32},{32,48},{48,0},{64,80},{80,96},{96,112},{112,64},{1... | collective-permute-start | bytes 417800 | tf_op jit(solution)/shard_map/ppermute | solution.py:419
  6.8 2.9 %collective-permute-start.3 = (bf16[544,128]{1,0:T(8,128)(2,1)S(1)}, bf16[544,128]{1,0:T(8,128)(2,1)S(1)}, u32[]{:S(2)}, u32[]{:S(2)}) collective-permute-start(bf16[544,128]{1,0:T(8,128)(2,1)S(1)} %get-tuple-element.32.refs_1_), channel_id=1, source_target_pairs={{0,32},{16,48},{32,0},{48,16},{64,96},{80,112},{96,64},{112,80},{1... | collective-permute-start | bytes 417800 | tf_op jit(solution)/shard_map/ppermute | solution.py:419
  9.7 1.3 %collective-permute-start.4 = (bf16[544,128]{1,0:T(8,128)(2,1)S(1)}, bf16[544,128]{1,0:T(8,128)(2,1)S(1)}, u32[]{:S(2)}, u32[]{:S(2)}) collective-permute-start(bf16[544,128]{1,0:T(8,128)(2,1)S(1)} %get-tuple-element.32.refs_1_), channel_id=1, source_target_pairs={{0,48},{16,0},{32,16},{48,32},{64,112},{80,64},{96,80},{112,96},{1... | collective-permute-start | bytes 417800 | tf_op jit(solution)/shard_map/ppermute | solution.py:419
  11.0 1.5 %collective-permute-start = (bf16[512,128]{1,0:T(8,128)(2,1)S(1)}, bf16[512,128]{1,0:T(8,128)(2,1)S(1)}, u32[]{:S(2)}, u32[]{:S(2)}) collective-permute-start(bf16[512,128]{1,0:T(8,128)(2,1)S(1)} %get-tuple-element.31.refs_5_), channel_id=1, source_target_pairs={{0,64},{16,80},{32,96},{48,112},{64,0},{80,16},{96,32},{112,48},{1... | collective-permute-start | bytes 393224 | tf_op jit(solution)/shard_map/ppermute | solution.py:418
  12.5 3.3 %shard_map.140.refs_7_.refs_3_ = f32[512,512]{1,0:T(8,128)S(1)} custom-call(s32[24]{0:T(128)S(1)} %stack.95.refs_0_, f32[16,512]{1,0:T(8,128)S(1)} %get-tuple-element.33.refs_1_, bf16[512,512]{1,0:T(8,128)(2,1)} %refs_2_.5, bf16[512,128]{1,0:T(8,128)(2,1)S(1)} %get-tuple-element.34.refs_3_, bf16[512,128]{1,0:T(8,128)(2,1)S(1)} %get-tuple-element.35.refs_4_, ...), custom_call_target="tpu_custom_call" | custom-call | flops 100000 | tf_op jit(solution)/shard_map/pallas_call | solution.py:48
  15.8 0.2 collective-permute-done.refs_6_.refs_4_
  16.0 0.0 collective-permute-done.2.refs_2_
  16.0 0.5 collective-permute-done.3.refs_3_
  16.5 0.0 collective-permute-done.4.refs_4_
  16.5 0.7 shard_map.141
  17.3 1.6 %collective-permute-start.8 = (bf16[544,128]{1,0:T(8,128)(2,1)S(1)}, bf16[544,128]{1,0:T(8,128)(2,1)S(1)}, u32[]{:S(2)}, u32[]{:S(2)}) collective-permute-start(bf16[544,128]{1,0:T(8,128)(2,1)S(1)} %get-tuple-element.39.refs_7_), channel_id=1, source_target_pairs={{0,64},{16,80},{32,96},{48,112},{64,0},{80,16},{96,32},{112,48},{1... | collective-permute-start | bytes 417800 | tf_op jit(solution)/shard_map/ppermute | solution.py:418
  18.9 1.2 %collective-permute-start.5 = (bf16[1024,128]{1,0:T(8,128)(2,1)S(1)}, bf16[1024,128]{1,0:T(8,128)(2,1)S(1)}, u32[]{:S(2)}, u32[]{:S(2)}) collective-permute-start(bf16[1024,128]{1,0:T(8,128)(2,1)S(1)} %get-tuple-element.36), channel_id=1, source_target_pairs={{0,16},{16,32},{32,48},{48,0},{64,80},{80,96},{96,112},{112,64},{1... | collective-permute-start | bytes 786440 | tf_op jit(solution)/shard_map/ppermute | solution.py:419
  20.1 2.4 %collective-permute-start.6 = (bf16[1024,128]{1,0:T(8,128)(2,1)S(1)}, bf16[1024,128]{1,0:T(8,128)(2,1)S(1)}, u32[]{:S(2)}, u32[]{:S(2)}) collective-permute-start(bf16[1024,128]{1,0:T(8,128)(2,1)S(1)} %get-tuple-element.36), channel_id=1, source_target_pairs={{0,32},{16,48},{32,0},{48,16},{64,96},{80,112},{96,64},{112,80},{1... | collective-permute-start | bytes 786440 | tf_op jit(solution)/shard_map/ppermute | solution.py:419
  22.5 1.6 %collective-permute-start.7 = (bf16[1024,128]{1,0:T(8,128)(2,1)S(1)}, bf16[1024,128]{1,0:T(8,128)(2,1)S(1)}, u32[]{:S(2)}, u32[]{:S(2)}) collective-permute-start(bf16[1024,128]{1,0:T(8,128)(2,1)S(1)} %get-tuple-element.36), channel_id=1, source_target_pairs={{0,48},{16,0},{32,16},{48,32},{64,112},{80,64},{96,80},{112,96},{1... | collective-permute-start | bytes 786440 | tf_op jit(solution)/shard_map/ppermute | solution.py:419
  24.1 0.0 collective-permute-done.8.refs_8_
  24.1 0.0 copy-done
  24.1 0.0 copy-done.2
  24.1 1.8 %shard_map.142 = (bf16[512,256]{1,0:T(8,128)(2,1)S(1)}, bf16[512,256]{1,0:T(8,128)(2,1)S(1)}, f32[4,16,128]{2,1,0:T(8,128)}) custom-call(s32[24]{0:T(128)S(1)} %stack.95.refs_0_, f32[16,512]{1,0:T(8,128)S(1)} %get-tuple-element.33.refs_1_, bf16[512,512]{1,0:T(8,128)(2,1)S(1)} %copy-done, f32[512,512]{1,0:T(8,128)S(1)} %shard_map.140.refs_7_.refs_3_, ...), custom_call_target="tpu_custom_call" | custom-call | flops 100000 | tf_op jit(solution)/shard_map/pallas_call | solution.py:48
  25.9 0.0 collective-permute-start.10
  25.9 0.0 collective-permute-done.11.refs_2_.refs_13_
  25.9 0.5 collective-permute-start.9
  26.4 3.2 %shard_map.143.refs_5_ = bf16[10,1024,256]{2,1,0:T(8,128)(2,1)S(1)} custom-call(s32[24]{0:T(128)S(1)} %stack.95.refs_0_, bf16[512,8192]{1,0:T(8,128)(2,1)} %refs_12_.1, bf16[512,8192]{1,0:T(8,128)(2,1)} %collective-permute-done.11.refs_2_.refs_13_, bf16[512,256]{1,0:T(8,128)(2,1)S(1)} %get-tuple-element.40.refs_3_.refs_1_.refs_8_), custom_call_target="tpu_custom_call" | custom-call | flops 10000000000 | tf_op jit(solution)/shard_map/pallas_call | solution.py:48
  29.6 0.0 copy-start.1
  29.6 0.0 collective-permute-done.10.refs_4_.refs_11_
  29.7 0.0 collective-permute-done.9.refs_3_.refs_10_
  29.7 3.4 %shard_map.144 = (bf16[4,512,256]{2,1,0:T(8,128)(2,1)S(1)}, bf16[2,512,256]{2,1,0:T(8,128)(2,1)S(1)}, bf16[2,512,256]{2,1,0:T(8,128)(2,1)S(1)}, bf16[2,512,256]{2,1,0:T(8,128)(2,1)S(1)}) custom-call(s32[24]{0:T(128)S(1)} %stack.95.refs_0_, bf16[512,256]{1,0:T(8,128)(2,1)S(1)} %get-tuple-element.40.refs_3_.refs_1_.refs_8_, ...), custom_call_target="tpu_custom_call" | custom-call | flops 100000 | tf_op jit(solution)/shard_map/pallas_call | solution.py:48
  33.1 0.0 collective-permute-done.5.refs_1_
  33.1 0.5 collective-permute-done.6.refs_2_
  33.6 0.1 collective-permute-done.7.refs_3_
  33.7 0.6 shard_map.145
  34.3 2.8 %collective-permute-start.16 = (bf16[4,512,256]{2,1,0:T(8,128)(2,1)S(1)}, bf16[4,512,256]{2,1,0:T(8,128)(2,1)S(1)}, u32[]{:S(2)}, u32[]{:S(2)}) collective-permute-start(bf16[4,512,256]{2,1,0:T(8,128)(2,1)S(1)} %get-tuple-element.49), channel_id=1, source_target_pairs={{0,2},{1,3},{2,0},{3,1},{4,6},{5,7},{6,4},{7,5},{8,10},{9,11},{10,... | collective-permute-start | bytes 3145736 | tf_op jit(solution)/shard_map/ppermute | solution.py:505
  37.1 0.0 collective-permute-start.12
  37.1 0.5 collective-permute-start.1
  37.6 3.9 %collective-permute-start.13 = (bf16[2,512,256]{2,1,0:T(8,128)(2,1)S(1)}, bf16[2,512,256]{2,1,0:T(8,128)(2,1)S(1)}, u32[]{:S(2)}, u32[]{:S(2)}) collective-permute-start(bf16[2,512,256]{2,1,0:T(8,128)(2,1)S(1)} %get-tuple-element.44.refs_14_), channel_id=1, source_target_pairs={{0,8},{1,9},{2,10},{3,11},{4,12},{5,13},{6,14},{7,15},{8,0},{9,1},... | collective-permute-start | bytes 1572872 | tf_op jit(solution)/shard_map/ppermute | solution.py:420
  41.5 1.0 %collective-permute-start.14 = (bf16[2,512,256]{2,1,0:T(8,128)(2,1)S(1)}, bf16[2,512,256]{2,1,0:T(8,128)(2,1)S(1)}, u32[]{:S(2)}, u32[]{:S(2)}) collective-permute-start(bf16[2,512,256]{2,1,0:T(8,128)(2,1)S(1)} %get-tuple-element.47), channel_id=1, source_target_pairs={{0,4},{1,5},{2,6},{3,7},{4,8},{5,9},{6,10},{7,11},{8,12},{9,13},{1... | collective-permute-start | bytes 1572872 | tf_op jit(solution)/shard_map/ppermute | solution.py:420
  42.5 0.0 collective-permute-done.1.refs_5_
  42.5 2.2 %collective-permute-start.15 = (bf16[2,512,256]{2,1,0:T(8,128)(2,1)S(1)}, bf16[2,512,256]{2,1,0:T(8,128)(2,1)S(1)}, u32[]{:S(2)}, u32[]{:S(2)}) collective-permute-start(bf16[2,512,256]{2,1,0:T(8,128)(2,1)S(1)} %get-tuple-element.48), channel_id=1, source_target_pairs={{0,12},{1,13},{2,14},{3,15},{4,0},{5,1},{6,2},{7,3},{8,4},{9,5},{1... | collective-permute-start | bytes 1572872 | tf_op jit(solution)/shard_map/ppermute | solution.py:420
  44.8 0.0 collective-permute-done.12.refs_7_
  44.8 0.0 copy-done.1
  44.8 6.5 %shard_map.146 = (bf16[512,512]{1,0:T(8,128)(2,1)}, bf16[6,1024,256]{2,1,0:T(8,128)(2,1)S(1)}, f32[4,512,256]{2,1,0:T(8,128)S(1)}) custom-call(s32[24]{0:T(128)S(1)} %stack.95.refs_0_, bf16[512,512]{1,0:T(8,128)(2,1)S(1)} %copy-done.1, bf16[512,128]{1,0:T(8,128)(2,1)S(1)} %get-tuple-element.29.refs_2_, bf16[512,128]{1,0:T(8,128)(2,1)S(1)} %get-tuple-element.30.refs_3_, ...), custom_call_target="tpu_custom_call" | custom-call | flops 100000 | tf_op jit(solution)/shard_map/pallas_call | solution.py:48
  51.3 9.1 %collective-permute-done.16.refs_2_.refs_9_ = bf16[4,512,256]{2,1,0:T(8,128)(2,1)S(1)} collective-permute-done((bf16[4,512,256]{2,1,0:T(8,128)(2,1)S(1)}, bf16[4,512,256]{2,1,0:T(8,128)(2,1)S(1)}, u32[]{:S(2)}, u32[]{:S(2)}) %collective-permute-start.16) | collective-permute-done | bytes 1048608 | tf_op jit(solution)/shard_map/ppermute | solution.py:505
  60.4 0.7 shard_map.147
  61.1 3.9 %collective-permute-start.18 = (bf16[512,256]{1,0:T(8,128)(2,1)S(1)}, bf16[512,256]{1,0:T(8,128)(2,1)S(1)}, u32[]{:S(2)}, u32[]{:S(2)}) collective-permute-start(bf16[512,256]{1,0:T(8,128)(2,1)S(1)} %get-tuple-element.51.refs_5_), channel_id=1, source_target_pairs={{0,8},{1,9},{2,10},{3,11},{4,12},{5,13},{6,14},{7,15},{8,0},{9,1},... | collective-permute-start | bytes 786440 | tf_op jit(solution)/shard_map/ppermute | solution.py:420
  65.0 0.0 collective-permute-done.13.refs_2_.refs_6_
  65.0 0.3 collective-permute-done.14.refs_3_.refs_7_
  65.3 0.8 %collective-permute-done.15.refs_4_.refs_8_ = bf16[2,512,256]{2,1,0:T(8,128)(2,1)S(1)} collective-permute-done((bf16[2,512,256]{2,1,0:T(8,128)(2,1)S(1)}, bf16[2,512,256]{2,1,0:T(8,128)(2,1)S(1)}, u32[]{:S(2)}, u32[]{:S(2)}) %collective-permute-start.15) | collective-permute-done | bytes 524320 | tf_op jit(solution)/shard_map/ppermute | solution.py:420
  66.1 0.7 shard_map.148.refs_10_
  66.7 1.8 %collective-permute-start.17 = (bf16[512,256]{1,0:T(8,128)(2,1)S(1)}, bf16[512,256]{1,0:T(8,128)(2,1)S(1)}, u32[]{:S(2)}, u32[]{:S(2)}) collective-permute-start(bf16[512,256]{1,0:T(8,128)(2,1)S(1)} %shard_map.148.refs_10_), channel_id=1, source_target_pairs={{0,2},{1,3},{2,0},{3,1},{4,6},{5,7},{6,4},{7,5},{8,10},{9,11},{10,... | collective-permute-start | bytes 786440 | tf_op jit(solution)/shard_map/ppermute | solution.py:540
  68.5 1.0 %collective-permute-start.19 = (bf16[512,256]{1,0:T(8,128)(2,1)S(1)}, bf16[512,256]{1,0:T(8,128)(2,1)S(1)}, u32[]{:S(2)}, u32[]{:S(2)}) collective-permute-start(bf16[512,256]{1,0:T(8,128)(2,1)S(1)} %get-tuple-element.52), channel_id=1, source_target_pairs={{0,4},{1,5},{2,6},{3,7},{4,8},{5,9},{6,10},{7,11},{8,12},{9,13},{1... | collective-permute-start | bytes 786440 | tf_op jit(solution)/shard_map/ppermute | solution.py:420
  69.5 2.2 %collective-permute-start.20 = (bf16[512,256]{1,0:T(8,128)(2,1)S(1)}, bf16[512,256]{1,0:T(8,128)(2,1)S(1)}, u32[]{:S(2)}, u32[]{:S(2)}) collective-permute-start(bf16[512,256]{1,0:T(8,128)(2,1)S(1)} %get-tuple-element.53), channel_id=1, source_target_pairs={{0,12},{1,13},{2,14},{3,15},{4,0},{5,1},{6,2},{7,3},{8,4},{9,5},{1... | collective-permute-start | bytes 786440 | tf_op jit(solution)/shard_map/ppermute | solution.py:420
  71.8 1.2 %shard_map.149.refs_1_ = f32[512,512]{1,0:T(8,128)S(1)} custom-call(s32[24]{0:T(128)S(1)} %stack.95.refs_0_, bf16[512,256]{1,0:T(8,128)(2,1)S(1)} %get-tuple-element.40.refs_3_.refs_1_.refs_8_, bf16[512,256]{1,0:T(8,128)(2,1)S(1)} %get-tuple-element.41.refs_2_.refs_9_, bf16[512,256]{1,0:T(8,128)(2,1)S(1)} %collective-permute-done.9.refs_3_.refs_10_, ...), custom_call_target="tpu_custom_call" | custom-call | flops 100000 | tf_op jit(solution)/shard_map/pallas_call | solution.py:48
  73.0 2.6 %collective-permute-done.17.refs_2_ = bf16[512,256]{1,0:T(8,128)(2,1)S(1)} collective-permute-done((bf16[512,256]{1,0:T(8,128)(2,1)S(1)}, bf16[512,256]{1,0:T(8,128)(2,1)S(1)}, u32[]{:S(2)}, u32[]{:S(2)}) %collective-permute-start.17) | collective-permute-done | bytes 262176 | tf_op jit(solution)/shard_map/ppermute | solution.py:540
  75.6 0.0 collective-permute-done.18.refs_3_
  75.7 0.5 collective-permute-done.19.refs_4_
  76.1 0.7 collective-permute-done.20.refs_5_
  76.9 1.5 %shard_map.150 = bf16[512,512]{1,0:T(8,128)(2,1)} custom-call(s32[24]{0:T(128)S(1)} %stack.95.refs_0_, f32[512,512]{1,0:T(8,128)S(1)} %shard_map.149.refs_1_, bf16[512,256]{1,0:T(8,128)(2,1)S(1)} %collective-permute-done.17.refs_2_, bf16[512,256]{1,0:T(8,128)(2,1)S(1)} %collective-permute-done.18.refs_3_, ...), custom_call_target="tpu_custom_call" | custom-call | flops 100000 | tf_op jit(solution)/shard_map/pallas_call | solution.py:48
Async XLA Ops:
  0.6 23.4 %copy-start = (bf16[512,512]{1,0:T(8,128)(2,1)S(1)}, bf16[512,512]{1,0:T(8,128)(2,1)}, u32[]{:S(2)}) copy-start(bf16[512,512]{1,0:T(8,128)(2,1)} %refs_2_.5) | copy-start | bytes 1572868
  0.6 23.4 %copy-start.2 = (bf16[512,512]{1,0:T(8,128)(2,1)S(1)}, bf16[512,512]{1,0:T(8,128)(2,1)}, u32[]{:S(2)}) copy-start(bf16[512,512]{1,0:T(8,128)(2,1)} %refs_4_.3) | copy-start | bytes 1572868
  0.7 25.2 %collective-permute-start.11 = (bf16[512,8192]{1,0:T(8,128)(2,1)}, bf16[512,8192]{1,0:T(8,128)(2,1)}, u32[]{:S(2)}, u32[]{:S(2)}) collective-permute-start(bf16[512,8192]{1,0:T(8,128)(2,1)} %refs_12_.1), channel_id=1, source_target_pairs={{0,1},{1,0},{2,3},{3,2},{4,5},{5,4},{6,7},{7,6},{8,9},{9,8},{10,11... | collective-permute-start | bytes 25165832 | tf_op jit(solution)/shard_map/ppermute | solution.py:417
  5.1 10.9 %collective-permute-start.2 = (bf16[544,128]{1,0:T(8,128)(2,1)S(1)}, bf16[544,128]{1,0:T(8,128)(2,1)S(1)}, u32[]{:S(2)}, u32[]{:S(2)}) collective-permute-start(bf16[544,128]{1,0:T(8,128)(2,1)S(1)} %get-tuple-element.32.refs_1_), channel_id=1, source_target_pairs={{0,16},{16,32},{32,48},{48,0},{64,80},{80,96},{96,112},{112,64},{1... | collective-permute-start | bytes 417800 | tf_op jit(solution)/shard_map/ppermute | solution.py:419
  6.8 9.7 %collective-permute-start.3 = (bf16[544,128]{1,0:T(8,128)(2,1)S(1)}, bf16[544,128]{1,0:T(8,128)(2,1)S(1)}, u32[]{:S(2)}, u32[]{:S(2)}) collective-permute-start(bf16[544,128]{1,0:T(8,128)(2,1)S(1)} %get-tuple-element.32.refs_1_), channel_id=1, source_target_pairs={{0,32},{16,48},{32,0},{48,16},{64,96},{80,112},{96,64},{112,80},{1... | collective-permute-start | bytes 417800 | tf_op jit(solution)/shard_map/ppermute | solution.py:419
  9.7 6.8 %collective-permute-start.4 = (bf16[544,128]{1,0:T(8,128)(2,1)S(1)}, bf16[544,128]{1,0:T(8,128)(2,1)S(1)}, u32[]{:S(2)}, u32[]{:S(2)}) collective-permute-start(bf16[544,128]{1,0:T(8,128)(2,1)S(1)} %get-tuple-element.32.refs_1_), channel_id=1, source_target_pairs={{0,48},{16,0},{32,16},{48,32},{64,112},{80,64},{96,80},{112,96},{1... | collective-permute-start | bytes 417800 | tf_op jit(solution)/shard_map/ppermute | solution.py:419
  11.0 5.0 %collective-permute-start = (bf16[512,128]{1,0:T(8,128)(2,1)S(1)}, bf16[512,128]{1,0:T(8,128)(2,1)S(1)}, u32[]{:S(2)}, u32[]{:S(2)}) collective-permute-start(bf16[512,128]{1,0:T(8,128)(2,1)S(1)} %get-tuple-element.31.refs_5_), channel_id=1, source_target_pairs={{0,64},{16,80},{32,96},{48,112},{64,0},{80,16},{96,32},{112,48},{1... | collective-permute-start | bytes 393224 | tf_op jit(solution)/shard_map/ppermute | solution.py:418
  17.3 6.8 %collective-permute-start.8 = (bf16[544,128]{1,0:T(8,128)(2,1)S(1)}, bf16[544,128]{1,0:T(8,128)(2,1)S(1)}, u32[]{:S(2)}, u32[]{:S(2)}) collective-permute-start(bf16[544,128]{1,0:T(8,128)(2,1)S(1)} %get-tuple-element.39.refs_7_), channel_id=1, source_target_pairs={{0,64},{16,80},{32,96},{48,112},{64,0},{80,16},{96,32},{112,48},{1... | collective-permute-start | bytes 417800 | tf_op jit(solution)/shard_map/ppermute | solution.py:418
  18.9 14.2 %collective-permute-start.5 = (bf16[1024,128]{1,0:T(8,128)(2,1)S(1)}, bf16[1024,128]{1,0:T(8,128)(2,1)S(1)}, u32[]{:S(2)}, u32[]{:S(2)}) collective-permute-start(bf16[1024,128]{1,0:T(8,128)(2,1)S(1)} %get-tuple-element.36), channel_id=1, source_target_pairs={{0,16},{16,32},{32,48},{48,0},{64,80},{80,96},{96,112},{112,64},{1... | collective-permute-start | bytes 786440 | tf_op jit(solution)/shard_map/ppermute | solution.py:419
  20.1 13.5 %collective-permute-start.6 = (bf16[1024,128]{1,0:T(8,128)(2,1)S(1)}, bf16[1024,128]{1,0:T(8,128)(2,1)S(1)}, u32[]{:S(2)}, u32[]{:S(2)}) collective-permute-start(bf16[1024,128]{1,0:T(8,128)(2,1)S(1)} %get-tuple-element.36), channel_id=1, source_target_pairs={{0,32},{16,48},{32,0},{48,16},{64,96},{80,112},{96,64},{112,80},{1... | collective-permute-start | bytes 786440 | tf_op jit(solution)/shard_map/ppermute | solution.py:419
  22.5 11.3 %collective-permute-start.7 = (bf16[1024,128]{1,0:T(8,128)(2,1)S(1)}, bf16[1024,128]{1,0:T(8,128)(2,1)S(1)}, u32[]{:S(2)}, u32[]{:S(2)}) collective-permute-start(bf16[1024,128]{1,0:T(8,128)(2,1)S(1)} %get-tuple-element.36), channel_id=1, source_target_pairs={{0,48},{16,0},{32,16},{48,32},{64,112},{80,64},{96,80},{112,96},{1... | collective-permute-start | bytes 786440 | tf_op jit(solution)/shard_map/ppermute | solution.py:419
  25.9 3.8 %collective-permute-start.10 = (bf16[512,256]{1,0:T(8,128)(2,1)S(1)}, bf16[512,256]{1,0:T(8,128)(2,1)S(1)}, u32[]{:S(2)}, u32[]{:S(2)}) collective-permute-start(bf16[512,256]{1,0:T(8,128)(2,1)S(1)} %get-tuple-element.41.refs_2_.refs_9_), channel_id=1, source_target_pairs={{0,1},{1,0},{2,3},{3,2},{4,5},{5,4},{6,7},{7,6},{8,9},{9,8},{10,11... | collective-permute-start | bytes 786440 | tf_op jit(solution)/shard_map/ppermute | solution.py:417
  25.9 3.8 %collective-permute-start.9 = (bf16[512,256]{1,0:T(8,128)(2,1)S(1)}, bf16[512,256]{1,0:T(8,128)(2,1)S(1)}, u32[]{:S(2)}, u32[]{:S(2)}) collective-permute-start(bf16[512,256]{1,0:T(8,128)(2,1)S(1)} %get-tuple-element.40.refs_3_.refs_1_.refs_8_), channel_id=1, source_target_pairs={{0,1},{1,0},{2,3},{3,2},{4,5},{5,4},{6,7},{7,6},{8,9},{9,8},{10,11... | collective-permute-start | bytes 786440 | tf_op jit(solution)/shard_map/ppermute | solution.py:417
  29.6 15.1 %copy-start.1 = (bf16[512,512]{1,0:T(8,128)(2,1)S(1)}, bf16[512,512]{1,0:T(8,128)(2,1)}, u32[]{:S(2)}) copy-start(bf16[512,512]{1,0:T(8,128)(2,1)} %refs_1_.5) | copy-start | bytes 1572868
  34.3 26.1 %collective-permute-start.16 = (bf16[4,512,256]{2,1,0:T(8,128)(2,1)S(1)}, bf16[4,512,256]{2,1,0:T(8,128)(2,1)S(1)}, u32[]{:S(2)}, u32[]{:S(2)}) collective-permute-start(bf16[4,512,256]{2,1,0:T(8,128)(2,1)S(1)} %get-tuple-element.49), channel_id=1, source_target_pairs={{0,2},{1,3},{2,0},{3,1},{4,6},{5,7},{6,4},{7,5},{8,10},{9,11},{10,... | collective-permute-start | bytes 3145736 | tf_op jit(solution)/shard_map/ppermute | solution.py:505
  37.1 7.6 %collective-permute-start.12 = (bf16[3,1024,128]{2,1,0:T(8,128)(2,1)S(1)}, bf16[3,1024,128]{2,1,0:T(8,128)(2,1)S(1)}, u32[]{:S(2)}, u32[]{:S(2)}) collective-permute-start(bf16[3,1024,128]{2,1,0:T(8,128)(2,1)S(1)} %get-tuple-element.43.refs_6_), channel_id=1, source_target_pairs={{0,1},{1,0},{2,3},{3,2},{4,5},{5,4},{6,7},{7,6},{8,9},{9,8},{10,11... | collective-permute-start | bytes 2359304 | tf_op jit(solution)/shard_map/ppermute | solution.py:417
  37.1 5.4 %collective-permute-start.1 = (bf16[512,128]{1,0:T(8,128)(2,1)S(1)}, bf16[512,128]{1,0:T(8,128)(2,1)S(1)}, u32[]{:S(2)}, u32[]{:S(2)}) collective-permute-start(bf16[512,128]{1,0:T(8,128)(2,1)S(1)} %collective-permute-done.refs_6_.refs_4_), channel_id=1, source_target_pairs={{0,1},{1,0},{2,3},{3,2},{4,5},{5,4},{6,7},{7,6},{8,9},{9,8},{10,11... | collective-permute-start | bytes 393224 | tf_op jit(solution)/shard_map/ppermute | solution.py:417
  37.6 27.4 %collective-permute-start.13 = (bf16[2,512,256]{2,1,0:T(8,128)(2,1)S(1)}, bf16[2,512,256]{2,1,0:T(8,128)(2,1)S(1)}, u32[]{:S(2)}, u32[]{:S(2)}) collective-permute-start(bf16[2,512,256]{2,1,0:T(8,128)(2,1)S(1)} %get-tuple-element.44.refs_14_), channel_id=1, source_target_pairs={{0,8},{1,9},{2,10},{3,11},{4,12},{5,13},{6,14},{7,15},{8,0},{9,1},... | collective-permute-start | bytes 1572872 | tf_op jit(solution)/shard_map/ppermute | solution.py:420
  41.5 23.8 %collective-permute-start.14 = (bf16[2,512,256]{2,1,0:T(8,128)(2,1)S(1)}, bf16[2,512,256]{2,1,0:T(8,128)(2,1)S(1)}, u32[]{:S(2)}, u32[]{:S(2)}) collective-permute-start(bf16[2,512,256]{2,1,0:T(8,128)(2,1)S(1)} %get-tuple-element.47), channel_id=1, source_target_pairs={{0,4},{1,5},{2,6},{3,7},{4,8},{5,9},{6,10},{7,11},{8,12},{9,13},{1... | collective-permute-start | bytes 1572872 | tf_op jit(solution)/shard_map/ppermute | solution.py:420
  42.5 23.5 %collective-permute-start.15 = (bf16[2,512,256]{2,1,0:T(8,128)(2,1)S(1)}, bf16[2,512,256]{2,1,0:T(8,128)(2,1)S(1)}, u32[]{:S(2)}, u32[]{:S(2)}) collective-permute-start(bf16[2,512,256]{2,1,0:T(8,128)(2,1)S(1)} %get-tuple-element.48), channel_id=1, source_target_pairs={{0,12},{1,13},{2,14},{3,15},{4,0},{5,1},{6,2},{7,3},{8,4},{9,5},{1... | collective-permute-start | bytes 1572872 | tf_op jit(solution)/shard_map/ppermute | solution.py:420
  61.1 14.6 %collective-permute-start.18 = (bf16[512,256]{1,0:T(8,128)(2,1)S(1)}, bf16[512,256]{1,0:T(8,128)(2,1)S(1)}, u32[]{:S(2)}, u32[]{:S(2)}) collective-permute-start(bf16[512,256]{1,0:T(8,128)(2,1)S(1)} %get-tuple-element.51.refs_5_), channel_id=1, source_target_pairs={{0,8},{1,9},{2,10},{3,11},{4,12},{5,13},{6,14},{7,15},{8,0},{9,1},... | collective-permute-start | bytes 786440 | tf_op jit(solution)/shard_map/ppermute | solution.py:420
  66.7 8.9 %collective-permute-start.17 = (bf16[512,256]{1,0:T(8,128)(2,1)S(1)}, bf16[512,256]{1,0:T(8,128)(2,1)S(1)}, u32[]{:S(2)}, u32[]{:S(2)}) collective-permute-start(bf16[512,256]{1,0:T(8,128)(2,1)S(1)} %shard_map.148.refs_10_), channel_id=1, source_target_pairs={{0,2},{1,3},{2,0},{3,1},{4,6},{5,7},{6,4},{7,5},{8,10},{9,11},{10,... | collective-permute-start | bytes 786440 | tf_op jit(solution)/shard_map/ppermute | solution.py:540
  68.5 7.6 %collective-permute-start.19 = (bf16[512,256]{1,0:T(8,128)(2,1)S(1)}, bf16[512,256]{1,0:T(8,128)(2,1)S(1)}, u32[]{:S(2)}, u32[]{:S(2)}) collective-permute-start(bf16[512,256]{1,0:T(8,128)(2,1)S(1)} %get-tuple-element.52), channel_id=1, source_target_pairs={{0,4},{1,5},{2,6},{3,7},{4,8},{5,9},{6,10},{7,11},{8,12},{9,13},{1... | collective-permute-start | bytes 786440 | tf_op jit(solution)/shard_map/ppermute | solution.py:420
  69.5 7.3 %collective-permute-start.20 = (bf16[512,256]{1,0:T(8,128)(2,1)S(1)}, bf16[512,256]{1,0:T(8,128)(2,1)S(1)}, u32[]{:S(2)}, u32[]{:S(2)}) collective-permute-start(bf16[512,256]{1,0:T(8,128)(2,1)S(1)} %get-tuple-element.53), channel_id=1, source_target_pairs={{0,12},{1,13},{2,14},{3,15},{4,0},{5,1},{6,2},{7,3},{8,4},{9,5},{1... | collective-permute-start | bytes 786440 | tf_op jit(solution)/shard_map/ppermute | solution.py:420

commit v6 on v5

--- a/solution.py
+++ b/solution.py
@@ -325,11 +325,11 @@
 
 
 def first_kernel(info, *refs):
-    gated, weights, to_x, to_z = refs[0:4], refs[4], refs[5], refs[6:9]
+    gated, weights, to_x, to_z = refs[0:4], refs[4], refs[5:7], refs[7:10]
     for i in range(2):
         acc = product(gated, weights, 2 * i, 2).astype(BF)
-        to_x[2 * i] = acc[:, 0:CB]
-        to_x[2 * i + 1] = acc[:, CB : 2 * CB]
+        to_x[i][0] = acc[:, 0:CB]
+        to_x[i][1] = acc[:, CB : 2 * CB]
     for out, d in zip(to_z, Z_FIRST):
         acc = product(gated, weights, 2 + 2 * d, 2).astype(BF)
         out[0] = acc[:, 0:CB]
@@ -341,9 +341,14 @@
         bundle_ref[d] = r[...]
 
 
-def second_z_kernel(info, ready, x, *to_z):
-    for out, d in zip(to_z, Z_SECOND):
-        out[...] = (ready[d] + x[lax.rem(info[ZPOS] + d, 4)].astype(F32)).astype(BF)
+def second_even_kernel(info, ready, x, to_z):
+    to_z[0:TOK, :] = (ready[2] + x[1].astype(F32)).astype(BF)
+    to_z[TOK:, :] = jnp.zeros((32, CB), BF)
+
+
+def second_odd_kernel(info, ready, x, *to_z):
+    for i, d in enumerate((1, 3)):
+        to_z[i][...] = (ready[d] + x[i].astype(F32)).astype(BF)
 
 
 def second_x_kernel(info, ready, z1, z2, z3, to_x):
@@ -360,14 +365,14 @@
     for r in (z1, z2, z3):
         total = total + r[info[XHI]].astype(F32)
     out_ref[:, 0:CB] = total
-    out_ref[:, CB : 2 * CB] = acc[:, CB : 2 * CB] + x[info[ZPOS]].astype(F32)
+    out_ref[:, CB : 2 * CB] = acc[:, CB : 2 * CB] + x[0].astype(F32)
 
 
 def finish_kernel(info, kept, x, z1, z2, z3, out_ref):
     out_ref[:, 0:CB] = (kept[:, 0:CB] + x[...].astype(F32)).astype(BF)
     total = kept[:, CB : 2 * CB]
     for r in (z1, z2, z3):
-        total = total + r[...].astype(F32)
+        total = total + r[0:TOK, :].astype(F32)
     out_ref[:, CB : 2 * CB] = total.astype(BF)
 
 
@@ -407,7 +412,7 @@
     z, x, c = head // 4, (head // 2) % 2, head % 2
     block = lambda zz, xx, half: ((zz % 4) * 4 + (xx % 2) * 2 + c) * 2 + half
     columns = (
-        [block(i, x + 1, 1) for i in range(4)]
+        [block(z + d, x + 1, 1) for d in (0, 2, 1, 3)]
         + [block(z + d, i, 0) for d in (1, 2, 3) for i in range(2)]
         + [block(z, x + 1, 0)]
         + [block(z + d, x, 1) for d in (1, 2, 3)]
@@ -482,27 +487,27 @@
     )
     gated += [core(a) for a in gated]
 
-    to_x, *to_z = call(
+    even_x, odd_x, *to_z = call(
         first_kernel,
         info,
         (*gated, weights),
         [VMEM] * 5,
-        [VMEM] * 4,
-        [kept_shape((4, TOK, CB), BF)] + [kept_shape((2, TOK, CB), BF)] * 3,
-        flops=US,
-    )
-    to_x, bundle = call(
+        [VMEM] * 5,
+        [kept_shape((2, TOK, CB), BF)] * 5,
+        flops=US,
+    )
+    even_x, bundle = call(
         bundle_kernel,
         info,
         from_y,
         [VMEM] * 3,
         [ANY, VMEM],
-        [kept_shape((4, TOK, CB), BF), kept_shape((3, 2 * TOK, HD), BF)],
-        flops=US,
-        after=(to_x,),
+        [kept_shape((2, TOK, CB), BF), kept_shape((3, 2 * TOK, HD), BF)],
+        flops=US,
+        after=(even_x,),
         alias=0,
     )
-    from_x = lax.ppermute(to_x, "head", X_SWAP)
+    from_even, from_odd = [lax.ppermute(a, "head", X_SWAP) for a in (even_x, odd_x)]
     from_z = [along_z(a, d) for a, d in zip(to_z, Z_FIRST)]
 
     attended, late, ready = call(
@@ -517,16 +522,27 @@
         limit=28 * 1024 * 1024,
         after=(to_z[0],),
     )
-    to_z2 = call(
-        second_z_kernel,
-        info,
-        (ready, from_x),
+    even_z = call(
+        second_even_kernel,
+        info,
+        (ready, from_even),
         [VMEM] * 2,
-        [VMEM] * 3,
-        [shape((TOK, CB), BF)] * 3,
-        flops=US,
-    )
-    from_z2 = [along_z(a, d) for a, d in zip(to_z2, Z_SECOND)]
+        VMEM,
+        shape((TOK + 32, CB), BF),
+        flops=US,
+    )
+    from_2 = along_z(even_z, 2)
+    odd_z = call(
+        second_odd_kernel,
+        info,
+        (ready, from_odd),
+        [VMEM] * 2,
+        [VMEM] * 2,
+        [shape((TOK, CB), BF)] * 2,
+        flops=US,
+        after=(even_z,),
+    )
+    from_z2 = [from_2, *[along_z(a, d) for a, d in zip(odd_z, (1, 3))]]
     to_x2 = call(
         second_x_kernel,
         info,
@@ -535,13 +551,13 @@
         VMEM,
         shape((TOK, CB), BF),
         flops=US,
-        after=(to_z2[0],),
+        after=(even_z,),
     )
     from_x2 = lax.ppermute(to_x2, "head", X_SWAP)
     kept = call(
         keep_kernel,
         info,
-        (*gated, late, *from_z, from_x),
+        (*gated, late, *from_z, from_even),
         [VMEM] * 9,
         VMEM,
         shape((TOK, ROWS), F32),

time: 79.3 us -> 79.5 us (level)
  starting transfers between devices: 34.2 us -> 36.1 us
  waiting for transfers between devices: 15.3 us -> 13.6 us
    ppermute x6, waiting for transfers between devices: 2.25 us -> 6.46 us  [body(): along_z = lambda a, d: lax.ppermute(a, 'head', Z_MOVE[d])]
    ppermute x1 -> x2, waiting for transfers between devices: 9.07 us -> 5.85 us  [body(): lax.ppermute(a, 'head', X_SWAP)]
    ppermute x1, waiting for transfers between devices: 2.65 us -> 0.01 us  [body(): from_x2 = lax.ppermute(to_x2, 'head', X_SWAP)]
    ppermute x1, starting transfers between devices: 1.79 us -> 2.8 us  [body(): from_x2 = lax.ppermute(to_x2, 'head', X_SWAP)]
    ppermute x1 -> x2, starting transfers between devices: 2.8 us -> 3.53 us  [body(): lax.ppermute(a, 'head', X_SWAP)]
    pallas_call x12 -> x13, Pallas kernels: 27 us -> 27.6 us  [call(): pl.pallas_call(run, grid_spec=spec, out_shape=out_shape, input_output_ali...]
  transfers between devices with their start and end apart: 21 -> 22, of which waited for: 10 -> 8; matrix products, arithmetic and copies ran while one was open for 0% -> 0% of each run, Pallas kernels for 32% -> 32%
where the time goes in v6:
time: 79.5 us; the launch traced here: 79.1 us
  starting transfers between devices  36.1 us (45%)
  Pallas kernels  27.6 us (35%)
  waiting for transfers between devices  13.6 us (17%)
  between operations  1.67 us (2%)
    pallas_call x13, Pallas kernels, call(): pl.pallas_call(run, grid_spec=spec, out_shape=out_shape, input_output_ali...  27.6 us
    ppermute x6, starting transfers between devices, body(): along_z = lambda a, d: lax.ppermute(a, 'head', Z_MOVE[d])  14.3 us
    ppermute x6, starting transfers between devices, body(): along_y = lambda a, d: lax.ppermute(a, 'seq', Y_MOVE[d])  11.2 us
    ppermute x6, waiting for transfers between devices, body(): along_z = lambda a, d: lax.ppermute(a, 'head', Z_MOVE[d])  6.46 us
    ppermute x2, waiting for transfers between devices, body(): lax.ppermute(a, 'head', X_SWAP)  5.85 us
    ppermute x2, starting transfers between devices, body(): lax.ppermute(a, 'head', X_SWAP)  3.53 us
    ppermute x2, starting transfers between devices, body(): lo = lambda a: lax.ppermute(a, 'seq', LO_SWAP)  3.06 us
    ppermute x1, starting transfers between devices, body(): from_x2 = lax.ppermute(to_x2, 'head', X_SWAP)  2.8 us
  transfers between devices with their start and end apart: 22, of which 8 were waited for; matrix products, arithmetic and copies ran while one was open for 0% of the time, Pallas kernels for 32%

profile of v6, /device:TPU:0, one launch (start us, length us, event | category | flops | bytes accessed | tf_op | source)
XLA Modules:
  0.0 79.1 jit_solution(18027790638571248015)
XLA Ops:
  0.6 0.0 copy-start
  0.6 0.0 copy-start.2
  0.7 0.1 collective-permute-start.11
  1.6 0.1 stack.95.refs_0_
  1.7 3.3 %shard_map.139 = (bf16[512,128]{1,0:T(8,128)(2,1)S(1)}, bf16[512,128]{1,0:T(8,128)(2,1)S(1)}, bf16[512,128]{1,0:T(8,128)(2,1)S(1)}, bf16[544,128]{1,0:T(8,128)(2...) custom-call(s32[24]{0:T(128)S(1)} %stack.95.refs_0_, ...), custom_call_target="tpu_custom_call" | custom-call | flops 100000 | tf_op jit(solution)/shard_map/pallas_call | solution.py:48
  5.1 1.7 %collective-permute-start.2 = (bf16[544,128]{1,0:T(8,128)(2,1)S(1)}, bf16[544,128]{1,0:T(8,128)(2,1)S(1)}, u32[]{:S(2)}, u32[]{:S(2)}) collective-permute-start(bf16[544,128]{1,0:T(8,128)(2,1)S(1)} %get-tuple-element.32.refs_1_), channel_id=1, source_target_pairs={{0,16},{16,32},{32,48},{48,0},{64,80},{80,96},{96,112},{112,64},{1... | collective-permute-start | bytes 417800 | tf_op jit(solution)/shard_map/ppermute | solution.py:424
  6.8 2.9 %collective-permute-start.3 = (bf16[544,128]{1,0:T(8,128)(2,1)S(1)}, bf16[544,128]{1,0:T(8,128)(2,1)S(1)}, u32[]{:S(2)}, u32[]{:S(2)}) collective-permute-start(bf16[544,128]{1,0:T(8,128)(2,1)S(1)} %get-tuple-element.32.refs_1_), channel_id=1, source_target_pairs={{0,32},{16,48},{32,0},{48,16},{64,96},{80,112},{96,64},{112,80},{1... | collective-permute-start | bytes 417800 | tf_op jit(solution)/shard_map/ppermute | solution.py:424
  9.7 1.3 %collective-permute-start.4 = (bf16[544,128]{1,0:T(8,128)(2,1)S(1)}, bf16[544,128]{1,0:T(8,128)(2,1)S(1)}, u32[]{:S(2)}, u32[]{:S(2)}) collective-permute-start(bf16[544,128]{1,0:T(8,128)(2,1)S(1)} %get-tuple-element.32.refs_1_), channel_id=1, source_target_pairs={{0,48},{16,0},{32,16},{48,32},{64,112},{80,64},{96,80},{112,96},{1... | collective-permute-start | bytes 417800 | tf_op jit(solution)/shard_map/ppermute | solution.py:424
  11.0 1.5 %collective-permute-start = (bf16[512,128]{1,0:T(8,128)(2,1)S(1)}, bf16[512,128]{1,0:T(8,128)(2,1)S(1)}, u32[]{:S(2)}, u32[]{:S(2)}) collective-permute-start(bf16[512,128]{1,0:T(8,128)(2,1)S(1)} %get-tuple-element.31.refs_5_), channel_id=1, source_target_pairs={{0,64},{16,80},{32,96},{48,112},{64,0},{80,16},{96,32},{112,48},{1... | collective-permute-start | bytes 393224 | tf_op jit(solution)/shard_map/ppermute | solution.py:423
  12.5 3.3 %shard_map.140.refs_7_.refs_3_ = f32[512,512]{1,0:T(8,128)S(1)} custom-call(s32[24]{0:T(128)S(1)} %stack.95.refs_0_, f32[16,512]{1,0:T(8,128)S(1)} %get-tuple-element.33.refs_1_, bf16[512,512]{1,0:T(8,128)(2,1)} %refs_2_.5, bf16[512,128]{1,0:T(8,128)(2,1)S(1)} %get-tuple-element.34.refs_3_, bf16[512,128]{1,0:T(8,128)(2,1)S(1)} %get-tuple-element.35.refs_4_, ...), custom_call_target="tpu_custom_call" | custom-call | flops 100000 | tf_op jit(solution)/shard_map/pallas_call | solution.py:48
  15.8 0.2 collective-permute-done.refs_6_.refs_4_
  16.0 0.0 collective-permute-done.2.refs_2_
  16.0 0.5 collective-permute-done.3.refs_3_
  16.5 0.0 collective-permute-done.4.refs_4_
  16.5 0.7 shard_map.141
  17.3 1.6 %collective-permute-start.8 = (bf16[544,128]{1,0:T(8,128)(2,1)S(1)}, bf16[544,128]{1,0:T(8,128)(2,1)S(1)}, u32[]{:S(2)}, u32[]{:S(2)}) collective-permute-start(bf16[544,128]{1,0:T(8,128)(2,1)S(1)} %get-tuple-element.39.refs_7_), channel_id=1, source_target_pairs={{0,64},{16,80},{32,96},{48,112},{64,0},{80,16},{96,32},{112,48},{1... | collective-permute-start | bytes 417800 | tf_op jit(solution)/shard_map/ppermute | solution.py:423
  18.9 1.2 %collective-permute-start.5 = (bf16[1024,128]{1,0:T(8,128)(2,1)S(1)}, bf16[1024,128]{1,0:T(8,128)(2,1)S(1)}, u32[]{:S(2)}, u32[]{:S(2)}) collective-permute-start(bf16[1024,128]{1,0:T(8,128)(2,1)S(1)} %get-tuple-element.36), channel_id=1, source_target_pairs={{0,16},{16,32},{32,48},{48,0},{64,80},{80,96},{96,112},{112,64},{1... | collective-permute-start | bytes 786440 | tf_op jit(solution)/shard_map/ppermute | solution.py:424
  20.1 2.4 %collective-permute-start.6 = (bf16[1024,128]{1,0:T(8,128)(2,1)S(1)}, bf16[1024,128]{1,0:T(8,128)(2,1)S(1)}, u32[]{:S(2)}, u32[]{:S(2)}) collective-permute-start(bf16[1024,128]{1,0:T(8,128)(2,1)S(1)} %get-tuple-element.36), channel_id=1, source_target_pairs={{0,32},{16,48},{32,0},{48,16},{64,96},{80,112},{96,64},{112,80},{1... | collective-permute-start | bytes 786440 | tf_op jit(solution)/shard_map/ppermute | solution.py:424
  22.5 1.6 %collective-permute-start.7 = (bf16[1024,128]{1,0:T(8,128)(2,1)S(1)}, bf16[1024,128]{1,0:T(8,128)(2,1)S(1)}, u32[]{:S(2)}, u32[]{:S(2)}) collective-permute-start(bf16[1024,128]{1,0:T(8,128)(2,1)S(1)} %get-tuple-element.36), channel_id=1, source_target_pairs={{0,48},{16,0},{32,16},{48,32},{64,112},{80,64},{96,80},{112,96},{1... | collective-permute-start | bytes 786440 | tf_op jit(solution)/shard_map/ppermute | solution.py:424
  24.1 0.0 collective-permute-done.8.refs_8_
  24.1 0.0 copy-done
  24.1 0.0 copy-done.2
  24.1 1.8 %shard_map.142 = (bf16[512,256]{1,0:T(8,128)(2,1)S(1)}, bf16[512,256]{1,0:T(8,128)(2,1)S(1)}, f32[4,16,128]{2,1,0:T(8,128)}) custom-call(s32[24]{0:T(128)S(1)} %stack.95.refs_0_, f32[16,512]{1,0:T(8,128)S(1)} %get-tuple-element.33.refs_1_, bf16[512,512]{1,0:T(8,128)(2,1)S(1)} %copy-done, f32[512,512]{1,0:T(8,128)S(1)} %shard_map.140.refs_7_.refs_3_, ...), custom_call_target="tpu_custom_call" | custom-call | flops 100000 | tf_op jit(solution)/shard_map/pallas_call | solution.py:48
  25.9 0.0 collective-permute-start.10
  25.9 0.0 collective-permute-done.11.refs_2_.refs_13_
  25.9 0.5 collective-permute-start.9
  26.4 3.2 %shard_map.143.refs_5_ = bf16[10,1024,256]{2,1,0:T(8,128)(2,1)S(1)} custom-call(s32[24]{0:T(128)S(1)} %stack.95.refs_0_, bf16[512,8192]{1,0:T(8,128)(2,1)} %refs_12_.1, bf16[512,8192]{1,0:T(8,128)(2,1)} %collective-permute-done.11.refs_2_.refs_13_, bf16[512,256]{1,0:T(8,128)(2,1)S(1)} %get-tuple-element.40.refs_3_.refs_1_.refs_8_), custom_call_target="tpu_custom_call" | custom-call | flops 10000000000 | tf_op jit(solution)/shard_map/pallas_call | solution.py:48
  29.6 0.0 copy-start.1
  29.6 0.0 collective-permute-done.10.refs_4_.refs_11_
  29.7 0.0 collective-permute-done.9.refs_3_.refs_10_
  29.7 3.4 %shard_map.144 = (bf16[2,512,256]{2,1,0:T(8,128)(2,1)S(1)}, bf16[2,512,256]{2,1,0:T(8,128)(2,1)S(1)}, bf16[2,512,256]{2,1,0:T(8,128)(2,1)S(1)}, bf16[2,512,256]{2,1,0:T(8,128)(2,1)S(1)}, bf16[2,512,256]{2,1,0:T(8,128)(2,1)S(1)}) custom-call(s32[24]{0:T(128)S(1)} %stack.95.refs_0_, bf16[512,256]{1,0:T(8,128)(2,1)S(1)} %get-tuple-element.40.refs_3_.refs_1_.refs_8_, ...), custom_call_target="tpu_custom_call" | custom-call | flops 100000 | tf_op jit(solution)/shard_map/pallas_call | solution.py:48
  33.1 0.0 collective-permute-done.5.refs_1_
  33.1 0.5 collective-permute-done.6.refs_2_
  33.6 0.1 collective-permute-done.7.refs_3_
  33.7 0.6 shard_map.145
  34.3 0.1 collective-permute-start.12
  34.4 0.5 collective-permute-start.1
  34.9 2.7 %collective-permute-start.16 = (bf16[2,512,256]{2,1,0:T(8,128)(2,1)S(1)}, bf16[2,512,256]{2,1,0:T(8,128)(2,1)S(1)}, u32[]{:S(2)}, u32[]{:S(2)}) collective-permute-start(bf16[2,512,256]{2,1,0:T(8,128)(2,1)S(1)} %get-tuple-element.49), channel_id=1, source_target_pairs={{0,2},{1,3},{2,0},{3,1},{4,6},{5,7},{6,4},{7,5},{8,10},{9,11},{10,... | collective-permute-start | bytes 1572872 | tf_op jit(solution)/shard_map/ppermute | solution.py:510
  37.6 0.8 %collective-permute-start.19 = (bf16[2,512,256]{2,1,0:T(8,128)(2,1)S(1)}, bf16[2,512,256]{2,1,0:T(8,128)(2,1)S(1)}, u32[]{:S(2)}, u32[]{:S(2)}) collective-permute-start(bf16[2,512,256]{2,1,0:T(8,128)(2,1)S(1)} %get-tuple-element.51), channel_id=1, source_target_pairs={{0,2},{1,3},{2,0},{3,1},{4,6},{5,7},{6,4},{7,5},{8,10},{9,11},{10,... | collective-permute-start | bytes 1572872 | tf_op jit(solution)/shard_map/ppermute | solution.py:510
  38.4 3.9 %collective-permute-start.13 = (bf16[2,512,256]{2,1,0:T(8,128)(2,1)S(1)}, bf16[2,512,256]{2,1,0:T(8,128)(2,1)S(1)}, u32[]{:S(2)}, u32[]{:S(2)}) collective-permute-start(bf16[2,512,256]{2,1,0:T(8,128)(2,1)S(1)} %get-tuple-element.44.refs_14_), channel_id=1, source_target_pairs={{0,8},{1,9},{2,10},{3,11},{4,12},{5,13},{6,14},{7,15},{8,0},{9,1},... | collective-permute-start | bytes 1572872 | tf_op jit(solution)/shard_map/ppermute | solution.py:425
  42.3 0.0 collective-permute-done.1.refs_5_
  42.3 1.0 %collective-permute-start.14 = (bf16[2,512,256]{2,1,0:T(8,128)(2,1)S(1)}, bf16[2,512,256]{2,1,0:T(8,128)(2,1)S(1)}, u32[]{:S(2)}, u32[]{:S(2)}) collective-permute-start(bf16[2,512,256]{2,1,0:T(8,128)(2,1)S(1)} %get-tuple-element.47), channel_id=1, source_target_pairs={{0,4},{1,5},{2,6},{3,7},{4,8},{5,9},{6,10},{7,11},{8,12},{9,13},{1... | collective-permute-start | bytes 1572872 | tf_op jit(solution)/shard_map/ppermute | solution.py:425
  43.3 0.0 collective-permute-done.12.refs_7_
  43.3 2.2 %collective-permute-start.15 = (bf16[2,512,256]{2,1,0:T(8,128)(2,1)S(1)}, bf16[2,512,256]{2,1,0:T(8,128)(2,1)S(1)}, u32[]{:S(2)}, u32[]{:S(2)}) collective-permute-start(bf16[2,512,256]{2,1,0:T(8,128)(2,1)S(1)} %get-tuple-element.48), channel_id=1, source_target_pairs={{0,12},{1,13},{2,14},{3,15},{4,0},{5,1},{6,2},{7,3},{8,4},{9,5},{1... | collective-permute-start | bytes 1572872 | tf_op jit(solution)/shard_map/ppermute | solution.py:425
  45.6 0.0 copy-done.1
  45.6 6.5 %shard_map.146 = (bf16[512,512]{1,0:T(8,128)(2,1)}, bf16[6,1024,256]{2,1,0:T(8,128)(2,1)S(1)}, f32[4,512,256]{2,1,0:T(8,128)S(1)}) custom-call(s32[24]{0:T(128)S(1)} %stack.95.refs_0_, bf16[512,512]{1,0:T(8,128)(2,1)S(1)} %copy-done.1, bf16[512,128]{1,0:T(8,128)(2,1)S(1)} %get-tuple-element.29.refs_2_, bf16[512,128]{1,0:T(8,128)(2,1)S(1)} %get-tuple-element.30.refs_3_, ...), custom_call_target="tpu_custom_call" | custom-call | flops 100000 | tf_op jit(solution)/shard_map/pallas_call | solution.py:48
  52.1 0.0 collective-permute-done.16.refs_2_.refs_9_
  52.1 0.6 shard_map.147.refs_5_.refs_3_
  52.7 3.0 %collective-permute-start.18 = (bf16[544,256]{1,0:T(8,128)(2,1)S(1)}, bf16[544,256]{1,0:T(8,128)(2,1)S(1)}, u32[]{:S(2)}, u32[]{:S(2)}) collective-permute-start(bf16[544,256]{1,0:T(8,128)(2,1)S(1)} %shard_map.147.refs_5_.refs_3_), channel_id=1, source_target_pairs={{0,8},{1,9},{2,10},{3,11},{4,12},{5,13},{6,14},{7,15},{8,0},{9,1},... | collective-permute-start | bytes 835592 | tf_op jit(solution)/shard_map/ppermute | solution.py:425
  55.7 5.8 %collective-permute-done.19.refs_2_ = bf16[2,512,256]{2,1,0:T(8,128)(2,1)S(1)} collective-permute-done((bf16[2,512,256]{2,1,0:T(8,128)(2,1)S(1)}, bf16[2,512,256]{2,1,0:T(8,128)(2,1)S(1)}, u32[]{:S(2)}, u32[]{:S(2)}) %collective-permute-start.19) | collective-permute-done | bytes 524320 | tf_op jit(solution)/shard_map/ppermute | solution.py:510
  61.6 0.6 shard_map.150
  62.2 2.0 %collective-permute-start.20 = (bf16[512,256]{1,0:T(8,128)(2,1)S(1)}, bf16[512,256]{1,0:T(8,128)(2,1)S(1)}, u32[]{:S(2)}, u32[]{:S(2)}) collective-permute-start(bf16[512,256]{1,0:T(8,128)(2,1)S(1)} %get-tuple-element.52), channel_id=1, source_target_pairs={{0,4},{1,5},{2,6},{3,7},{4,8},{5,9},{6,10},{7,11},{8,12},{9,13},{1... | collective-permute-start | bytes 786440 | tf_op jit(solution)/shard_map/ppermute | solution.py:425
  64.2 0.0 collective-permute-done.13.refs_2_.refs_6_
  64.2 2.2 %collective-permute-start.21 = (bf16[512,256]{1,0:T(8,128)(2,1)S(1)}, bf16[512,256]{1,0:T(8,128)(2,1)S(1)}, u32[]{:S(2)}, u32[]{:S(2)}) collective-permute-start(bf16[512,256]{1,0:T(8,128)(2,1)S(1)} %get-tuple-element.53), channel_id=1, source_target_pairs={{0,12},{1,13},{2,14},{3,15},{4,0},{5,1},{6,2},{7,3},{8,4},{9,5},{1... | collective-permute-start | bytes 786440 | tf_op jit(solution)/shard_map/ppermute | solution.py:425
  66.4 0.0 collective-permute-done.14.refs_3_.refs_7_
  66.4 1.0 %collective-permute-done.15.refs_4_.refs_8_ = bf16[2,512,256]{2,1,0:T(8,128)(2,1)S(1)} collective-permute-done((bf16[2,512,256]{2,1,0:T(8,128)(2,1)S(1)}, bf16[2,512,256]{2,1,0:T(8,128)(2,1)S(1)}, u32[]{:S(2)}, u32[]{:S(2)}) %collective-permute-start.15) | collective-permute-done | bytes 524320 | tf_op jit(solution)/shard_map/ppermute | solution.py:425
  67.5 0.7 shard_map.148.refs_10_
  68.1 2.8 %collective-permute-start.17 = (bf16[512,256]{1,0:T(8,128)(2,1)S(1)}, bf16[512,256]{1,0:T(8,128)(2,1)S(1)}, u32[]{:S(2)}, u32[]{:S(2)}) collective-permute-start(bf16[512,256]{1,0:T(8,128)(2,1)S(1)} %shard_map.148.refs_10_), channel_id=1, source_target_pairs={{0,2},{1,3},{2,0},{3,1},{4,6},{5,7},{6,4},{7,5},{8,10},{9,11},{10,... | collective-permute-start | bytes 786440 | tf_op jit(solution)/shard_map/ppermute | solution.py:556
  70.9 1.2 %shard_map.149.refs_1_ = f32[512,512]{1,0:T(8,128)S(1)} custom-call(s32[24]{0:T(128)S(1)} %stack.95.refs_0_, bf16[512,256]{1,0:T(8,128)(2,1)S(1)} %get-tuple-element.40.refs_3_.refs_1_.refs_8_, bf16[512,256]{1,0:T(8,128)(2,1)S(1)} %get-tuple-element.41.refs_2_.refs_9_, bf16[512,256]{1,0:T(8,128)(2,1)S(1)} %collective-permute-done.9.refs_3_.refs_10_, ...), custom_call_target="tpu_custom_call" | custom-call | flops 100000 | tf_op jit(solution)/shard_map/pallas_call | solution.py:48
  72.2 4.6 %collective-permute-done.20.refs_4_ = bf16[512,256]{1,0:T(8,128)(2,1)S(1)} collective-permute-done((bf16[512,256]{1,0:T(8,128)(2,1)S(1)}, bf16[512,256]{1,0:T(8,128)(2,1)S(1)}, u32[]{:S(2)}, u32[]{:S(2)}) %collective-permute-start.20) | collective-permute-done | bytes 262176 | tf_op jit(solution)/shard_map/ppermute | solution.py:425
  76.8 0.8 collective-permute-done.21.refs_5_
  77.6 0.0 collective-permute-done.17.refs_2_
  77.6 0.0 collective-permute-done.18.refs_3_
  77.6 1.5 %shard_map.151 = bf16[512,512]{1,0:T(8,128)(2,1)} custom-call(s32[24]{0:T(128)S(1)} %stack.95.refs_0_, f32[512,512]{1,0:T(8,128)S(1)} %shard_map.149.refs_1_, bf16[512,256]{1,0:T(8,128)(2,1)S(1)} %collective-permute-done.17.refs_2_, bf16[544,256]{1,0:T(8,128)(2,1)S(1)} %collective-permute-done.18.refs_3_, ...), custom_call_target="tpu_custom_call" | custom-call | flops 100000 | tf_op jit(solution)/shard_map/pallas_call | solution.py:48
Async XLA Ops:
  0.6 23.4 %copy-start = (bf16[512,512]{1,0:T(8,128)(2,1)S(1)}, bf16[512,512]{1,0:T(8,128)(2,1)}, u32[]{:S(2)}) copy-start(bf16[512,512]{1,0:T(8,128)(2,1)} %refs_2_.5) | copy-start | bytes 1572868
  0.6 23.4 %copy-start.2 = (bf16[512,512]{1,0:T(8,128)(2,1)S(1)}, bf16[512,512]{1,0:T(8,128)(2,1)}, u32[]{:S(2)}) copy-start(bf16[512,512]{1,0:T(8,128)(2,1)} %refs_4_.3) | copy-start | bytes 1572868
  0.7 25.2 %collective-permute-start.11 = (bf16[512,8192]{1,0:T(8,128)(2,1)}, bf16[512,8192]{1,0:T(8,128)(2,1)}, u32[]{:S(2)}, u32[]{:S(2)}) collective-permute-start(bf16[512,8192]{1,0:T(8,128)(2,1)} %refs_12_.1), channel_id=1, source_target_pairs={{0,1},{1,0},{2,3},{3,2},{4,5},{5,4},{6,7},{7,6},{8,9},{9,8},{10,11... | collective-permute-start | bytes 25165832 | tf_op jit(solution)/shard_map/ppermute | solution.py:422
  5.1 11.0 %collective-permute-start.2 = (bf16[544,128]{1,0:T(8,128)(2,1)S(1)}, bf16[544,128]{1,0:T(8,128)(2,1)S(1)}, u32[]{:S(2)}, u32[]{:S(2)}) collective-permute-start(bf16[544,128]{1,0:T(8,128)(2,1)S(1)} %get-tuple-element.32.refs_1_), channel_id=1, source_target_pairs={{0,16},{16,32},{32,48},{48,0},{64,80},{80,96},{96,112},{112,64},{1... | collective-permute-start | bytes 417800 | tf_op jit(solution)/shard_map/ppermute | solution.py:424
  6.8 9.7 %collective-permute-start.3 = (bf16[544,128]{1,0:T(8,128)(2,1)S(1)}, bf16[544,128]{1,0:T(8,128)(2,1)S(1)}, u32[]{:S(2)}, u32[]{:S(2)}) collective-permute-start(bf16[544,128]{1,0:T(8,128)(2,1)S(1)} %get-tuple-element.32.refs_1_), channel_id=1, source_target_pairs={{0,32},{16,48},{32,0},{48,16},{64,96},{80,112},{96,64},{112,80},{1... | collective-permute-start | bytes 417800 | tf_op jit(solution)/shard_map/ppermute | solution.py:424
  9.7 6.8 %collective-permute-start.4 = (bf16[544,128]{1,0:T(8,128)(2,1)S(1)}, bf16[544,128]{1,0:T(8,128)(2,1)S(1)}, u32[]{:S(2)}, u32[]{:S(2)}) collective-permute-start(bf16[544,128]{1,0:T(8,128)(2,1)S(1)} %get-tuple-element.32.refs_1_), channel_id=1, source_target_pairs={{0,48},{16,0},{32,16},{48,32},{64,112},{80,64},{96,80},{112,96},{1... | collective-permute-start | bytes 417800 | tf_op jit(solution)/shard_map/ppermute | solution.py:424
  11.0 5.0 %collective-permute-start = (bf16[512,128]{1,0:T(8,128)(2,1)S(1)}, bf16[512,128]{1,0:T(8,128)(2,1)S(1)}, u32[]{:S(2)}, u32[]{:S(2)}) collective-permute-start(bf16[512,128]{1,0:T(8,128)(2,1)S(1)} %get-tuple-element.31.refs_5_), channel_id=1, source_target_pairs={{0,64},{16,80},{32,96},{48,112},{64,0},{80,16},{96,32},{112,48},{1... | collective-permute-start | bytes 393224 | tf_op jit(solution)/shard_map/ppermute | solution.py:423
  17.3 6.8 %collective-permute-start.8 = (bf16[544,128]{1,0:T(8,128)(2,1)S(1)}, bf16[544,128]{1,0:T(8,128)(2,1)S(1)}, u32[]{:S(2)}, u32[]{:S(2)}) collective-permute-start(bf16[544,128]{1,0:T(8,128)(2,1)S(1)} %get-tuple-element.39.refs_7_), channel_id=1, source_target_pairs={{0,64},{16,80},{32,96},{48,112},{64,0},{80,16},{96,32},{112,48},{1... | collective-permute-start | bytes 417800 | tf_op jit(solution)/shard_map/ppermute | solution.py:423
  18.9 14.2 %collective-permute-start.5 = (bf16[1024,128]{1,0:T(8,128)(2,1)S(1)}, bf16[1024,128]{1,0:T(8,128)(2,1)S(1)}, u32[]{:S(2)}, u32[]{:S(2)}) collective-permute-start(bf16[1024,128]{1,0:T(8,128)(2,1)S(1)} %get-tuple-element.36), channel_id=1, source_target_pairs={{0,16},{16,32},{32,48},{48,0},{64,80},{80,96},{96,112},{112,64},{1... | collective-permute-start | bytes 786440 | tf_op jit(solution)/shard_map/ppermute | solution.py:424
  20.1 13.6 %collective-permute-start.6 = (bf16[1024,128]{1,0:T(8,128)(2,1)S(1)}, bf16[1024,128]{1,0:T(8,128)(2,1)S(1)}, u32[]{:S(2)}, u32[]{:S(2)}) collective-permute-start(bf16[1024,128]{1,0:T(8,128)(2,1)S(1)} %get-tuple-element.36), channel_id=1, source_target_pairs={{0,32},{16,48},{32,0},{48,16},{64,96},{80,112},{96,64},{112,80},{1... | collective-permute-start | bytes 786440 | tf_op jit(solution)/shard_map/ppermute | solution.py:424
  22.5 11.3 %collective-permute-start.7 = (bf16[1024,128]{1,0:T(8,128)(2,1)S(1)}, bf16[1024,128]{1,0:T(8,128)(2,1)S(1)}, u32[]{:S(2)}, u32[]{:S(2)}) collective-permute-start(bf16[1024,128]{1,0:T(8,128)(2,1)S(1)} %get-tuple-element.36), channel_id=1, source_target_pairs={{0,48},{16,0},{32,16},{48,32},{64,112},{80,64},{96,80},{112,96},{1... | collective-permute-start | bytes 786440 | tf_op jit(solution)/shard_map/ppermute | solution.py:424
  25.9 3.8 %collective-permute-start.10 = (bf16[512,256]{1,0:T(8,128)(2,1)S(1)}, bf16[512,256]{1,0:T(8,128)(2,1)S(1)}, u32[]{:S(2)}, u32[]{:S(2)}) collective-permute-start(bf16[512,256]{1,0:T(8,128)(2,1)S(1)} %get-tuple-element.41.refs_2_.refs_9_), channel_id=1, source_target_pairs={{0,1},{1,0},{2,3},{3,2},{4,5},{5,4},{6,7},{7,6},{8,9},{9,8},{10,11... | collective-permute-start | bytes 786440 | tf_op jit(solution)/shard_map/ppermute | solution.py:422
  25.9 3.8 %collective-permute-start.9 = (bf16[512,256]{1,0:T(8,128)(2,1)S(1)}, bf16[512,256]{1,0:T(8,128)(2,1)S(1)}, u32[]{:S(2)}, u32[]{:S(2)}) collective-permute-start(bf16[512,256]{1,0:T(8,128)(2,1)S(1)} %get-tuple-element.40.refs_3_.refs_1_.refs_8_), channel_id=1, source_target_pairs={{0,1},{1,0},{2,3},{3,2},{4,5},{5,4},{6,7},{7,6},{8,9},{9,8},{10,11... | collective-permute-start | bytes 786440 | tf_op jit(solution)/shard_map/ppermute | solution.py:422
  29.6 15.9 %copy-start.1 = (bf16[512,512]{1,0:T(8,128)(2,1)S(1)}, bf16[512,512]{1,0:T(8,128)(2,1)}, u32[]{:S(2)}) copy-start(bf16[512,512]{1,0:T(8,128)(2,1)} %refs_1_.5) | copy-start | bytes 1572868
  34.3 9.0 %collective-permute-start.12 = (bf16[3,1024,128]{2,1,0:T(8,128)(2,1)S(1)}, bf16[3,1024,128]{2,1,0:T(8,128)(2,1)S(1)}, u32[]{:S(2)}, u32[]{:S(2)}) collective-permute-start(bf16[3,1024,128]{2,1,0:T(8,128)(2,1)S(1)} %get-tuple-element.43.refs_6_), channel_id=1, source_target_pairs={{0,1},{1,0},{2,3},{3,2},{4,5},{5,4},{6,7},{7,6},{8,9},{9,8},{10,11... | collective-permute-start | bytes 2359304 | tf_op jit(solution)/shard_map/ppermute | solution.py:422
  34.4 7.9 %collective-permute-start.1 = (bf16[512,128]{1,0:T(8,128)(2,1)S(1)}, bf16[512,128]{1,0:T(8,128)(2,1)S(1)}, u32[]{:S(2)}, u32[]{:S(2)}) collective-permute-start(bf16[512,128]{1,0:T(8,128)(2,1)S(1)} %collective-permute-done.refs_6_.refs_4_), channel_id=1, source_target_pairs={{0,1},{1,0},{2,3},{3,2},{4,5},{5,4},{6,7},{7,6},{8,9},{9,8},{10,11... | collective-permute-start | bytes 393224 | tf_op jit(solution)/shard_map/ppermute | solution.py:422
  34.9 17.2 %collective-permute-start.16 = (bf16[2,512,256]{2,1,0:T(8,128)(2,1)S(1)}, bf16[2,512,256]{2,1,0:T(8,128)(2,1)S(1)}, u32[]{:S(2)}, u32[]{:S(2)}) collective-permute-start(bf16[2,512,256]{2,1,0:T(8,128)(2,1)S(1)} %get-tuple-element.49), channel_id=1, source_target_pairs={{0,2},{1,3},{2,0},{3,1},{4,6},{5,7},{6,4},{7,5},{8,10},{9,11},{10,... | collective-permute-start | bytes 1572872 | tf_op jit(solution)/shard_map/ppermute | solution.py:510
  37.6 23.9 %collective-permute-start.19 = (bf16[2,512,256]{2,1,0:T(8,128)(2,1)S(1)}, bf16[2,512,256]{2,1,0:T(8,128)(2,1)S(1)}, u32[]{:S(2)}, u32[]{:S(2)}) collective-permute-start(bf16[2,512,256]{2,1,0:T(8,128)(2,1)S(1)} %get-tuple-element.51), channel_id=1, source_target_pairs={{0,2},{1,3},{2,0},{3,1},{4,6},{5,7},{6,4},{7,5},{8,10},{9,11},{10,... | collective-permute-start | bytes 1572872 | tf_op jit(solution)/shard_map/ppermute | solution.py:510
  38.4 25.7 %collective-permute-start.13 = (bf16[2,512,256]{2,1,0:T(8,128)(2,1)S(1)}, bf16[2,512,256]{2,1,0:T(8,128)(2,1)S(1)}, u32[]{:S(2)}, u32[]{:S(2)}) collective-permute-start(bf16[2,512,256]{2,1,0:T(8,128)(2,1)S(1)} %get-tuple-element.44.refs_14_), channel_id=1, source_target_pairs={{0,8},{1,9},{2,10},{3,11},{4,12},{5,13},{6,14},{7,15},{8,0},{9,1},... | collective-permute-start | bytes 1572872 | tf_op jit(solution)/shard_map/ppermute | solution.py:425
  42.3 24.1 %collective-permute-start.14 = (bf16[2,512,256]{2,1,0:T(8,128)(2,1)S(1)}, bf16[2,512,256]{2,1,0:T(8,128)(2,1)S(1)}, u32[]{:S(2)}, u32[]{:S(2)}) collective-permute-start(bf16[2,512,256]{2,1,0:T(8,128)(2,1)S(1)} %get-tuple-element.47), channel_id=1, source_target_pairs={{0,4},{1,5},{2,6},{3,7},{4,8},{5,9},{6,10},{7,11},{8,12},{9,13},{1... | collective-permute-start | bytes 1572872 | tf_op jit(solution)/shard_map/ppermute | solution.py:425
  43.3 24.1 %collective-permute-start.15 = (bf16[2,512,256]{2,1,0:T(8,128)(2,1)S(1)}, bf16[2,512,256]{2,1,0:T(8,128)(2,1)S(1)}, u32[]{:S(2)}, u32[]{:S(2)}) collective-permute-start(bf16[2,512,256]{2,1,0:T(8,128)(2,1)S(1)} %get-tuple-element.48), channel_id=1, source_target_pairs={{0,12},{1,13},{2,14},{3,15},{4,0},{5,1},{6,2},{7,3},{8,4},{9,5},{1... | collective-permute-start | bytes 1572872 | tf_op jit(solution)/shard_map/ppermute | solution.py:425
  52.7 24.9 %collective-permute-start.18 = (bf16[544,256]{1,0:T(8,128)(2,1)S(1)}, bf16[544,256]{1,0:T(8,128)(2,1)S(1)}, u32[]{:S(2)}, u32[]{:S(2)}) collective-permute-start(bf16[544,256]{1,0:T(8,128)(2,1)S(1)} %shard_map.147.refs_5_.refs_3_), channel_id=1, source_target_pairs={{0,8},{1,9},{2,10},{3,11},{4,12},{5,13},{6,14},{7,15},{8,0},{9,1},... | collective-permute-start | bytes 835592 | tf_op jit(solution)/shard_map/ppermute | solution.py:425
  62.2 14.6 %collective-permute-start.20 = (bf16[512,256]{1,0:T(8,128)(2,1)S(1)}, bf16[512,256]{1,0:T(8,128)(2,1)S(1)}, u32[]{:S(2)}, u32[]{:S(2)}) collective-permute-start(bf16[512,256]{1,0:T(8,128)(2,1)S(1)} %get-tuple-element.52), channel_id=1, source_target_pairs={{0,4},{1,5},{2,6},{3,7},{4,8},{5,9},{6,10},{7,11},{8,12},{9,13},{1... | collective-permute-start | bytes 786440 | tf_op jit(solution)/shard_map/ppermute | solution.py:425
  64.2 13.4 %collective-permute-start.21 = (bf16[512,256]{1,0:T(8,128)(2,1)S(1)}, bf16[512,256]{1,0:T(8,128)(2,1)S(1)}, u32[]{:S(2)}, u32[]{:S(2)}) collective-permute-start(bf16[512,256]{1,0:T(8,128)(2,1)S(1)} %get-tuple-element.53), channel_id=1, source_target_pairs={{0,12},{1,13},{2,14},{3,15},{4,0},{5,1},{6,2},{7,3},{8,4},{9,5},{1... | collective-permute-start | bytes 786440 | tf_op jit(solution)/shard_map/ppermute | solution.py:425
  68.1 9.5 %collective-permute-start.17 = (bf16[512,256]{1,0:T(8,128)(2,1)S(1)}, bf16[512,256]{1,0:T(8,128)(2,1)S(1)}, u32[]{:S(2)}, u32[]{:S(2)}) collective-permute-start(bf16[512,256]{1,0:T(8,128)(2,1)S(1)} %shard_map.148.refs_10_), channel_id=1, source_target_pairs={{0,2},{1,3},{2,0},{3,1},{4,6},{5,7},{6,4},{7,5},{8,10},{9,11},{10,... | collective-permute-start | bytes 786440 | tf_op jit(solution)/shard_map/ppermute | solution.py:556

commit v7 on v5

--- a/solution.py
+++ b/solution.py
@@ -26,7 +26,21 @@
 NT = (((1,), (1,)), ((), ()))
 VMEM_LIMIT = 16 * 1024 * 1024
 
-SEQ, CORE, GROUP, LENGTH, YPOS, XLO, ZPOS, XHI, COLUMNS = range(9)
+SEQ, CORE, GROUP, LENGTH, YPOS, XLO, ZPOS, XHI = range(8)
+
+
+class Places:
+    def __init__(self, ref):
+        self.ref = ref
+
+    def __getitem__(self, which):
+        if which == LENGTH:
+            return self.ref[2]
+        if which in (SEQ, YPOS, XLO):
+            seq = self.ref[0]
+            return {SEQ: seq, YPOS: seq & 3, XLO: seq >> 2}[which]
+        head = self.ref[1]
+        return {CORE: head & 1, GROUP: head >> 1, ZPOS: head >> 2, XHI: (head >> 1) & 1}[which]
 
 
 def call(kernel, info, args, in_specs, out_specs, out_shape, grid=(1,), scratch=(), flops=0, nbytes=0, trans=0, extra=(), after=(), limit=VMEM_LIMIT, alias=None):
@@ -34,7 +48,7 @@
     first = scalars + len(args)
 
     def run(*refs):
-        kernel(*refs[:first], *refs[first + len(after) :])
+        kernel(Places(refs[0]), *refs[1:first], *refs[first + len(after) :])
 
     aliases = {} if alias is None else {first + alias: 0}
 
@@ -299,10 +313,27 @@
         ready_ref[2 * i + 1] = acc[:, CB : 2 * CB]
 
 
+def column_block(info, k):
+    z, x = info[ZPOS], info[XHI]
+
+    def block(zz, xx, half):
+        return ((zz & 3) << 3) + ((xx & 1) << 2) + (info[CORE] << 1) + half
+
+    if k < 4:
+        return block(k, x + 1, 1)
+    if k < 10:
+        return block(z + (k - 2) // 2, k % 2, 0)
+    if k == 10:
+        return block(z, x + 1, 0)
+    if k < 14:
+        return block(z + k - 10, x, 1)
+    return block(z, x, k - 14)
+
+
 def weight_copies(info, near, far, out_ref, sems, first, n):
     copies = []
     for k in range(n):
-        part = pl.ds(pl.multiple_of(info[COLUMNS + first + k] * CB, CB), CB)
+        part = pl.ds(pl.multiple_of(column_block(info, first + k) * CB, CB), CB)
         copies += [
             pltpu.make_async_copy(near.at[:, part], out_ref.at[k, 0:TOK, :], sems.at[0, k]),
             pltpu.make_async_copy(far.at[:, part], out_ref.at[k, TOK : 2 * TOK, :], sems.at[1, k]),
@@ -404,16 +435,7 @@
 ):
     seq = lax.axis_index("seq")
     head = lax.axis_index("head")
-    z, x, c = head // 4, (head // 2) % 2, head % 2
-    block = lambda zz, xx, half: ((zz % 4) * 4 + (xx % 2) * 2 + c) * 2 + half
-    columns = (
-        [block(i, x + 1, 1) for i in range(4)]
-        + [block(z + d, i, 0) for d in (1, 2, 3) for i in range(2)]
-        + [block(z, x + 1, 0)]
-        + [block(z + d, x, 1) for d in (1, 2, 3)]
-        + [block(z, x, 0), block(z, x, 1)]
-    )
-    info = jnp.stack([seq, c, head // 2, length[0], seq % 4, seq // 4, z, x, *columns]).astype(jnp.int32)
+    info = jnp.stack([seq, head, length[0]]).astype(jnp.int32)
     core = lambda a: lax.ppermute(a, "head", CORE_SWAP)
     lo = lambda a: lax.ppermute(a, "seq", LO_SWAP)
     along_y = lambda a, d: lax.ppermute(a, "seq", Y_MOVE[d])

time: 79.3 us -> 79.3 us (level)
  no operation moved by 1% of the time
where the time goes in v7:
time: 79.3 us; the launch traced here: 78.3 us
  starting transfers between devices  33.7 us (42%)
  Pallas kernels  27.1 us (34%)
  waiting for transfers between devices  16 us (20%)
  between operations  1.5 us (2%)
    pallas_call x12, Pallas kernels, call(): pl.pallas_call(run, grid_spec=spec, out_shape=out_shape, input_output_ali...  27.1 us
    ppermute x6, starting transfers between devices, body(): along_z = lambda a, d: lax.ppermute(a, 'head', Z_MOVE[d])  14.3 us
    ppermute x6, starting transfers between devices, body(): along_y = lambda a, d: lax.ppermute(a, 'seq', Y_MOVE[d])  11.2 us
    ppermute x1, waiting for transfers between devices, body(): from_x = lax.ppermute(to_x, 'head', X_SWAP)  8.74 us
    ppermute x2, starting transfers between devices, body(): lo = lambda a: lax.ppermute(a, 'seq', LO_SWAP)  3.07 us
    ppermute x1, waiting for transfers between devices, body(): from_x2 = lax.ppermute(to_x2, 'head', X_SWAP)  2.99 us
    ppermute x1, starting transfers between devices, body(): from_x = lax.ppermute(to_x, 'head', X_SWAP)  2.79 us
    ppermute x6, waiting for transfers between devices, body(): along_z = lambda a, d: lax.ppermute(a, 'head', Z_MOVE[d])  2.64 us
  transfers between devices with their start and end apart: 21, of which 10 were waited for; matrix products, arithmetic and copies ran while one was open for 0% of the time, Pallas kernels for 32%

profile of v7, /device:TPU:0, one launch (start us, length us, event | category | flops | bytes accessed | tf_op | source)
XLA Modules:
  0.0 78.3 jit_solution(7020099082739239762)
XLA Ops:
  0.6 0.0 copy-start
  0.6 0.0 copy-start.2
  0.7 0.1 collective-permute-start.11
  1.5 0.1 pad_add_fusion.refs_0_
  1.5 3.2 %shard_map.139 = (bf16[512,128]{1,0:T(8,128)(2,1)S(1)}, bf16[512,128]{1,0:T(8,128)(2,1)S(1)}, bf16[512,128]{1,0:T(8,128)(2,1)S(1)}, bf16[544,128]{1,0:T(8,128)(2...) custom-call(s32[3]{0:T(128)S(1)} %pad_add_fusion.refs_0_, ...), custom_call_target="tpu_custom_call" | custom-call | flops 100000 | tf_op jit(solution)/shard_map/pallas_call | solution.py:62
  4.8 1.7 %collective-permute-start.2 = (bf16[544,128]{1,0:T(8,128)(2,1)S(1)}, bf16[544,128]{1,0:T(8,128)(2,1)S(1)}, u32[]{:S(2)}, u32[]{:S(2)}) collective-permute-start(bf16[544,128]{1,0:T(8,128)(2,1)S(1)} %get-tuple-element.32.refs_1_), channel_id=1, source_target_pairs={{0,16},{16,32},{32,48},{48,0},{64,80},{80,96},{96,112},{112,64},{1... | collective-permute-start | bytes 417800 | tf_op jit(solution)/shard_map/ppermute | solution.py:441
  6.5 2.9 %collective-permute-start.3 = (bf16[544,128]{1,0:T(8,128)(2,1)S(1)}, bf16[544,128]{1,0:T(8,128)(2,1)S(1)}, u32[]{:S(2)}, u32[]{:S(2)}) collective-permute-start(bf16[544,128]{1,0:T(8,128)(2,1)S(1)} %get-tuple-element.32.refs_1_), channel_id=1, source_target_pairs={{0,32},{16,48},{32,0},{48,16},{64,96},{80,112},{96,64},{112,80},{1... | collective-permute-start | bytes 417800 | tf_op jit(solution)/shard_map/ppermute | solution.py:441
  9.4 1.3 %collective-permute-start.4 = (bf16[544,128]{1,0:T(8,128)(2,1)S(1)}, bf16[544,128]{1,0:T(8,128)(2,1)S(1)}, u32[]{:S(2)}, u32[]{:S(2)}) collective-permute-start(bf16[544,128]{1,0:T(8,128)(2,1)S(1)} %get-tuple-element.32.refs_1_), channel_id=1, source_target_pairs={{0,48},{16,0},{32,16},{48,32},{64,112},{80,64},{96,80},{112,96},{1... | collective-permute-start | bytes 417800 | tf_op jit(solution)/shard_map/ppermute | solution.py:441
  10.7 1.5 %collective-permute-start = (bf16[512,128]{1,0:T(8,128)(2,1)S(1)}, bf16[512,128]{1,0:T(8,128)(2,1)S(1)}, u32[]{:S(2)}, u32[]{:S(2)}) collective-permute-start(bf16[512,128]{1,0:T(8,128)(2,1)S(1)} %get-tuple-element.31.refs_5_), channel_id=1, source_target_pairs={{0,64},{16,80},{32,96},{48,112},{64,0},{80,16},{96,32},{112,48},{1... | collective-permute-start | bytes 393224 | tf_op jit(solution)/shard_map/ppermute | solution.py:440
  12.2 3.3 %shard_map.140.refs_7_.refs_3_ = f32[512,512]{1,0:T(8,128)S(1)} custom-call(s32[3]{0:T(128)S(1)} %pad_add_fusion.refs_0_, f32[16,512]{1,0:T(8,128)S(1)} %get-tuple-element.33.refs_1_, bf16[512,512]{1,0:T(8,128)(2,1)} %refs_2_.5, bf16[512,128]{1,0:T(8,128)(2,1)S(1)} %get-tuple-element.34.refs_3_, bf16[512,128]{1,0:T(8,128)(2,1)S(1)} %get-tuple-element.35.refs_4_, ...), custom_call_target="tpu_custom_call" | custom-call | flops 100000 | tf_op jit(solution)/shard_map/pallas_call | solution.py:62
  15.5 0.2 collective-permute-done.refs_6_.refs_4_
  15.7 0.0 collective-permute-done.2.refs_2_
  15.7 0.6 collective-permute-done.3.refs_3_
  16.4 0.0 collective-permute-done.4.refs_4_
  16.4 0.8 shard_map.141
  17.1 1.6 %collective-permute-start.8 = (bf16[544,128]{1,0:T(8,128)(2,1)S(1)}, bf16[544,128]{1,0:T(8,128)(2,1)S(1)}, u32[]{:S(2)}, u32[]{:S(2)}) collective-permute-start(bf16[544,128]{1,0:T(8,128)(2,1)S(1)} %get-tuple-element.39.refs_7_), channel_id=1, source_target_pairs={{0,64},{16,80},{32,96},{48,112},{64,0},{80,16},{96,32},{112,48},{1... | collective-permute-start | bytes 417800 | tf_op jit(solution)/shard_map/ppermute | solution.py:440
  18.7 1.2 %collective-permute-start.5 = (bf16[1024,128]{1,0:T(8,128)(2,1)S(1)}, bf16[1024,128]{1,0:T(8,128)(2,1)S(1)}, u32[]{:S(2)}, u32[]{:S(2)}) collective-permute-start(bf16[1024,128]{1,0:T(8,128)(2,1)S(1)} %get-tuple-element.36), channel_id=1, source_target_pairs={{0,16},{16,32},{32,48},{48,0},{64,80},{80,96},{96,112},{112,64},{1... | collective-permute-start | bytes 786440 | tf_op jit(solution)/shard_map/ppermute | solution.py:441
  19.9 2.4 %collective-permute-start.6 = (bf16[1024,128]{1,0:T(8,128)(2,1)S(1)}, bf16[1024,128]{1,0:T(8,128)(2,1)S(1)}, u32[]{:S(2)}, u32[]{:S(2)}) collective-permute-start(bf16[1024,128]{1,0:T(8,128)(2,1)S(1)} %get-tuple-element.36), channel_id=1, source_target_pairs={{0,32},{16,48},{32,0},{48,16},{64,96},{80,112},{96,64},{112,80},{1... | collective-permute-start | bytes 786440 | tf_op jit(solution)/shard_map/ppermute | solution.py:441
  22.3 1.6 %collective-permute-start.7 = (bf16[1024,128]{1,0:T(8,128)(2,1)S(1)}, bf16[1024,128]{1,0:T(8,128)(2,1)S(1)}, u32[]{:S(2)}, u32[]{:S(2)}) collective-permute-start(bf16[1024,128]{1,0:T(8,128)(2,1)S(1)} %get-tuple-element.36), channel_id=1, source_target_pairs={{0,48},{16,0},{32,16},{48,32},{64,112},{80,64},{96,80},{112,96},{1... | collective-permute-start | bytes 786440 | tf_op jit(solution)/shard_map/ppermute | solution.py:441
  23.9 0.0 collective-permute-done.8.refs_8_
  23.9 0.0 copy-done
  23.9 0.0 copy-done.2
  23.9 1.8 %shard_map.142 = (bf16[512,256]{1,0:T(8,128)(2,1)S(1)}, bf16[512,256]{1,0:T(8,128)(2,1)S(1)}, f32[4,16,128]{2,1,0:T(8,128)}) custom-call(s32[3]{0:T(128)S(1)} %pad_add_fusion.refs_0_, f32[16,512]{1,0:T(8,128)S(1)} %get-tuple-element.33.refs_1_, bf16[512,512]{1,0:T(8,128)(2,1)S(1)} %copy-done, f32[512,512]{1,0:T(8,128)S(1)} %shard_map.140.refs_7_.refs_3_, ...), custom_call_target="tpu_custom_call" | custom-call | flops 100000 | tf_op jit(solution)/shard_map/pallas_call | solution.py:62
  25.7 0.0 collective-permute-start.10
  25.7 0.0 collective-permute-done.11.refs_2_.refs_13_
  25.7 0.5 collective-permute-start.9
  26.2 3.3 %shard_map.143.refs_5_ = bf16[10,1024,256]{2,1,0:T(8,128)(2,1)S(1)} custom-call(s32[3]{0:T(128)S(1)} %pad_add_fusion.refs_0_, bf16[512,8192]{1,0:T(8,128)(2,1)} %refs_12_.1, bf16[512,8192]{1,0:T(8,128)(2,1)} %collective-permute-done.11.refs_2_.refs_13_, bf16[512,256]{1,0:T(8,128)(2,1)S(1)} %get-tuple-element.40.refs_3_.refs_1_.refs_8_), custom_call_target="tpu_custom_call" | custom-call | flops 10000000000 | tf_op jit(solution)/shard_map/pallas_call | solution.py:62
  29.5 0.0 copy-start.1
  29.5 0.0 collective-permute-done.10.refs_4_.refs_11_
  29.5 0.0 collective-permute-done.9.refs_3_.refs_10_
  29.5 3.4 %shard_map.144 = (bf16[4,512,256]{2,1,0:T(8,128)(2,1)S(1)}, bf16[2,512,256]{2,1,0:T(8,128)(2,1)S(1)}, bf16[2,512,256]{2,1,0:T(8,128)(2,1)S(1)}, bf16[2,512,256]{2,1,0:T(8,128)(2,1)S(1)}) custom-call(s32[3]{0:T(128)S(1)} %pad_add_fusion.refs_0_, bf16[512,256]{1,0:T(8,128)(2,1)S(1)} %get-tuple-element.40.refs_3_.refs_1_.refs_8_, ...), custom_call_target="tpu_custom_call" | custom-call | flops 100000 | tf_op jit(solution)/shard_map/pallas_call | solution.py:62
  32.9 0.0 collective-permute-done.5.refs_1_
  32.9 0.7 collective-permute-done.6.refs_2_
  33.6 0.1 collective-permute-done.7.refs_3_
  33.7 0.6 shard_map.145
  34.3 2.8 %collective-permute-start.16 = (bf16[4,512,256]{2,1,0:T(8,128)(2,1)S(1)}, bf16[4,512,256]{2,1,0:T(8,128)(2,1)S(1)}, u32[]{:S(2)}, u32[]{:S(2)}) collective-permute-start(bf16[4,512,256]{2,1,0:T(8,128)(2,1)S(1)} %get-tuple-element.49), channel_id=1, source_target_pairs={{0,2},{1,3},{2,0},{3,1},{4,6},{5,7},{6,4},{7,5},{8,10},{9,11},{10,... | collective-permute-start | bytes 3145736 | tf_op jit(solution)/shard_map/ppermute | solution.py:527
  37.1 0.0 collective-permute-start.12
  37.1 0.5 collective-permute-start.1
  37.6 3.9 %collective-permute-start.13 = (bf16[2,512,256]{2,1,0:T(8,128)(2,1)S(1)}, bf16[2,512,256]{2,1,0:T(8,128)(2,1)S(1)}, u32[]{:S(2)}, u32[]{:S(2)}) collective-permute-start(bf16[2,512,256]{2,1,0:T(8,128)(2,1)S(1)} %get-tuple-element.44.refs_14_), channel_id=1, source_target_pairs={{0,8},{1,9},{2,10},{3,11},{4,12},{5,13},{6,14},{7,15},{8,0},{9,1},... | collective-permute-start | bytes 1572872 | tf_op jit(solution)/shard_map/ppermute | solution.py:442
  41.5 1.0 %collective-permute-start.14 = (bf16[2,512,256]{2,1,0:T(8,128)(2,1)S(1)}, bf16[2,512,256]{2,1,0:T(8,128)(2,1)S(1)}, u32[]{:S(2)}, u32[]{:S(2)}) collective-permute-start(bf16[2,512,256]{2,1,0:T(8,128)(2,1)S(1)} %get-tuple-element.47), channel_id=1, source_target_pairs={{0,4},{1,5},{2,6},{3,7},{4,8},{5,9},{6,10},{7,11},{8,12},{9,13},{1... | collective-permute-start | bytes 1572872 | tf_op jit(solution)/shard_map/ppermute | solution.py:442
  42.5 0.0 collective-permute-done.1.refs_5_
  42.5 2.2 %collective-permute-start.15 = (bf16[2,512,256]{2,1,0:T(8,128)(2,1)S(1)}, bf16[2,512,256]{2,1,0:T(8,128)(2,1)S(1)}, u32[]{:S(2)}, u32[]{:S(2)}) collective-permute-start(bf16[2,512,256]{2,1,0:T(8,128)(2,1)S(1)} %get-tuple-element.48), channel_id=1, source_target_pairs={{0,12},{1,13},{2,14},{3,15},{4,0},{5,1},{6,2},{7,3},{8,4},{9,5},{1... | collective-permute-start | bytes 1572872 | tf_op jit(solution)/shard_map/ppermute | solution.py:442
  44.8 0.0 collective-permute-done.12.refs_7_
  44.8 0.0 copy-done.1
  44.8 6.7 %shard_map.146 = (bf16[512,512]{1,0:T(8,128)(2,1)}, bf16[6,1024,256]{2,1,0:T(8,128)(2,1)S(1)}, f32[4,512,256]{2,1,0:T(8,128)S(1)}) custom-call(s32[3]{0:T(128)S(1)} %pad_add_fusion.refs_0_, bf16[512,512]{1,0:T(8,128)(2,1)S(1)} %copy-done.1, bf16[512,128]{1,0:T(8,128)(2,1)S(1)} %get-tuple-element.29.refs_2_, bf16[512,128]{1,0:T(8,128)(2,1)S(1)} %get-tuple-element.30.refs_3_, ...), custom_call_target="tpu_custom_call" | custom-call | flops 100000 | tf_op jit(solution)/shard_map/pallas_call | solution.py:62
  51.5 8.7 %collective-permute-done.16.refs_2_.refs_9_ = bf16[4,512,256]{2,1,0:T(8,128)(2,1)S(1)} collective-permute-done((bf16[4,512,256]{2,1,0:T(8,128)(2,1)S(1)}, bf16[4,512,256]{2,1,0:T(8,128)(2,1)S(1)}, u32[]{:S(2)}, u32[]{:S(2)}) %collective-permute-start.16) | collective-permute-done | bytes 1048608 | tf_op jit(solution)/shard_map/ppermute | solution.py:527
  60.2 0.7 shard_map.147
  60.9 4.0 %collective-permute-start.18 = (bf16[512,256]{1,0:T(8,128)(2,1)S(1)}, bf16[512,256]{1,0:T(8,128)(2,1)S(1)}, u32[]{:S(2)}, u32[]{:S(2)}) collective-permute-start(bf16[512,256]{1,0:T(8,128)(2,1)S(1)} %get-tuple-element.51.refs_5_), channel_id=1, source_target_pairs={{0,8},{1,9},{2,10},{3,11},{4,12},{5,13},{6,14},{7,15},{8,0},{9,1},... | collective-permute-start | bytes 786440 | tf_op jit(solution)/shard_map/ppermute | solution.py:442
  64.8 0.0 collective-permute-done.13.refs_2_.refs_6_
  64.9 0.6 collective-permute-done.14.refs_3_.refs_7_
  65.4 1.0 %collective-permute-done.15.refs_4_.refs_8_ = bf16[2,512,256]{2,1,0:T(8,128)(2,1)S(1)} collective-permute-done((bf16[2,512,256]{2,1,0:T(8,128)(2,1)S(1)}, bf16[2,512,256]{2,1,0:T(8,128)(2,1)S(1)}, u32[]{:S(2)}, u32[]{:S(2)}) %collective-permute-start.15) | collective-permute-done | bytes 524320 | tf_op jit(solution)/shard_map/ppermute | solution.py:442
  66.4 0.7 shard_map.148.refs_10_
  67.1 1.2 %collective-permute-start.17 = (bf16[512,256]{1,0:T(8,128)(2,1)S(1)}, bf16[512,256]{1,0:T(8,128)(2,1)S(1)}, u32[]{:S(2)}, u32[]{:S(2)}) collective-permute-start(bf16[512,256]{1,0:T(8,128)(2,1)S(1)} %shard_map.148.refs_10_), channel_id=1, source_target_pairs={{0,2},{1,3},{2,0},{3,1},{4,6},{5,7},{6,4},{7,5},{8,10},{9,11},{10,... | collective-permute-start | bytes 786440 | tf_op jit(solution)/shard_map/ppermute | solution.py:562
  68.3 1.0 %collective-permute-start.19 = (bf16[512,256]{1,0:T(8,128)(2,1)S(1)}, bf16[512,256]{1,0:T(8,128)(2,1)S(1)}, u32[]{:S(2)}, u32[]{:S(2)}) collective-permute-start(bf16[512,256]{1,0:T(8,128)(2,1)S(1)} %get-tuple-element.52), channel_id=1, source_target_pairs={{0,4},{1,5},{2,6},{3,7},{4,8},{5,9},{6,10},{7,11},{8,12},{9,13},{1... | collective-permute-start | bytes 786440 | tf_op jit(solution)/shard_map/ppermute | solution.py:442
  69.4 2.2 %collective-permute-start.20 = (bf16[512,256]{1,0:T(8,128)(2,1)S(1)}, bf16[512,256]{1,0:T(8,128)(2,1)S(1)}, u32[]{:S(2)}, u32[]{:S(2)}) collective-permute-start(bf16[512,256]{1,0:T(8,128)(2,1)S(1)} %get-tuple-element.53), channel_id=1, source_target_pairs={{0,12},{1,13},{2,14},{3,15},{4,0},{5,1},{6,2},{7,3},{8,4},{9,5},{1... | collective-permute-start | bytes 786440 | tf_op jit(solution)/shard_map/ppermute | solution.py:442
  71.6 1.2 %shard_map.149.refs_1_ = f32[512,512]{1,0:T(8,128)S(1)} custom-call(s32[3]{0:T(128)S(1)} %pad_add_fusion.refs_0_, bf16[512,256]{1,0:T(8,128)(2,1)S(1)} %get-tuple-element.40.refs_3_.refs_1_.refs_8_, bf16[512,256]{1,0:T(8,128)(2,1)S(1)} %get-tuple-element.41.refs_2_.refs_9_, bf16[512,256]{1,0:T(8,128)(2,1)S(1)} %collective-permute-done.9.refs_3_.refs_10_, ...), custom_call_target="tpu_custom_call" | custom-call | flops 100000 | tf_op jit(solution)/shard_map/pallas_call | solution.py:62
  72.8 3.0 %collective-permute-done.17.refs_2_ = bf16[512,256]{1,0:T(8,128)(2,1)S(1)} collective-permute-done((bf16[512,256]{1,0:T(8,128)(2,1)S(1)}, bf16[512,256]{1,0:T(8,128)(2,1)S(1)}, u32[]{:S(2)}, u32[]{:S(2)}) %collective-permute-start.17) | collective-permute-done | bytes 262176 | tf_op jit(solution)/shard_map/ppermute | solution.py:562
  75.8 0.0 collective-permute-done.18.refs_3_
  75.8 0.4 collective-permute-done.19.refs_4_
  76.2 0.6 collective-permute-done.20.refs_5_
  76.9 1.5 %shard_map.150 = bf16[512,512]{1,0:T(8,128)(2,1)} custom-call(s32[3]{0:T(128)S(1)} %pad_add_fusion.refs_0_, f32[512,512]{1,0:T(8,128)S(1)} %shard_map.149.refs_1_, bf16[512,256]{1,0:T(8,128)(2,1)S(1)} %collective-permute-done.17.refs_2_, bf16[512,256]{1,0:T(8,128)(2,1)S(1)} %collective-permute-done.18.refs_3_, ...), custom_call_target="tpu_custom_call" | custom-call | flops 100000 | tf_op jit(solution)/shard_map/pallas_call | solution.py:62
Async XLA Ops:
  0.6 23.3 %copy-start = (bf16[512,512]{1,0:T(8,128)(2,1)S(1)}, bf16[512,512]{1,0:T(8,128)(2,1)}, u32[]{:S(2)}) copy-start(bf16[512,512]{1,0:T(8,128)(2,1)} %refs_2_.5) | copy-start | bytes 1572868
  0.6 23.3 %copy-start.2 = (bf16[512,512]{1,0:T(8,128)(2,1)S(1)}, bf16[512,512]{1,0:T(8,128)(2,1)}, u32[]{:S(2)}) copy-start(bf16[512,512]{1,0:T(8,128)(2,1)} %refs_4_.3) | copy-start | bytes 1572868
  0.7 25.0 %collective-permute-start.11 = (bf16[512,8192]{1,0:T(8,128)(2,1)}, bf16[512,8192]{1,0:T(8,128)(2,1)}, u32[]{:S(2)}, u32[]{:S(2)}) collective-permute-start(bf16[512,8192]{1,0:T(8,128)(2,1)} %refs_12_.1), channel_id=1, source_target_pairs={{0,1},{1,0},{2,3},{3,2},{4,5},{5,4},{6,7},{7,6},{8,9},{9,8},{10,11... | collective-permute-start | bytes 25165832 | tf_op jit(solution)/shard_map/ppermute | solution.py:439
  4.8 11.0 %collective-permute-start.2 = (bf16[544,128]{1,0:T(8,128)(2,1)S(1)}, bf16[544,128]{1,0:T(8,128)(2,1)S(1)}, u32[]{:S(2)}, u32[]{:S(2)}) collective-permute-start(bf16[544,128]{1,0:T(8,128)(2,1)S(1)} %get-tuple-element.32.refs_1_), channel_id=1, source_target_pairs={{0,16},{16,32},{32,48},{48,0},{64,80},{80,96},{96,112},{112,64},{1... | collective-permute-start | bytes 417800 | tf_op jit(solution)/shard_map/ppermute | solution.py:441
  6.5 9.9 %collective-permute-start.3 = (bf16[544,128]{1,0:T(8,128)(2,1)S(1)}, bf16[544,128]{1,0:T(8,128)(2,1)S(1)}, u32[]{:S(2)}, u32[]{:S(2)}) collective-permute-start(bf16[544,128]{1,0:T(8,128)(2,1)S(1)} %get-tuple-element.32.refs_1_), channel_id=1, source_target_pairs={{0,32},{16,48},{32,0},{48,16},{64,96},{80,112},{96,64},{112,80},{1... | collective-permute-start | bytes 417800 | tf_op jit(solution)/shard_map/ppermute | solution.py:441
  9.4 7.0 %collective-permute-start.4 = (bf16[544,128]{1,0:T(8,128)(2,1)S(1)}, bf16[544,128]{1,0:T(8,128)(2,1)S(1)}, u32[]{:S(2)}, u32[]{:S(2)}) collective-permute-start(bf16[544,128]{1,0:T(8,128)(2,1)S(1)} %get-tuple-element.32.refs_1_), channel_id=1, source_target_pairs={{0,48},{16,0},{32,16},{48,32},{64,112},{80,64},{96,80},{112,96},{1... | collective-permute-start | bytes 417800 | tf_op jit(solution)/shard_map/ppermute | solution.py:441
  10.7 5.0 %collective-permute-start = (bf16[512,128]{1,0:T(8,128)(2,1)S(1)}, bf16[512,128]{1,0:T(8,128)(2,1)S(1)}, u32[]{:S(2)}, u32[]{:S(2)}) collective-permute-start(bf16[512,128]{1,0:T(8,128)(2,1)S(1)} %get-tuple-element.31.refs_5_), channel_id=1, source_target_pairs={{0,64},{16,80},{32,96},{48,112},{64,0},{80,16},{96,32},{112,48},{1... | collective-permute-start | bytes 393224 | tf_op jit(solution)/shard_map/ppermute | solution.py:440
  17.1 6.8 %collective-permute-start.8 = (bf16[544,128]{1,0:T(8,128)(2,1)S(1)}, bf16[544,128]{1,0:T(8,128)(2,1)S(1)}, u32[]{:S(2)}, u32[]{:S(2)}) collective-permute-start(bf16[544,128]{1,0:T(8,128)(2,1)S(1)} %get-tuple-element.39.refs_7_), channel_id=1, source_target_pairs={{0,64},{16,80},{32,96},{48,112},{64,0},{80,16},{96,32},{112,48},{1... | collective-permute-start | bytes 417800 | tf_op jit(solution)/shard_map/ppermute | solution.py:440
  18.7 14.2 %collective-permute-start.5 = (bf16[1024,128]{1,0:T(8,128)(2,1)S(1)}, bf16[1024,128]{1,0:T(8,128)(2,1)S(1)}, u32[]{:S(2)}, u32[]{:S(2)}) collective-permute-start(bf16[1024,128]{1,0:T(8,128)(2,1)S(1)} %get-tuple-element.36), channel_id=1, source_target_pairs={{0,16},{16,32},{32,48},{48,0},{64,80},{80,96},{96,112},{112,64},{1... | collective-permute-start | bytes 786440 | tf_op jit(solution)/shard_map/ppermute | solution.py:441
  19.9 13.7 %collective-permute-start.6 = (bf16[1024,128]{1,0:T(8,128)(2,1)S(1)}, bf16[1024,128]{1,0:T(8,128)(2,1)S(1)}, u32[]{:S(2)}, u32[]{:S(2)}) collective-permute-start(bf16[1024,128]{1,0:T(8,128)(2,1)S(1)} %get-tuple-element.36), channel_id=1, source_target_pairs={{0,32},{16,48},{32,0},{48,16},{64,96},{80,112},{96,64},{112,80},{1... | collective-permute-start | bytes 786440 | tf_op jit(solution)/shard_map/ppermute | solution.py:441
  22.3 11.4 %collective-permute-start.7 = (bf16[1024,128]{1,0:T(8,128)(2,1)S(1)}, bf16[1024,128]{1,0:T(8,128)(2,1)S(1)}, u32[]{:S(2)}, u32[]{:S(2)}) collective-permute-start(bf16[1024,128]{1,0:T(8,128)(2,1)S(1)} %get-tuple-element.36), channel_id=1, source_target_pairs={{0,48},{16,0},{32,16},{48,32},{64,112},{80,64},{96,80},{112,96},{1... | collective-permute-start | bytes 786440 | tf_op jit(solution)/shard_map/ppermute | solution.py:441
  25.7 3.8 %collective-permute-start.10 = (bf16[512,256]{1,0:T(8,128)(2,1)S(1)}, bf16[512,256]{1,0:T(8,128)(2,1)S(1)}, u32[]{:S(2)}, u32[]{:S(2)}) collective-permute-start(bf16[512,256]{1,0:T(8,128)(2,1)S(1)} %get-tuple-element.41.refs_2_.refs_9_), channel_id=1, source_target_pairs={{0,1},{1,0},{2,3},{3,2},{4,5},{5,4},{6,7},{7,6},{8,9},{9,8},{10,11... | collective-permute-start | bytes 786440 | tf_op jit(solution)/shard_map/ppermute | solution.py:439
  25.7 3.8 %collective-permute-start.9 = (bf16[512,256]{1,0:T(8,128)(2,1)S(1)}, bf16[512,256]{1,0:T(8,128)(2,1)S(1)}, u32[]{:S(2)}, u32[]{:S(2)}) collective-permute-start(bf16[512,256]{1,0:T(8,128)(2,1)S(1)} %get-tuple-element.40.refs_3_.refs_1_.refs_8_), channel_id=1, source_target_pairs={{0,1},{1,0},{2,3},{3,2},{4,5},{5,4},{6,7},{7,6},{8,9},{9,8},{10,11... | collective-permute-start | bytes 786440 | tf_op jit(solution)/shard_map/ppermute | solution.py:439
  29.5 15.3 %copy-start.1 = (bf16[512,512]{1,0:T(8,128)(2,1)S(1)}, bf16[512,512]{1,0:T(8,128)(2,1)}, u32[]{:S(2)}) copy-start(bf16[512,512]{1,0:T(8,128)(2,1)} %refs_1_.5) | copy-start | bytes 1572868
  34.3 25.9 %collective-permute-start.16 = (bf16[4,512,256]{2,1,0:T(8,128)(2,1)S(1)}, bf16[4,512,256]{2,1,0:T(8,128)(2,1)S(1)}, u32[]{:S(2)}, u32[]{:S(2)}) collective-permute-start(bf16[4,512,256]{2,1,0:T(8,128)(2,1)S(1)} %get-tuple-element.49), channel_id=1, source_target_pairs={{0,2},{1,3},{2,0},{3,1},{4,6},{5,7},{6,4},{7,5},{8,10},{9,11},{10,... | collective-permute-start | bytes 3145736 | tf_op jit(solution)/shard_map/ppermute | solution.py:527
  37.1 7.6 %collective-permute-start.12 = (bf16[3,1024,128]{2,1,0:T(8,128)(2,1)S(1)}, bf16[3,1024,128]{2,1,0:T(8,128)(2,1)S(1)}, u32[]{:S(2)}, u32[]{:S(2)}) collective-permute-start(bf16[3,1024,128]{2,1,0:T(8,128)(2,1)S(1)} %get-tuple-element.43.refs_6_), channel_id=1, source_target_pairs={{0,1},{1,0},{2,3},{3,2},{4,5},{5,4},{6,7},{7,6},{8,9},{9,8},{10,11... | collective-permute-start | bytes 2359304 | tf_op jit(solution)/shard_map/ppermute | solution.py:439
  37.1 5.4 %collective-permute-start.1 = (bf16[512,128]{1,0:T(8,128)(2,1)S(1)}, bf16[512,128]{1,0:T(8,128)(2,1)S(1)}, u32[]{:S(2)}, u32[]{:S(2)}) collective-permute-start(bf16[512,128]{1,0:T(8,128)(2,1)S(1)} %collective-permute-done.refs_6_.refs_4_), channel_id=1, source_target_pairs={{0,1},{1,0},{2,3},{3,2},{4,5},{5,4},{6,7},{7,6},{8,9},{9,8},{10,11... | collective-permute-start | bytes 393224 | tf_op jit(solution)/shard_map/ppermute | solution.py:439
  37.6 27.2 %collective-permute-start.13 = (bf16[2,512,256]{2,1,0:T(8,128)(2,1)S(1)}, bf16[2,512,256]{2,1,0:T(8,128)(2,1)S(1)}, u32[]{:S(2)}, u32[]{:S(2)}) collective-permute-start(bf16[2,512,256]{2,1,0:T(8,128)(2,1)S(1)} %get-tuple-element.44.refs_14_), channel_id=1, source_target_pairs={{0,8},{1,9},{2,10},{3,11},{4,12},{5,13},{6,14},{7,15},{8,0},{9,1},... | collective-permute-start | bytes 1572872 | tf_op jit(solution)/shard_map/ppermute | solution.py:442
  41.5 23.9 %collective-permute-start.14 = (bf16[2,512,256]{2,1,0:T(8,128)(2,1)S(1)}, bf16[2,512,256]{2,1,0:T(8,128)(2,1)S(1)}, u32[]{:S(2)}, u32[]{:S(2)}) collective-permute-start(bf16[2,512,256]{2,1,0:T(8,128)(2,1)S(1)} %get-tuple-element.47), channel_id=1, source_target_pairs={{0,4},{1,5},{2,6},{3,7},{4,8},{5,9},{6,10},{7,11},{8,12},{9,13},{1... | collective-permute-start | bytes 1572872 | tf_op jit(solution)/shard_map/ppermute | solution.py:442
  42.5 23.9 %collective-permute-start.15 = (bf16[2,512,256]{2,1,0:T(8,128)(2,1)S(1)}, bf16[2,512,256]{2,1,0:T(8,128)(2,1)S(1)}, u32[]{:S(2)}, u32[]{:S(2)}) collective-permute-start(bf16[2,512,256]{2,1,0:T(8,128)(2,1)S(1)} %get-tuple-element.48), channel_id=1, source_target_pairs={{0,12},{1,13},{2,14},{3,15},{4,0},{5,1},{6,2},{7,3},{8,4},{9,5},{1... | collective-permute-start | bytes 1572872 | tf_op jit(solution)/shard_map/ppermute | solution.py:442
  60.9 14.9 %collective-permute-start.18 = (bf16[512,256]{1,0:T(8,128)(2,1)S(1)}, bf16[512,256]{1,0:T(8,128)(2,1)S(1)}, u32[]{:S(2)}, u32[]{:S(2)}) collective-permute-start(bf16[512,256]{1,0:T(8,128)(2,1)S(1)} %get-tuple-element.51.refs_5_), channel_id=1, source_target_pairs={{0,8},{1,9},{2,10},{3,11},{4,12},{5,13},{6,14},{7,15},{8,0},{9,1},... | collective-permute-start | bytes 786440 | tf_op jit(solution)/shard_map/ppermute | solution.py:442
  67.1 8.7 %collective-permute-start.17 = (bf16[512,256]{1,0:T(8,128)(2,1)S(1)}, bf16[512,256]{1,0:T(8,128)(2,1)S(1)}, u32[]{:S(2)}, u32[]{:S(2)}) collective-permute-start(bf16[512,256]{1,0:T(8,128)(2,1)S(1)} %shard_map.148.refs_10_), channel_id=1, source_target_pairs={{0,2},{1,3},{2,0},{3,1},{4,6},{5,7},{6,4},{7,5},{8,10},{9,11},{10,... | collective-permute-start | bytes 786440 | tf_op jit(solution)/shard_map/ppermute | solution.py:562
  68.3 7.9 %collective-permute-start.19 = (bf16[512,256]{1,0:T(8,128)(2,1)S(1)}, bf16[512,256]{1,0:T(8,128)(2,1)S(1)}, u32[]{:S(2)}, u32[]{:S(2)}) collective-permute-start(bf16[512,256]{1,0:T(8,128)(2,1)S(1)} %get-tuple-element.52), channel_id=1, source_target_pairs={{0,4},{1,5},{2,6},{3,7},{4,8},{5,9},{6,10},{7,11},{8,12},{9,13},{1... | collective-permute-start | bytes 786440 | tf_op jit(solution)/shard_map/ppermute | solution.py:442
  69.4 7.5 %collective-permute-start.20 = (bf16[512,256]{1,0:T(8,128)(2,1)S(1)}, bf16[512,256]{1,0:T(8,128)(2,1)S(1)}, u32[]{:S(2)}, u32[]{:S(2)}) collective-permute-start(bf16[512,256]{1,0:T(8,128)(2,1)S(1)} %get-tuple-element.53), channel_id=1, source_target_pairs={{0,12},{1,13},{2,14},{3,15},{4,0},{5,1},{6,2},{7,3},{8,4},{9,5},{1... | collective-permute-start | bytes 786440 | tf_op jit(solution)/shard_map/ppermute | solution.py:442
